TPU v7x, 32 devices: a whole 2x2x4 slice. The times are simulated.
32 devices in a mesh: section: 2 (over core), ctx: 4 (over z), fsdp: 4 (over y, x).
Axes of the slice: x: 2, y: 2, z: 4, core: 2. Of those that a mesh axis runs over, the one named last changes fastest.
Arguments:
- inputs: bfloat16 [2, 4, 1024, 576], P(None, 'fsdp', 'ctx'), may hold values from -6 to 6
- positions: int32 [2, 4, 1024], P(None, 'fsdp', 'ctx'), may hold values from 0 to 1023, as said below
- out_grad: bfloat16 [2, 4, 1024, 576], P(None, 'fsdp', 'ctx'), may hold values from -6 to 6
- attn_gain: bfloat16 [2, 576], P('section', 'fsdp'), may hold values from 0.5 to 1.5
- query_proj: bfloat16 [2, 576, 576], P('section', 'fsdp'), may hold values from -0.25 to 0.25
- key_proj: bfloat16 [2, 576, 192], P('section', 'fsdp'), may hold values from -0.25 to 0.25
- value_proj: bfloat16 [2, 576, 192], P('section', 'fsdp'), may hold values from -0.25 to 0.25
- out_proj: bfloat16 [2, 576, 576], P('section', 'fsdp'), may hold values from -2 to 2
- mlp_gain: bfloat16 [2, 576], P('section', 'fsdp'), may hold values from 0.5 to 1.5
- gate_proj: bfloat16 [2, 576, 1536], P('section', 'fsdp'), may hold values from -0.25 to 0.25
- up_proj: bfloat16 [2, 576, 1536], P('section', 'fsdp'), may hold values from -0.25 to 0.25
- down_proj: bfloat16 [2, 1536, 576], P('section', 'fsdp'), may hold values from -0.15625 to 0.15625
Outputs:
- section_out: bfloat16 [2, 2, 4, 1024, 576], P('section', None, 'fsdp', 'ctx')
- input_grad: bfloat16 [2, 2, 4, 1024, 576], P('section', None, 'fsdp', 'ctx')
- attn_gain_grad: float32 [2, 576], P('section', 'fsdp')
- query_proj_grad: float32 [2, 576, 576], P('section', 'fsdp')
- key_proj_grad: float32 [2, 576, 192], P('section', 'fsdp')
- value_proj_grad: float32 [2, 576, 192], P('section', 'fsdp')
- out_proj_grad: float32 [2, 576, 576], P('section', 'fsdp')
- mlp_gain_grad: float32 [2, 576], P('section', 'fsdp')
- gate_proj_grad: float32 [2, 576, 1536], P('section', 'fsdp')
- up_proj_grad: float32 [2, 576, 1536], P('section', 'fsdp')
- down_proj_grad: float32 [2, 1536, 576], P('section', 'fsdp')
Inputs may be any that keep to these rules, and one draw needn't show every extreme that they name: `positions`: along each sequence a position counts up by one from 0 at the start of each document; in every draw some sequence is one document of 1024 tokens.
All inputs are finite; a program needn't handle non-finite values.
Results may differ from a plain program's by a relative error of at most 0.03.
Values may be sent and summed in bfloat16 or wider, within the bound.
No kernel may reach another device: no remote copies, remote signals or barrier semaphores. Data moves between devices by JAX's collectives and lax.ppermute only.
A program may use at most 192 MiB of HBM per device.

v0:
```python
import jax
import jax.numpy as jnp
from jax import lax
from jax.sharding import PartitionSpec as P

HQ = 9
HK = 3
HD = 64


epsilon = 1e-05
rope_base = 100000.0
masked_score = -1e30


def shifted(block, axis, distance):
    devices = range(lax.axis_size(axis))
    route = [(i - distance, i) for i in devices if i - distance in devices]
    return lax.ppermute(block, axis, route)


def passed_along(block, axis, distance):
    devices = range(lax.axis_size(axis))
    route = [((i - distance) % len(devices), i) for i in devices]
    return lax.ppermute(block, axis, route)


def guarded(active, function, *operands):

    def blank_out(*inner_ops):
        return jax.tree.map(jnp.zeros_like, function(*inner_ops))

    return lax.cond(active, function, blank_out, *operands)


def keep_carried(carried, *others):
    return carried


def rope_tables(places):
    frequency = rope_base ** (-(jnp.arange(HD // 2, dtype=jnp.float32) * 2.0 / HD))
    angles = places.astype(jnp.float32)[..., None] * frequency
    angles = jnp.concatenate([angles, angles], axis=-1)[..., None, :]
    return (jnp.cos(angles), jnp.sin(angles))


def rotate(features, cosine_table, sine_table):
    half_size = features.shape[-1] // 2
    turned = jnp.concatenate([-features[..., half_size:], features[..., :half_size]], axis=-1)
    return features * cosine_table + turned * sine_table


def rotate_back(gradient, cosine_table, sine_table):
    half_size = gradient.shape[-1] // 2
    scaled = gradient * sine_table
    turned = jnp.concatenate([scaled[..., half_size:], -scaled[..., :half_size]], axis=-1)
    return gradient * cosine_table + turned


def across_rows(former, latter):
    return lax.dot_general(
        former, latter, (((0,), (0,)), ((), ())), preferred_element_type=jnp.float32
    )


def against(former, latter):
    return lax.dot_general(
        former, latter, (((1,), (1,)), ((), ())), preferred_element_type=jnp.float32
    )


def norm_scale(features):
    return lax.rsqrt(jnp.mean(features * features, axis=-1, keepdims=True) + epsilon)


def norm_back(features, gain_vec, incoming):
    inverse = norm_scale(features)
    weighted = incoming * gain_vec
    gain_grad = jnp.sum(incoming * features * inverse, axis=0)
    feature_grad = inverse * weighted - features * inverse**3 * jnp.mean(
        features * weighted, axis=-1, keepdims=True
    )
    return (gain_grad, feature_grad)


def to_groups(heads, seq_count, block_len):
    return heads.reshape(seq_count, block_len, HK, HQ // HK, HD).transpose(0, 2, 3, 1, 4)


def from_groups(grouped):
    seq_count, kv_heads, group_size, block_len, head_size = grouped.shape
    return grouped.transpose(0, 3, 1, 2, 4).reshape(
        seq_count, block_len, kv_heads * group_size, head_size
    )


def split_pairs(visiting):
    seq_count, block_len, doubled = visiting.shape
    key_heads = visiting[..., : doubled // 2].reshape(seq_count, block_len, HK, HD)
    value_heads = visiting[..., doubled // 2 :].reshape(seq_count, block_len, HK, HD)
    return (key_heads, value_heads)


def block_scores(query_matrix, key_heads, block_gap):
    block_len = key_heads.shape[1]
    scores = jnp.einsum(
        "shgqd,skhd->shgqk", query_matrix, key_heads, preferred_element_type=jnp.float32
    ) * HD ** (-0.5)
    row_index = lax.broadcasted_iota(jnp.int32, (block_len, block_len), 0)
    column_index = lax.broadcasted_iota(jnp.int32, (block_len, block_len), 1)
    allowed = block_gap * block_len + row_index - column_index >= 0
    return jnp.where(allowed, scores, masked_score)


def attention_inputs(layer_input, cosine_table, sine_table, weights):
    seq_count, block_len, model_width = layer_input.shape
    features = layer_input.reshape(seq_count * block_len, model_width).astype(jnp.float32)
    normalized_rows = (features * norm_scale(features) * weights[0].astype(jnp.float32)).astype(
        jnp.bfloat16
    )
    query_matrix = jnp.dot(normalized_rows, weights[1], preferred_element_type=jnp.float32).reshape(
        seq_count, block_len, HQ, HD
    )
    query_matrix = to_groups(
        rotate(query_matrix, cosine_table, sine_table).astype(jnp.bfloat16), seq_count, block_len
    )
    key_heads = jnp.dot(normalized_rows, weights[2], preferred_element_type=jnp.float32).reshape(
        seq_count, block_len, HK, HD
    )
    key_heads = (
        rotate(key_heads, cosine_table, sine_table)
        .astype(jnp.bfloat16)
        .reshape(seq_count, block_len, HK * HD)
    )
    value_heads = jnp.dot(normalized_rows, weights[3], preferred_element_type=jnp.float32).astype(
        jnp.bfloat16
    )
    value_heads = value_heads.reshape(seq_count, block_len, HK * HD)
    return (normalized_rows, query_matrix, jnp.concatenate([key_heads, value_heads], axis=-1))


def attend_block(carried, query_matrix, visiting, block_gap):
    run_max, run_sum, weighted_sum = carried
    key_heads, value_heads = split_pairs(visiting)
    scores = block_scores(query_matrix, key_heads, block_gap)
    new_max = jnp.maximum(run_max, jnp.max(scores, axis=-1))
    raw_probs = jnp.exp(scores - new_max[..., None])
    factor = jnp.exp(run_max - new_max)
    new_sum = run_sum * factor + jnp.sum(raw_probs, axis=-1)
    update = jnp.einsum(
        "shgqk,skhd->shgqd",
        raw_probs.astype(jnp.bfloat16),
        value_heads,
        preferred_element_type=jnp.float32,
    )
    return (new_max, new_sum, weighted_sum * factor[..., None] + update)


def block_output(layer_input, carried, weights):
    run_max, run_sum, weighted_sum = carried
    seq_count, block_len, model_width = layer_input.shape
    attended = weighted_sum / run_sum[..., None]
    log_total = run_max + jnp.log(run_sum)
    attn_rows = from_groups(attended.astype(jnp.bfloat16)).reshape(seq_count * block_len, HQ * HD)
    resid = layer_input.reshape(seq_count * block_len, model_width).astype(jnp.float32)
    resid = resid + jnp.dot(attn_rows, weights[4], preferred_element_type=jnp.float32)
    mlp_normed = (resid * norm_scale(resid) * weights[5].astype(jnp.float32)).astype(jnp.bfloat16)
    gate_vals = jnp.dot(mlp_normed, weights[6], preferred_element_type=jnp.float32)
    up_vals = jnp.dot(mlp_normed, weights[7], preferred_element_type=jnp.float32)
    hidden = (jax.nn.silu(gate_vals) * up_vals).astype(jnp.bfloat16)
    result = resid + jnp.dot(hidden, weights[8], preferred_element_type=jnp.float32)
    result = result.astype(jnp.bfloat16).reshape(seq_count, block_len, model_width)
    return (result, (log_total, attended, attn_rows, resid, mlp_normed, gate_vals, up_vals, hidden))


def output_back(grad_rows, saved_records, weights):
    attended, attn_rows, resid, mlp_normed = (
        saved_records[5],
        saved_records[6],
        saved_records[7],
        saved_records[8],
    )
    gate_vals, up_vals, hidden = (saved_records[9], saved_records[10], saved_records[11])
    down_in = grad_rows.astype(jnp.bfloat16)
    hidden_grad = against(down_in, weights[8])
    sigmoid_gate = jax.nn.sigmoid(gate_vals)
    gate_in = (
        hidden_grad * up_vals * sigmoid_gate * (1.0 + gate_vals * (1.0 - sigmoid_gate))
    ).astype(jnp.bfloat16)
    up_in = (hidden_grad * gate_vals * sigmoid_gate).astype(jnp.bfloat16)
    normed_grad = against(gate_in, weights[6]) + against(up_in, weights[7])
    mlp_gain_grad, resid_part = norm_back(resid, weights[5].astype(jnp.float32), normed_grad)
    resid_grad = grad_rows + resid_part
    mixed_in = resid_grad.astype(jnp.bfloat16)
    seq_count, kv_heads, group_size, block_len, head_size = attended.shape
    attended_grad = (
        against(mixed_in, weights[4]).astype(jnp.bfloat16).reshape(seq_count, block_len, HQ, HD)
    )
    attended_grad = to_groups(attended_grad, seq_count, block_len)
    row_delta = jnp.sum(attended_grad.astype(jnp.float32) * attended, axis=-1)
    return (
        resid_grad,
        attended_grad,
        row_delta,
        mlp_gain_grad,
        (hidden, down_in, mlp_normed, gate_in, up_in, attn_rows, mixed_in),
    )


def attend_back(carried, query_matrix, visiting, grad_heads, log_total, row_delta, block_gap):
    query_grad, kv_grad = carried
    seq_count, block_len = (visiting.shape[0], visiting.shape[1])
    key_heads, value_heads = split_pairs(visiting)
    scores = block_scores(query_matrix, key_heads, block_gap)
    probabilities = jnp.exp(scores - log_total[..., None])
    value_grad = jnp.einsum(
        "shgqk,shgqd->skhd",
        probabilities.astype(jnp.bfloat16),
        grad_heads,
        preferred_element_type=jnp.float32,
    )
    prob_grad = jnp.einsum(
        "shgqd,skhd->shgqk", grad_heads, value_heads, preferred_element_type=jnp.float32
    )
    score_grad = (probabilities * (prob_grad - row_delta[..., None])).astype(jnp.bfloat16)
    query_grad = query_grad + jnp.einsum(
        "shgqk,skhd->shgqd", score_grad, key_heads, preferred_element_type=jnp.float32
    ) * HD ** (-0.5)
    key_grad = jnp.einsum(
        "shgqk,shgqd->skhd", score_grad, query_matrix, preferred_element_type=jnp.float32
    ) * HD ** (-0.5)
    joined = jnp.concatenate(
        [
            key_grad.reshape(seq_count, block_len, HK * HD),
            value_grad.reshape(seq_count, block_len, HK * HD),
        ],
        axis=-1,
    )
    return (query_grad, kv_grad + joined)


def input_back(resid_grad, query_grad, kv_grad, saved_records, weights, cosine_table, sine_table):
    layer_input, normalized_rows = (saved_records[0], saved_records[1])
    seq_count, block_len, model_width = layer_input.shape
    row_total = seq_count * block_len
    kv_width = kv_grad.shape[-1] // 2
    query_rows = (
        rotate_back(from_groups(query_grad), cosine_table, sine_table)
        .astype(jnp.bfloat16)
        .reshape(row_total, HQ * HD)
    )
    key_rows = rotate_back(
        kv_grad[..., :kv_width].reshape(seq_count, block_len, HK, HD), cosine_table, sine_table
    )
    key_rows = key_rows.astype(jnp.bfloat16).reshape(row_total, kv_width)
    value_rows = kv_grad[..., kv_width:].astype(jnp.bfloat16).reshape(row_total, kv_width)
    normed_grad = (
        against(query_rows, weights[1])
        + against(key_rows, weights[2])
        + against(value_rows, weights[3])
    )
    features = layer_input.reshape(row_total, model_width).astype(jnp.float32)
    attn_gain_grad, feature_grad = norm_back(features, weights[0].astype(jnp.float32), normed_grad)
    entry_grad = (
        (resid_grad + feature_grad).astype(jnp.bfloat16).reshape(seq_count, block_len, model_width)
    )
    return (entry_grad, attn_gain_grad, (normalized_rows, query_rows, key_rows, value_rows))


def unpack_flat(flat_values, templates):
    pieces = []
    offset = 0
    for template in templates:
        count = template.size
        pieces.append(flat_values[offset : offset + count].reshape(template.shape))
        offset += count
    return pieces


def body(
    inputs,
    positions,
    out_grad,
    attn_gain,
    query_proj,
    key_proj,
    value_proj,
    out_proj,
    mlp_gain,
    gate_proj,
    up_proj,
    down_proj,
):
    section_index = lax.axis_index("section")
    cycle_index = lax.axis_index("ctx")
    cycle_count = lax.axis_size("ctx")
    micro_count, seq_count, block_len, model_width = inputs.shape
    tick_count = micro_count + 1
    weights = (
        lax.all_gather(attn_gain[0], "fsdp", axis=0, tiled=True),
        lax.all_gather(query_proj[0], "fsdp", axis=0, tiled=True),
        lax.all_gather(key_proj[0], "fsdp", axis=0, tiled=True),
        lax.all_gather(value_proj[0], "fsdp", axis=0, tiled=True),
        lax.all_gather(out_proj[0], "fsdp", axis=0, tiled=True),
        lax.all_gather(mlp_gain[0], "fsdp", axis=0, tiled=True),
        lax.all_gather(gate_proj[0], "fsdp", axis=0, tiled=True),
        lax.all_gather(up_proj[0], "fsdp", axis=0, tiled=True),
        lax.all_gather(down_proj[0], "fsdp", axis=0, tiled=True),
    )
    received = jnp.zeros((seq_count, block_len, model_width), jnp.bfloat16)
    results = []
    saved_tensors = []
    for tick_index in range(tick_count):
        micro_index = tick_index - section_index
        active = (micro_index >= 0) & (micro_index < micro_count)
        chosen = jnp.clip(micro_index, 0, micro_count - 1)
        own_input = lax.dynamic_index_in_dim(inputs, chosen, 0, keepdims=False)
        layer_input = jnp.where(section_index == 0, own_input, received)
        cosine_table, sine_table = rope_tables(
            lax.dynamic_index_in_dim(positions, chosen, 0, keepdims=False)
        )
        normalized_rows, query_matrix, key_value_pairs = guarded(
            active, attention_inputs, layer_input, cosine_table, sine_table, weights
        )
        carried = (
            jnp.full(query_matrix.shape[:-1], masked_score, jnp.float32),
            jnp.zeros(query_matrix.shape[:-1], jnp.float32),
            jnp.zeros(query_matrix.shape, jnp.float32),
        )
        visiting = key_value_pairs
        for cycle_step in range(cycle_count):
            source = (cycle_index - cycle_step) % cycle_count
            block_live = active & (source <= cycle_index)
            carried = lax.cond(
                block_live,
                attend_block,
                keep_carried,
                carried,
                query_matrix,
                visiting,
                cycle_index - source,
            )
            if cycle_step + 1 < cycle_count:
                visiting = shifted(visiting, "ctx", 1)
        result, saved_records = guarded(active, block_output, layer_input, carried, weights)
        results.append(result)
        saved_tensors.append(
            (layer_input, normalized_rows, query_matrix, key_value_pairs) + saved_records
        )
        if tick_index < micro_count:
            received = shifted(result, "section", 1)
    section_out = lax.dynamic_slice_in_dim(jnp.stack(results), section_index, micro_count, 0)[None]
    stored_values = jax.tree.map(lambda *layer_entries: jnp.stack(layer_entries), *saved_tensors)
    gain_first = jnp.zeros(weights[0].shape, jnp.float32)
    gain_second = jnp.zeros(weights[5].shape, jnp.float32)
    grad_received = jnp.zeros((seq_count, block_len, model_width), jnp.bfloat16)
    entry_grads = []
    product_rows = []
    for tick_index in range(tick_count):
        micro_index = tick_index - 1 + section_index
        active = (micro_index >= 0) & (micro_index < micro_count)
        chosen = jnp.clip(micro_index, 0, micro_count - 1)
        forward_tick = jnp.clip(micro_index + section_index, 0, tick_count - 1)
        saved_records = jax.tree.map(
            lambda element: lax.dynamic_index_in_dim(element, forward_tick, 0, keepdims=False),
            stored_values,
        )
        own_grad = lax.dynamic_index_in_dim(out_grad, chosen, 0, keepdims=False)
        grad_rows = (
            jnp.where(section_index == 1, own_grad, grad_received)
            .astype(jnp.float32)
            .reshape(seq_count * block_len, model_width)
        )
        cosine_table, sine_table = rope_tables(
            lax.dynamic_index_in_dim(positions, chosen, 0, keepdims=False)
        )
        resid_grad, attended_grad, row_delta, mlp_gain_part, tail_rows = guarded(
            active, output_back, grad_rows, saved_records, weights
        )
        query_matrix, visiting, log_total = (saved_records[2], saved_records[3], saved_records[4])
        query_grad = jnp.zeros(query_matrix.shape, jnp.float32)
        kv_grad = jnp.zeros(visiting.shape, jnp.float32)
        for cycle_step in range(cycle_count):
            source = (cycle_index - cycle_step) % cycle_count
            block_live = active & (source <= cycle_index)
            query_grad, kv_grad = lax.cond(
                block_live,
                attend_back,
                keep_carried,
                (query_grad, kv_grad),
                query_matrix,
                visiting,
                attended_grad,
                log_total,
                row_delta,
                cycle_index - source,
            )
            kv_grad = passed_along(kv_grad.astype(jnp.bfloat16), "ctx", 1).astype(kv_grad.dtype)
            if cycle_step + 1 < cycle_count:
                visiting = shifted(visiting, "ctx", 1)
        entry_grad, attn_gain_part, head_rows = guarded(
            active,
            input_back,
            resid_grad,
            query_grad,
            kv_grad,
            saved_records,
            weights,
            cosine_table,
            sine_table,
        )
        gain_first = gain_first + attn_gain_part
        gain_second = gain_second + mlp_gain_part
        product_rows.append(head_rows + tail_rows)
        entry_grads.append(entry_grad)
        if tick_index < micro_count:
            grad_received = shifted(entry_grad, "section", -1)
    input_grad = lax.dynamic_slice_in_dim(
        jnp.stack(entry_grads), 1 - section_index, micro_count, 0
    )[None]
    live_rows = jax.tree.map(
        lambda *tick_entries: lax.dynamic_slice_in_dim(
            jnp.stack(tick_entries), 1 - section_index, micro_count, 0
        ),
        *product_rows
    )
    live_rows = jax.tree.map(lambda element: element.reshape(-1, element.shape[-1]), live_rows)
    (
        normalized_all,
        query_all,
        key_all,
        value_all,
        hidden_all,
        down_all,
        mlp_all,
        gate_all,
        up_all,
        attn_all,
        mixed_all,
    ) = live_rows
    query_sum = across_rows(normalized_all, query_all)
    key_sum = across_rows(normalized_all, key_all)
    value_sum = across_rows(normalized_all, value_all)
    out_sum = across_rows(attn_all, mixed_all)
    gate_sum = across_rows(mlp_all, gate_all)
    up_sum = across_rows(mlp_all, up_all)
    down_sum = across_rows(hidden_all, down_all)
    shard_parts = (
        lax.psum_scatter(
            gain_first.astype(jnp.bfloat16), "fsdp", scatter_dimension=0, tiled=True
        ).astype(jnp.float32),
        lax.psum_scatter(
            query_sum.astype(jnp.bfloat16), "fsdp", scatter_dimension=0, tiled=True
        ).astype(jnp.float32),
        lax.psum_scatter(
            key_sum.astype(jnp.bfloat16), "fsdp", scatter_dimension=0, tiled=True
        ).astype(jnp.float32),
        lax.psum_scatter(
            value_sum.astype(jnp.bfloat16), "fsdp", scatter_dimension=0, tiled=True
        ).astype(jnp.float32),
        lax.psum_scatter(
            out_sum.astype(jnp.bfloat16), "fsdp", scatter_dimension=0, tiled=True
        ).astype(jnp.float32),
        lax.psum_scatter(
            gain_second.astype(jnp.bfloat16), "fsdp", scatter_dimension=0, tiled=True
        ).astype(jnp.float32),
        lax.psum_scatter(
            gate_sum.astype(jnp.bfloat16), "fsdp", scatter_dimension=0, tiled=True
        ).astype(jnp.float32),
        lax.psum_scatter(
            up_sum.astype(jnp.bfloat16), "fsdp", scatter_dimension=0, tiled=True
        ).astype(jnp.float32),
        lax.psum_scatter(
            down_sum.astype(jnp.bfloat16), "fsdp", scatter_dimension=0, tiled=True
        ).astype(jnp.float32),
    )
    flat_parts = jnp.concatenate([element.reshape(-1) for element in shard_parts])
    quarter = flat_parts.shape[0] // cycle_count
    summed_part = lax.psum_scatter(
        flat_parts.reshape(cycle_count, quarter).astype(jnp.bfloat16),
        "ctx",
        scatter_dimension=0,
        tiled=True,
    ).astype(jnp.float32)
    regathered = (
        lax.all_gather(summed_part.astype(jnp.bfloat16), "ctx", axis=0, tiled=True)
        .astype(summed_part.dtype)
        .reshape(-1)
    )
    shard_parts = unpack_flat(regathered, shard_parts)
    return (section_out, input_grad) + tuple((finished[None] for finished in shard_parts))


def solution(mesh):
    return jax.shard_map(
        body,
        mesh=mesh,
        in_specs=(
            P(None, "fsdp", "ctx", None),
            P(None, "fsdp", "ctx"),
            P(None, "fsdp", "ctx", None),
            P("section", "fsdp"),
            P("section", "fsdp", None),
            P("section", "fsdp", None),
            P("section", "fsdp", None),
            P("section", "fsdp", None),
            P("section", "fsdp"),
            P("section", "fsdp", None),
            P("section", "fsdp", None),
            P("section", "fsdp", None),
        ),
        out_specs=(
            P("section", None, "fsdp", "ctx", None),
            P("section", None, "fsdp", "ctx", None),
            P("section", "fsdp"),
            P("section", "fsdp", None),
            P("section", "fsdp", None),
            P("section", "fsdp", None),
            P("section", "fsdp", None),
            P("section", "fsdp"),
            P("section", "fsdp", None),
            P("section", "fsdp", None),
            P("section", "fsdp", None),
        ),
        check_vma=False,
    )
```

profile of v0, /device:TPU:0, one launch (start us, length us, event | category | flops | bytes accessed | tf_op | source)
XLA Modules:
  0.0 1102.1 jit_solution(12439788020972899354)
XLA Ops:
  12.7 11.4 %all-reduce.8 = (bf16[576]{0:T(1024)(128)(2,1)S(1)}, bf16[576]{0:T(1024)(128)(2,1)S(1)}) all-reduce(bf16[576]{0:T(1024)(128)(2,1)S(1)} %dynamic-update-slice, bf16[576]{0:T(1024)(128)(2,1)S(1)} %dynamic-update-slice.1), channel_id=2, replica_groups=mesh['section'=2,'ctx'=4,'fsdp'=4] {'fsdp'}, use_global_device_ids=true, to_apply=%add | all-reduce | flops 1152 | bytes 4608 | tf_op jit(solution)/shard_map/all_gather | solution.py:300
  24.2 8.9 all-gather.2
  33.0 12.9 %all-gather.3 = bf16[1,576,192]{2,1,0:T(8,128)(2,1)} all-gather(bf16[1,144,192]{2,1,0:T(8,128)(2,1)S(1)} %copy-done.94), channel_id=5, replica_groups=mesh['section'=2,'ctx'=4,'fsdp'=4] {'fsdp'}, dimensions={1}, use_global_device_ids=true | all-gather | bytes 276480 | tf_op jit(solution)/shard_map/all_gather | solution.py:303
  46.8 10.2 all-gather.1
  57.0 5.0 conditional.36
  68.9 4.9 collective-permute-start.1
  81.5 10.6 all-gather.4
  92.2 30.0 %all-gather.19.cloned.1.call-done = bf16[1,1536,576]{2,1,0:T(8,128)(2,1)} async-done(((bf16[1,384,576]{2,1,0:T(8,128)(2,1)}), bf16[1,1536,576]{2,1,0:T(8,128)(2,1)}) %all-gather.19.cloned.1.call-update) | async-done | bytes 1769488 | tf_op jit(solution)/shard_map/all_gather | solution.py:308
  122.3 17.7 %conditional.41 = (bf16[1,256,576]{1,2,0:T(8,128)(2,1)}, bf16[1,1,256,576]{2,3,1,0:T(8,128)(2,1)}, f32[1,1,3,3,256]{4,3,2,1,0:T(4,128)S(1)}, f32[1,1,3,3,256,64]...) conditional(s32[]{:T(128)} %convert_element_type.939, ...), branch_computations={%region_19.20_spmd, %region_20.22_spmd} | conditional | flops 1533692928 | bytes 43282780 | solution.py:33
  146.0 5.2 conditional.42
  158.7 4.4 collective-permute-start.5
  165.6 5.1 collective-permute-start.6
  177.2 19.0 %conditional.47 = (bf16[1,256,576]{1,2,0:T(8,128)(2,1)}, bf16[1,1,256,576]{2,3,1,0:T(8,128)(2,1)}, f32[1,1,3,3,256]{4,3,2,1,0:T(4,128)S(1)}, f32[1,1,3,3,256,64]...) conditional(s32[]{:T(128)} %convert_element_type.946, ...), branch_computations={%region_41.42_spmd, %region_42.44_spmd} | conditional | flops 1533692928 | bytes 36241756 | solution.py:33
  214.6 5.8 collective-permute-start.8
  223.8 6.9 collective-permute-start.9
  245.6 8.2 conditional.53
  270.9 8.9 conditional.54
  324.4 106.8 %collective-permute-done.18 = bf16[1,256,576]{1,2,0:T(8,128)(2,1)} collective-permute-done((bf16[1,256,576]{1,2,0:T(8,128)(2,1)}, bf16[1,256,576]{1,2,0:T(8,128)(2,1)}, u32[]{:S(2)}, u32[]{:S(2)}) %collective-permute-start.18) | collective-permute-done | bytes 294944 | tf_op jit(solution)/shard_map/ppermute | solution.py:19
  432.3 24.1 %conditional.60 = (f32[256,576]{0,1:T(8,128)}, bf16[1,3,3,256,64]{3,4,2,1,0:T(8,128)(2,1)}, f32[1,3,3,256]{3,2,1,0:T(4,128)}, f32[576]{0:T(1024)}, bf16[1,256,15...) conditional(s32[]{:T(128)} %convert_element_type.977, ...), branch_computations={%region_85.86_spmd, %region_86.91_spmd} | conditional | flops 1537178112 | bytes 39229740 | solution.py:33
  433.5 4.9 fusion.309
  456.5 12.2 %conditional.61 = (f32[1,3,3,256,64]{3,4,2,1,0:T(8,128)}, bf16[1,256,384]{1,2,0:T(8,128)(2,1)}) conditional(s32[]{:T(128)} %convert_element_type.981, () %tuple.483, (s32[]{:T(128)}, bf16[1,3,3,256,64]{3,4,2,1,0:T(8,128)(2,1)}, bf16[1,256,384]{1,2,0:T(8,128)(2,1)}, f32[1,3,3,256]{3,2,1,0:T(4,128)}, bf16[1,3,3,256,64]{3,4,2,1,0:T(8,128)(2,1)}, ...), branch_computations={%region_91.92_spmd, %region_92.93_spmd} | conditional | flops 384155904 | bytes 25330860 | solution.py:386
  468.7 4.6 collective-permute-start.20
  473.2 4.4 collective-permute-done.19
  481.2 15.4 %collective-permute-start.21 = (bf16[1,256,384]{1,2,0:T(8,128)(2,1)}, bf16[1,256,384]{1,2,0:T(8,128)(2,1)}, u32[]{:S(2)}, u32[]{:S(2)}) collective-permute-start(bf16[1,256,384]{1,2,0:T(8,128)(2,1)} %convert_element_type.985), channel_id=1, source_target_pairs={{12,0},{0,4},{4,8},{8,12},{13,1},{1,5},{5,9},{9,13},{14,2},{2,6},{... | collective-permute-start | bytes 589832 | tf_op jit(solution)/shard_map/ppermute | solution.py:25
  509.2 18.4 %collective-permute-start.24 = (bf16[1,256,384]{1,2,0:T(8,128)(2,1)}, bf16[1,256,384]{1,2,0:T(8,128)(2,1)}, u32[]{:S(2)}, u32[]{:S(2)}) collective-permute-start(bf16[1,256,384]{1,2,0:T(8,128)(2,1)} %collective-permute-done.22), channel_id=1, source_target_pairs={{0,4},{4,8},{8,12},{1,5},{5,9},{9,13},{2,6},{6,10},{10,14},{3,7},{... | collective-permute-start | bytes 589832 | tf_op jit(solution)/shard_map/ppermute | solution.py:19
  534.8 19.2 %collective-permute-done.25 = bf16[1,256,384]{1,2,0:T(8,128)(2,1)S(1)} collective-permute-done((bf16[1,256,384]{1,2,0:T(8,128)(2,1)S(1)}, bf16[1,256,384]{1,2,0:T(8,128)(2,1)S(1)}, u32[]{:S(2)}, u32[]{:S(2)}) %collective-permute-start.25) | collective-permute-done | bytes 196640 | tf_op jit(solution)/shard_map/ppermute | solution.py:25
  554.0 16.5 %conditional.65 = (bf16[1,256,576]{1,2,0:T(8,128)(2,1)}, f32[576]{0:T(1024)S(1)}, bf16[1,1,256,576]{2,3,1,0:T(8,128)(2,1)}, bf16[1,256,576]{1,2,0:T(8,128)(2,1)}...) conditional(s32[]{:T(128)} %convert_element_type.977, ...), branch_computations={%region_99.100_spmd, %region_100.104_spmd} | conditional | flops 287736576 | bytes 18527432 | solution.py:33
  575.5 21.2 %conditional.66 = (f32[256,576]{0,1:T(8,128)}, bf16[1,3,3,256,64]{3,4,2,1,0:T(8,128)(2,1)}, f32[1,3,3,256]{3,2,1,0:T(4,128)}, f32[576]{0:T(1024)S(1)}, bf16[1,25...) conditional(s32[]{:T(128)} %convert_element_type.993, ...), branch_computations={%region_104.105_spmd, %region_105.110_spmd} | conditional | flops 1537178112 | bytes 39229740 | solution.py:33
  577.1 4.9 fusion.398
  596.7 8.4 conditional.67
  608.3 5.9 collective-permute-done.27
  614.4 10.7 collective-permute-start.29
  633.6 13.4 %collective-permute-start.32 = (bf16[1,256,384]{1,2,0:T(8,128)(2,1)}, bf16[1,256,384]{1,2,0:T(8,128)(2,1)S(1)}, u32[]{:S(2)}, u32[]{:S(2)}) collective-permute-start(bf16[1,256,384]{1,2,0:T(8,128)(2,1)} %collective-permute-done.30), channel_id=1, source_target_pairs={{0,4},{4,8},{8,12},{1,5},{5,9},{9,13},{2,6},{6,10},{10,14},{3,7},{... | collective-permute-start | bytes 589832 | tf_op jit(solution)/shard_map/ppermute | solution.py:19
  653.2 11.7 %collective-permute-done.33 = bf16[1,256,384]{1,2,0:T(8,128)(2,1)S(1)} collective-permute-done((bf16[1,256,384]{1,2,0:T(8,128)(2,1)S(1)}, bf16[1,256,384]{1,2,0:T(8,128)(2,1)S(1)}, u32[]{:S(2)}, u32[]{:S(2)}) %collective-permute-start.33) | collective-permute-done | bytes 196640 | tf_op jit(solution)/shard_map/ppermute | solution.py:25
  664.9 8.1 conditional.71
  684.3 4.4 bitcast_convert_fusion.6
  688.8 4.4 bitcast_convert_fusion.5
  699.7 8.9 all-reduce.7
  709.8 17.0 %reduce-scatter.16.cloned.1.call-done = bf16[144,192]{1,0:T(8,128)(2,1)} async-done(((bf16[576,192]{1,0:T(8,128)(2,1)}), bf16[144,192]{1,0:T(8,128)(2,1)}) %reduce-scatter.16.cloned.1.call-update) | async-done | bytes 55312 | tf_op jit(solution)/shard_map/reduce_scatter | solution.py:458
  727.8 27.6 %reduce-scatter.26.cloned.1.call-done = bf16[144,576]{1,0:T(8,128)(2,1)} async-done(((bf16[576,576]{1,0:T(8,128)(2,1)}), bf16[144,576]{1,0:T(8,128)(2,1)}) %reduce-scatter.26.cloned.1.call-update) | async-done | bytes 165904
  757.2 27.5 %reduce-scatter.24.cloned.1.call-done = bf16[144,576]{1,0:T(8,128)(2,1)} async-done(((bf16[576,576]{1,0:T(8,128)(2,1)}), bf16[144,576]{1,0:T(8,128)(2,1)}) %reduce-scatter.24.cloned.1.call-update) | async-done | bytes 165904
  786.5 33.7 %reduce-scatter.18.cloned.1.call-done = bf16[144,1536]{1,0:T(8,128)(2,1)} async-done(((bf16[576,1536]{1,0:T(8,128)(2,1)}), bf16[144,1536]{1,0:T(8,128)(2,1)}) %reduce-scatter.18.cloned.1.call-update) | async-done | bytes 442384 | tf_op jit(solution)/shard_map/reduce_scatter | solution.py:467
  821.8 34.0 %reduce-scatter.20.cloned.1.call-done = bf16[144,1536]{1,0:T(8,128)(2,1)} async-done(((bf16[576,1536]{1,0:T(8,128)(2,1)}), bf16[144,1536]{1,0:T(8,128)(2,1)}) %reduce-scatter.20.cloned.1.call-update) | async-done | bytes 442384 | tf_op jit(solution)/shard_map/reduce_scatter | solution.py:470
  857.3 35.5 %reduce-scatter.22.cloned.1.call-done = bf16[384,576]{1,0:T(8,128)(2,1)} async-done(((bf16[1536,576]{1,0:T(8,128)(2,1)}), bf16[384,576]{1,0:T(8,128)(2,1)}) %reduce-scatter.22.cloned.1.call-update) | async-done | bytes 442384 | tf_op jit(solution)/shard_map/reduce_scatter | solution.py:473
  894.3 17.1 %concatenate.223 = bf16[885024]{0:T(1024)(128)(2,1)S(1)} concatenate(bf16[144]{0:T(256)(128)(2,1)S(1)} %dynamic-slice.3, bf16[82944]{0:T(1024)(128)(2,1)} %reshape.2836, bf16[27648]{0:T(1024)(128)(2,1)S(1)} %reshape.2837, bf16[27648]{0:T(1024)(128)(2,1)S(1)} %reshape.2838, bf16[82944]{0:T(1024)(128)(2,1)} %reshape.2839, bf16[144]{0:T(256)(128)(2,1)S(1)} %dynamic-slice.9, ...), dimensions={0} | concatenate | bytes 3540096 | tf_op jit(solution)/shard_map/concatenate | solution.py:477
  915.9 75.5 %all-reduce.11.cloned.1.call-done = bf16[4,221256]{1,0:T(4,128)(2,1)} async-done(((bf16[4,221256]{1,0:T(4,128)(2,1)}), bf16[4,221256]{1,0:T(4,128)(2,1)}) %all-reduce.11.cloned.1.call-update) | async-done | bytes 1770064
  999.3 64.8 %all-gather.21.cloned.1.call-done = bf16[4,1,221256]{2,1,0:T(2,128)(2,1)} async-done(((bf16[1,1,221256]{2,1,0:T(2,128)(2,1)}), bf16[4,1,221256]{2,1,0:T(2,128)(2,1)}) %all-gather.21.cloned.1.call-update) | async-done | bytes 1770064 | tf_op jit(solution)/shard_map/all_gather | solution.py:486
  1064.2 12.0 %convert_reduce_fusion = f32[4,221256]{1,0:T(4,128)S(1)} fusion(bf16[4,1,221256]{2,1,0:T(2,128)(2,1)} %all-gather.21.cloned.1.call-done), kind=kLoop, calls=%fused_computation.843 | loop fusion | flops 885024 | bytes 5310144 | tf_op jit(solution)/shard_map/reshape | solution.py:488
  (554 shorter events, 403.4 us)
Async XLA Ops:
  7.3 84.9 %all-gather.15.cloned.1.call-start = ((), (), s32[]{:S(2)}) async-start(), calls=%async_computation.11 | async-start | bytes 2211840 | tf_op jit(solution)/shard_map/all_gather | solution.py:306
  8.0 84.2 %all-gather.17.cloned.1.call-start = ((), (), s32[]{:S(2)}) async-start(), calls=%async_computation.12 | async-start | bytes 2211840 | tf_op jit(solution)/shard_map/all_gather | solution.py:307
  8.7 113.5 %all-gather.19.cloned.1.call-start = ((), (), s32[]{:S(2)}) async-start(), calls=%async_computation.13 | async-start | bytes 2457600 | tf_op jit(solution)/shard_map/all_gather | solution.py:308
  10.8 697.9 %reduce-scatter.14.cloned.1.call-start = ((), (), s32[]{:S(2)}) async-start(), calls=%async_computation.7 | async-start | bytes 368640 | tf_op jit(solution)/shard_map/reduce_scatter | solution.py:455
  24.1 98.1 %copy-start.89 = (bf16[576]{0:T(1024)(128)(2,1)}, bf16[576]{0:T(1024)(128)(2,1)S(1)}, u32[]{:S(2)}) copy-start(bf16[576]{0:T(1024)(128)(2,1)S(1)} %get-tuple-element.2275) | copy-start | bytes 3460
  62.0 6.9 collective-permute-start
  68.9 8.4 collective-permute-start.1
  77.3 14.8 %collective-permute-start.2 = (bf16[1,256,384]{1,2,0:T(8,128)(2,1)}, bf16[1,256,384]{1,2,0:T(8,128)(2,1)S(1)}, u32[]{:S(2)}, u32[]{:S(2)}) collective-permute-start(bf16[1,256,384]{1,2,0:T(8,128)(2,1)} %collective-permute-done.1), channel_id=1, source_target_pairs={{0,4},{4,8},{8,12},{1,5},{5,9},{9,13},{2,6},{6,10},{10,14},{3,7},{... | collective-permute-start | bytes 589832 | tf_op jit(solution)/shard_map/ppermute | solution.py:19
  140.0 5.2 collective-permute-start.3
  151.3 7.4 collective-permute-start.4
  158.7 6.9 collective-permute-start.5
  165.6 9.3 collective-permute-start.6
  196.2 15.4 %collective-permute-start.7 = (bf16[1,256,576]{1,2,0:T(8,128)(2,1)}, bf16[1,256,576]{1,2,0:T(8,128)(2,1)S(1)}, u32[]{:S(2)}, u32[]{:S(2)}) collective-permute-start(bf16[1,256,576]{1,2,0:T(8,128)(2,1)} %get-tuple-element.1764), channel_id=1, source_target_pairs={{0,16},{1,17},{2,18},{3,19},{4,20},{5,21},{6,22},{7,23},{8,24},{9,... | collective-permute-start | bytes 884744 | tf_op jit(solution)/shard_map/ppermute | solution.py:19
  214.6 9.2 collective-permute-start.8
  223.8 13.3 %collective-permute-start.9 = (bf16[1,256,384]{1,2,0:T(8,128)(2,1)S(1)}, bf16[1,256,384]{1,2,0:T(8,128)(2,1)}, u32[]{:S(2)}, u32[]{:S(2)}) collective-permute-start(bf16[1,256,384]{1,2,0:T(8,128)(2,1)S(1)} %collective-permute-done.8), channel_id=1, source_target_pairs={{0,4},{4,8},{8,12},{1,5},{5,9},{9,13},{2,6},{6,10},{10,14},{3,7},{... | collective-permute-start | bytes 589832 | tf_op jit(solution)/shard_map/ppermute | solution.py:19
  232.8 51.1 %collective-permute-start.12 = (bf16[1,256,384]{1,2,0:T(8,128)(2,1)}, bf16[1,256,384]{1,2,0:T(8,128)(2,1)}, u32[]{:S(2)}, u32[]{:S(2)}) collective-permute-start(bf16[1,256,384]{1,2,0:T(8,128)(2,1)} %get-tuple-element.2488), channel_id=1, source_target_pairs={{0,4},{4,8},{8,12},{1,5},{5,9},{9,13},{2,6},{6,10},{10,14},{3,7},{... | collective-permute-start | bytes 589832 | tf_op jit(solution)/shard_map/ppermute | solution.py:19
  237.1 8.5 collective-permute-start.10
  281.4 7.8 collective-permute-start.11
  283.9 12.2 %collective-permute-start.14 = (bf16[1,256,384]{1,2,0:T(8,128)(2,1)}, bf16[1,256,384]{1,2,0:T(8,128)(2,1)}, u32[]{:S(2)}, u32[]{:S(2)}) collective-permute-start(bf16[1,256,384]{1,2,0:T(8,128)(2,1)} %collective-permute-done.12), channel_id=1, source_target_pairs={{0,4},{4,8},{8,12},{1,5},{5,9},{9,13},{2,6},{6,10},{10,14},{3,7},{... | collective-permute-start | bytes 589832 | tf_op jit(solution)/shard_map/ppermute | solution.py:19
  291.9 8.1 collective-permute-start.13
  296.1 14.0 %collective-permute-start.16 = (bf16[1,256,384]{1,2,0:T(8,128)(2,1)}, bf16[1,256,384]{1,2,0:T(8,128)(2,1)}, u32[]{:S(2)}, u32[]{:S(2)}) collective-permute-start(bf16[1,256,384]{1,2,0:T(8,128)(2,1)} %collective-permute-done.14), channel_id=1, source_target_pairs={{0,4},{4,8},{8,12},{1,5},{5,9},{9,13},{2,6},{6,10},{10,14},{3,7},{... | collective-permute-start | bytes 589832 | tf_op jit(solution)/shard_map/ppermute | solution.py:19
  301.8 7.5 collective-permute-start.15
  311.3 7.5 collective-permute-start.17
  323.1 109.2 %copy-start.101 = (f32[576]{0:T(1024)}, f32[576]{0:T(1024)S(1)}, u32[]{:S(2)}) copy-start(f32[576]{0:T(1024)S(1)} %get-tuple-element.1845) | copy-start | bytes 6916
  323.1 108.1 %collective-permute-start.18 = (bf16[1,256,576]{1,2,0:T(8,128)(2,1)}, bf16[1,256,576]{1,2,0:T(8,128)(2,1)}, u32[]{:S(2)}, u32[]{:S(2)}) collective-permute-start(bf16[1,256,576]{1,2,0:T(8,128)(2,1)} %get-tuple-element.1819), channel_id=1, source_target_pairs={{16,0},{17,1},{18,2},{19,3},{20,4},{21,5},{22,6},{23,7},{24,8},{25... | collective-permute-start | bytes 884744 | tf_op jit(solution)/shard_map/ppermute | solution.py:19
  468.7 9.0 collective-permute-start.19
  468.7 10.7 collective-permute-start.20
  481.2 21.7 %collective-permute-start.21 = (bf16[1,256,384]{1,2,0:T(8,128)(2,1)}, bf16[1,256,384]{1,2,0:T(8,128)(2,1)}, u32[]{:S(2)}, u32[]{:S(2)}) collective-permute-start(bf16[1,256,384]{1,2,0:T(8,128)(2,1)} %convert_element_type.985), channel_id=1, source_target_pairs={{12,0},{0,4},{4,8},{8,12},{13,1},{1,5},{5,9},{9,13},{14,2},{2,6},{... | collective-permute-start | bytes 589832 | tf_op jit(solution)/shard_map/ppermute | solution.py:25
  496.7 8.4 collective-permute-start.22
  506.7 22.2 %collective-permute-start.23 = (bf16[1,256,384]{1,2,0:T(8,128)(2,1)}, bf16[1,256,384]{1,2,0:T(8,128)(2,1)}, u32[]{:S(2)}, u32[]{:S(2)}) collective-permute-start(bf16[1,256,384]{1,2,0:T(8,128)(2,1)} %convert_element_type.987), channel_id=1, source_target_pairs={{12,0},{0,4},{4,8},{8,12},{13,1},{1,5},{5,9},{9,13},{14,2},{2,6},{... | collective-permute-start | bytes 589832 | tf_op jit(solution)/shard_map/ppermute | solution.py:25
  509.2 21.5 %collective-permute-start.24 = (bf16[1,256,384]{1,2,0:T(8,128)(2,1)}, bf16[1,256,384]{1,2,0:T(8,128)(2,1)}, u32[]{:S(2)}, u32[]{:S(2)}) collective-permute-start(bf16[1,256,384]{1,2,0:T(8,128)(2,1)} %collective-permute-done.22), channel_id=1, source_target_pairs={{0,4},{4,8},{8,12},{1,5},{5,9},{9,13},{2,6},{6,10},{10,14},{3,7},{... | collective-permute-start | bytes 589832 | tf_op jit(solution)/shard_map/ppermute | solution.py:19
  531.7 22.3 %collective-permute-start.25 = (bf16[1,256,384]{1,2,0:T(8,128)(2,1)S(1)}, bf16[1,256,384]{1,2,0:T(8,128)(2,1)S(1)}, u32[]{:S(2)}, u32[]{:S(2)}) collective-permute-start(bf16[1,256,384]{1,2,0:T(8,128)(2,1)S(1)} %convert_element_type.991), channel_id=1, source_target_pairs={{12,0},{0,4},{4,8},{8,12},{13,1},{1,5},{5,9},{9,13},{14,2},{2,6},{... | collective-permute-start | bytes 589832 | tf_op jit(solution)/shard_map/ppermute | solution.py:25
  570.6 3.8 collective-permute-start.26
  605.1 9.2 collective-permute-start.27
  605.1 9.2 collective-permute-start.28
  614.4 15.9 %collective-permute-start.29 = (bf16[1,256,384]{1,2,0:T(8,128)(2,1)S(1)}, bf16[1,256,384]{1,2,0:T(8,128)(2,1)S(1)}, u32[]{:S(2)}, u32[]{:S(2)}) collective-permute-start(bf16[1,256,384]{1,2,0:T(8,128)(2,1)S(1)} %convert_element_type.1001), channel_id=1, source_target_pairs={{12,0},{0,4},{4,8},{8,12},{13,1},{1,5},{5,9},{9,13},{14,2},{2,6},{... | collective-permute-start | bytes 589832 | tf_op jit(solution)/shard_map/ppermute | solution.py:25
  625.1 5.9 collective-permute-start.30
  631.1 16.6 %collective-permute-start.31 = (bf16[1,256,384]{1,2,0:T(8,128)(2,1)S(1)}, bf16[1,256,384]{1,2,0:T(8,128)(2,1)S(1)}, u32[]{:S(2)}, u32[]{:S(2)}) collective-permute-start(bf16[1,256,384]{1,2,0:T(8,128)(2,1)S(1)} %convert_element_type.1003), channel_id=1, source_target_pairs={{12,0},{0,4},{4,8},{8,12},{13,1},{1,5},{5,9},{9,13},{14,2},{2,6},{... | collective-permute-start | bytes 589832 | tf_op jit(solution)/shard_map/ppermute | solution.py:25
  633.6 16.9 %collective-permute-start.32 = (bf16[1,256,384]{1,2,0:T(8,128)(2,1)}, bf16[1,256,384]{1,2,0:T(8,128)(2,1)S(1)}, u32[]{:S(2)}, u32[]{:S(2)}) collective-permute-start(bf16[1,256,384]{1,2,0:T(8,128)(2,1)} %collective-permute-done.30), channel_id=1, source_target_pairs={{0,4},{4,8},{8,12},{1,5},{5,9},{9,13},{2,6},{6,10},{10,14},{3,7},{... | collective-permute-start | bytes 589832 | tf_op jit(solution)/shard_map/ppermute | solution.py:19
  650.7 14.1 %collective-permute-start.33 = (bf16[1,256,384]{1,2,0:T(8,128)(2,1)S(1)}, bf16[1,256,384]{1,2,0:T(8,128)(2,1)S(1)}, u32[]{:S(2)}, u32[]{:S(2)}) collective-permute-start(bf16[1,256,384]{1,2,0:T(8,128)(2,1)S(1)} %convert_element_type.1007), channel_id=1, source_target_pairs={{12,0},{0,4},{4,8},{8,12},{13,1},{1,5},{5,9},{9,13},{14,2},{2,6},{... | collective-permute-start | bytes 589832 | tf_op jit(solution)/shard_map/ppermute | solution.py:25
  676.3 50.5 %reduce-scatter.16.cloned.1.call-start = ((), (), s32[]{:S(2)}) async-start(), calls=%async_computation.8 | async-start | bytes 368640 | tf_op jit(solution)/shard_map/reduce_scatter | solution.py:458
  678.4 76.9 %reduce-scatter.26.cloned.1.call-start = ((), (), s32[]{:S(2)}) async-start(), calls=%async_computation.18 | async-start | bytes 921600
  681.6 103.0 %reduce-scatter.24.cloned.1.call-start = ((), (), s32[]{:S(2)}) async-start(), calls=%async_computation.17 | async-start | bytes 921600
  684.3 135.9 %reduce-scatter.18.cloned.1.call-start = ((), (), s32[]{:S(2)}) async-start(), calls=%async_computation.9 | async-start | bytes 2211840 | tf_op jit(solution)/shard_map/reduce_scatter | solution.py:467
  688.8 167.0 %reduce-scatter.20.cloned.1.call-start = ((), (), s32[]{:S(2)}) async-start(), calls=%async_computation.10 | async-start | bytes 2211840 | tf_op jit(solution)/shard_map/reduce_scatter | solution.py:470
  693.2 199.6 %reduce-scatter.22.cloned.1.call-start = ((), (), s32[]{:S(2)}) async-start(), calls=%async_computation.15 | async-start | bytes 2457600 | tf_op jit(solution)/shard_map/reduce_scatter | solution.py:473
  698.9 292.5 %all-reduce.11.cloned.1.call-start = ((), (), s32[]{:S(2)}) async-start(), calls=%async_computation.16 | async-start | bytes 3540992
  915.0 149.2 %all-gather.21.cloned.1.call-start = ((), (), s32[]{:S(2)}) async-start(), calls=%async_computation.14 | async-start | bytes 4426240 | tf_op jit(solution)/shard_map/all_gather | solution.py:486
  (69 other events, 656.8 us)
Sparse Core Ops, SparseCore 0:
  9.9 38.6 all-gather.14
  50.5 35.5 all-gather.16
  88.5 33.6 all-gather.18
  676.4 22.8 reduce-scatter.13
  702.5 24.1 reduce-scatter.15
  729.6 25.7 reduce-scatter.25
  758.9 25.7 reduce-scatter.23
  787.7 32.4 reduce-scatter.17
  823.3 32.4 reduce-scatter.19
  858.7 34.0 reduce-scatter.21
  915.1 76.2 all-reduce.10
  995.1 69.0 all-gather.20
where the time goes:
time: 1120 us; the launch traced here: 1100 us
  waiting for transfers between devices  522 us (47%)
  local copies, waits for them, and re-layouts  175 us (16%)
  starting transfers between devices  145 us (13%)
  matrix products  99.6 us (9%)
  other arithmetic  77.4 us (7%)
  blocking collectives  63 us (6%)
  between operations  16.9 us (2%)
    unnamed x15, waiting for transfers between devices  132 us
    ppermute x22, waiting for transfers between devices, shifted(): return lax.ppermute(block, axis, route)  118 us
    ppermute x22, starting transfers between devices, shifted(): return lax.ppermute(block, axis, route)  105 us
    all_gather x1, waiting for transfers between devices, body(): lax.all_gather(summed_part.astype(jnp.bfloat16), 'ctx', axis=0, tiled=True)  64.8 us
    ppermute x12, waiting for transfers between devices, passed_along(): return lax.ppermute(block, axis, route)  56.4 us
    unnamed x128, local copies, waits for them, and re-layouts  46.3 us
    ppermute x12, starting transfers between devices, passed_along(): return lax.ppermute(block, axis, route)  39.3 us
    reduce_scatter x1, waiting for transfers between devices, body(): lax.psum_scatter(down_sum.astype(jnp.bfloat16), 'fsdp', scatter_dimension...  35.5 us
  transfers between devices with their start and end apart: 46, of which 28 were waited for; matrix products, arithmetic and copies ran while one was open for 13% of the time, Pallas kernels for 0%

commit v1 on v0

v1 whole, which is shorter than its diff:
```python
import functools

import jax
import jax.numpy as jnp
from jax import lax
from jax.experimental import pallas as pl
from jax.experimental.pallas import tpu as pltpu
from jax.sharding import PartitionSpec as P

HQ = 9
HK = 3
HD = 64
GROUP = HQ // HK
LANES = 128

epsilon = 1e-05
rope_base = 100000.0
masked_score = -1e30

BF = jnp.bfloat16
F32 = jnp.float32
VMEM_LIMIT = 56 * 1024 * 1024

IN_VMEM = pl.BlockSpec(memory_space=pltpu.VMEM)
IN_SMEM = pl.BlockSpec(memory_space=pltpu.SMEM)
ANYWHERE = pl.BlockSpec(memory_space=pl.ANY)


def nn(a, b):
    return lax.dot_general(a, b, (((1,), (0,)), ((), ())), preferred_element_type=F32)


def nt(a, b):
    return lax.dot_general(a, b, (((1,), (1,)), ((), ())), preferred_element_type=F32)


def tn(a, b):
    return lax.dot_general(a, b, (((0,), (0,)), ((), ())), preferred_element_type=F32)


def shape(dims, kind):
    return jax.ShapeDtypeStruct(dims, kind)


def call(kernel, outs, in_specs, scratch, args, flops):
    moved = sum(a.size * a.dtype.itemsize for a in args)
    moved += sum(o.size * o.dtype.itemsize for o in outs)
    return pl.pallas_call(
        kernel,
        out_shape=tuple(outs),
        in_specs=in_specs,
        out_specs=tuple(IN_VMEM for _ in outs),
        scratch_shapes=scratch,
        compiler_params=pltpu.CompilerParams(vmem_limit_bytes=VMEM_LIMIT),
        cost_estimate=pl.CostEstimate(flops=flops, bytes_accessed=moved, transcendentals=0),
    )(*args)


def fetch(flag, yes_ref, no_ref, target, sem):
    @pl.when(flag)
    def _():
        pltpu.make_async_copy(yes_ref, target, sem).start()

    @pl.when(jnp.logical_not(flag))
    def _():
        pltpu.make_async_copy(no_ref, target, sem).start()


def arrive(ref, target, sem):
    pltpu.make_async_copy(ref, target, sem).wait()


def norm_scale(z):
    return lax.rsqrt(jnp.mean(z * z, axis=-1, keepdims=True) + epsilon)


def gain_row(tile):
    lane = lax.broadcasted_iota(jnp.int32, (8, LANES), 1)
    pick = jnp.where(lane == 0, 1.0, 0.0).astype(BF)
    return nt(pick, tile)[0:1]


def gain_tile(rows):
    return tn(rows.astype(BF), jnp.ones((rows.shape[0], LANES), BF)).astype(BF)


def wide(table, width):
    return jnp.concatenate([table] * (width // LANES), axis=1)


def low_half(width, rows):
    lane = lax.broadcasted_iota(jnp.int32, (rows, width), 1)
    return lax.rem(lane, HD) < HD // 2


def rot(a, cosine, sine):
    width = a.shape[1]
    up = pltpu.roll(a, HD // 2, 1)
    down = pltpu.roll(a, width - HD // 2, 1)
    turned = jnp.where(low_half(width, a.shape[0]), -down, up)
    return a * wide(cosine, width) + turned * wide(sine, width)


def rot_back(b, cosine, sine):
    width = b.shape[1]
    c = b * wide(sine, width)
    up = pltpu.roll(c, HD // 2, 1)
    down = pltpu.roll(c, width - HD // 2, 1)
    turned = jnp.where(low_half(width, b.shape[0]), down, -up)
    return b * wide(cosine, width) + turned


def attn_in_kernel(layer, idx, x, a_own, a_got, v_own, v_got, cos, sin, normed_out, q_out, kv_out, a_w, v_w, sems):
    own = idx[0] == layer
    fetch(own, a_own, a_got, a_w, sems.at[0])
    fetch(own, v_own, v_got, v_w, sems.at[1])
    z = x[...].astype(F32)
    scaled = z * norm_scale(z)
    arrive(a_own, a_w, sems.at[0])
    width = (HQ + HK) * HD
    gain = gain_row(a_w[:, width:])
    normed = (scaled * gain).astype(BF)
    normed_out[...] = normed
    qk = rot(nn(normed, a_w[:, :width]), cos[...], sin[...])
    q_out[...] = (qk[:, : HQ * HD].astype(BF).astype(F32) * HD ** (-0.5)).astype(BF)
    arrive(v_own, v_w, sems.at[1])
    value = nn(normed, v_w[:, :width])[:, HQ * HD :]
    kv_out[...] = jnp.concatenate([qk[:, HQ * HD :].astype(BF), value.astype(BF)], axis=1)


def attn_in(layer, idx, x, weights, cos, sin):
    rows, depth = x.shape
    a_own, a_got, v_own, v_got = weights
    args = (idx, x, a_own, a_got, v_own, v_got, cos, sin)
    return call(
        functools.partial(attn_in_kernel, layer),
        (shape((rows, depth), BF), shape((rows, HQ * HD), BF), shape((rows, 2 * HK * HD), BF)),
        [IN_SMEM, IN_VMEM] + [ANYWHERE] * 4 + [IN_VMEM] * 2,
        [pltpu.VMEM(a_own.shape, BF), pltpu.VMEM(v_own.shape, BF), pltpu.SemaphoreType.DMA((2,))],
        args,
        2 * rows * depth * 1536,
    )


def score_block(keys, query, block, reach, causal):
    s = nt(keys, query)
    if block == 0:
        return jnp.where(causal, s, masked_score)
    return jnp.where(block <= reach, s, masked_score)


def causal_mask(rows):
    key_at = lax.broadcasted_iota(jnp.int32, (rows, rows), 0)
    query_at = lax.broadcasted_iota(jnp.int32, (rows, rows), 1)
    return key_at <= query_at


def head(values, at):
    return values[:, at * HD : (at + 1) * HD]


def attend_kernel(blocks, idx, q, *refs):
    kv = [r[...] for r in refs[:blocks]]
    attn_out, lse_out = refs[blocks:]
    rows = q.shape[0]
    reach = idx[1]
    causal = causal_mask(rows)
    queries = q[...]
    pieces = []
    lse_out[...] = jnp.zeros_like(lse_out)
    for g in range(HK):
        keys = [head(b, g) for b in kv]
        values = jnp.concatenate([head(b, HK + g) for b in kv], axis=0)
        for i in range(GROUP):
            h = g * GROUP + i
            query = head(queries, h)
            s = jnp.concatenate(
                [score_block(k, query, d, reach, causal) for d, k in enumerate(keys)], axis=0
            )
            top = jnp.max(s, axis=0, keepdims=True)
            p = jnp.exp(s - top)
            total = jnp.sum(p, axis=0, keepdims=True)
            lse_out[h : h + 1, :] = top + jnp.log(total)
            p_low = (p * (1.0 / total)).astype(BF)
            pieces.append(tn(p_low, values).astype(BF))
    attn_out[...] = jnp.concatenate(pieces, axis=1)


def attend(idx, q, kv):
    rows = q.shape[0]
    return call(
        functools.partial(attend_kernel, len(kv)),
        (shape((rows, HQ * HD), BF), shape((16, rows), F32)),
        [IN_SMEM] + [IN_VMEM] * (1 + len(kv)),
        [],
        (idx, q) + tuple(kv),
        2 * 2 * rows * rows * len(kv) * HQ * HD * 4,
    )


def mlp_kernel(layer, idx, x, attn, v_own, v_got, g_m, g_t, d, y_out, resid_out, mn_out, gate_out, up_out, hid_out, v_w, sems):
    own = idx[0] == layer
    first = idx[0] == 0
    fetch(own, v_own, v_got, v_w, sems.at[0])
    arrive(v_own, v_w, sems.at[0])
    width = HQ * HD
    depth = x.shape[1]
    resid = x[...].astype(F32) + nn(attn[...], v_w[:, :depth])
    resid_out[...] = resid
    gain = gain_row(v_w[:, width + HK * HD :])
    mn = (resid * norm_scale(resid) * gain).astype(BF)
    mn_out[...] = mn
    mine = nn(mn, g_m[...])
    theirs = nn(mn, g_t[...])
    gate = jnp.where(first, mine, theirs)
    up = jnp.where(first, theirs, mine)
    gate_out[...] = gate
    up_out[...] = up
    hid = (gate * jax.nn.sigmoid(gate) * up).astype(BF)
    hid_out[...] = hid
    y_out[...] = (resid + nn(hid, d[...])).astype(BF)


def mlp(layer, idx, x, attn, weights, g_m, g_t, d):
    rows, depth = x.shape
    _, _, v_own, v_got = weights
    ff = g_m.shape[1]
    args = (idx, x, attn, v_own, v_got, g_m, g_t, d)
    return call(
        functools.partial(mlp_kernel, layer),
        (
            shape((rows, depth), BF),
            shape((rows, depth), F32),
            shape((rows, depth), BF),
            shape((rows, ff), F32),
            shape((rows, ff), F32),
            shape((rows, ff), BF),
        ),
        [IN_SMEM, IN_VMEM, IN_VMEM] + [ANYWHERE] * 2 + [IN_VMEM] * 3,
        [pltpu.VMEM(v_own.shape, BF), pltpu.SemaphoreType.DMA((1,))],
        args,
        2 * rows * depth * (3 * ff + depth),
    )


def mlp_back_kernel(layer, idx, e, resid, gate, up, g_m, g_t, d, v_own, v_got, gm_out, gt_out, rg_out, mix_out, ag_out, mg_out, v_w, sems):
    own = idx[0] == layer
    first = idx[0] == 0
    fetch(own, v_own, v_got, v_w, sems.at[0])
    low = e[...]
    hg = nt(low, d[...])
    gv = gate[...]
    sig = jax.nn.sigmoid(gv)
    g_in = (hg * up[...] * sig * (1.0 + gv * (1.0 - sig))).astype(BF)
    u_in = (hg * gv * sig).astype(BF)
    mine = jnp.where(first, g_in, u_in)
    theirs = jnp.where(first, u_in, g_in)
    gm_out[...] = mine
    gt_out[...] = theirs
    ng = nt(mine, g_m[...]) + nt(theirs, g_t[...])
    arrive(v_own, v_w, sems.at[0])
    width = HQ * HD
    depth = e.shape[1]
    gain = gain_row(v_w[:, width + HK * HD :])
    z = resid[...]
    inv = norm_scale(z)
    weighted = ng * gain
    mg_out[...] = gain_tile(ng * z * inv)
    part = inv * weighted - z * (inv * inv * inv) * jnp.mean(z * weighted, axis=-1, keepdims=True)
    rg = low.astype(F32) + part
    rg_out[...] = rg
    mix = rg.astype(BF)
    mix_out[...] = mix
    ag_out[...] = nt(mix, v_w[:, :depth]).astype(BF)


def mlp_back(layer, idx, e, resid, gate, up, g_m, g_t, d, weights):
    rows, depth = e.shape
    _, _, v_own, v_got = weights
    ff = g_m.shape[1]
    args = (idx, e, resid, gate, up, g_m, g_t, d, v_own, v_got)
    return call(
        functools.partial(mlp_back_kernel, layer),
        (
            shape((rows, ff), BF),
            shape((rows, ff), BF),
            shape((rows, depth), F32),
            shape((rows, depth), BF),
            shape((rows, HQ * HD), BF),
            shape((depth, LANES), BF),
        ),
        [IN_SMEM] + [IN_VMEM] * 7 + [ANYWHERE] * 2,
        [pltpu.VMEM(v_own.shape, BF), pltpu.SemaphoreType.DMA((1,))],
        args,
        2 * rows * depth * (3 * ff + depth),
    )


def mlp_grads_kernel(hid, e, mn, gm, gt, attn, mix, mg, ggm_out, ggt_out, dg_out, og_out):
    mnv = mn[...]
    ggm_out[...] = tn(mnv, gm[...]).astype(BF)
    ggt_out[...] = tn(mnv, gt[...]).astype(BF)
    dg_out[...] = tn(hid[...], e[...]).astype(BF)
    depth = mn.shape[1]
    width = (HQ + HK) * HD
    og_out[...] = jnp.zeros_like(og_out)
    og_out[:, :depth] = tn(attn[...], mix[...]).astype(BF)
    og_out[:, width:] = mg[...]


def mlp_grads(hid, e, mn, gm, gt, attn, mix, mg):
    rows, depth = e.shape
    ff = gm.shape[1]
    return call(
        mlp_grads_kernel,
        (
            shape((depth, ff), BF),
            shape((depth, ff), BF),
            shape((ff, depth), BF),
            shape((depth, (HQ + HK) * HD + LANES), BF),
        ),
        [IN_VMEM] * 8,
        [],
        (hid, e, mn, gm, gt, attn, mix, mg),
        2 * rows * depth * (3 * ff + depth),
    )


def attend_back_kernel(blocks, idx, q, ag, lse, *refs):
    kv = [r[...] for r in refs[:blocks]]
    dq_out, own_out = refs[blocks : blocks + 2]
    far_out = refs[blocks + 2 :]
    rows = q.shape[0]
    reach = idx[1]
    causal = causal_mask(rows)
    queries = q[...]
    grads = ag[...]
    dq_parts = []
    dk_parts = []
    dv_parts = []
    for g in range(HK):
        keys = [head(b, g) for b in kv]
        all_keys = jnp.concatenate(keys, axis=0)
        values = jnp.concatenate([head(b, HK + g) for b in kv], axis=0)
        dk = None
        dv = None
        for i in range(GROUP):
            h = g * GROUP + i
            query = head(queries, h)
            grad = head(grads, h)
            s = jnp.concatenate(
                [score_block(k, query, d, reach, causal) for d, k in enumerate(keys)], axis=0
            )
            p = jnp.exp(s - lse[h : h + 1, :])
            dp = nt(values, grad)
            delta = jnp.sum(p * dp, axis=0, keepdims=True)
            ds = (p * (dp - delta)).astype(BF)
            dv_h = nn(p.astype(BF), grad)
            dk_h = nn(ds, query)
            dk = dk_h if dk is None else dk + dk_h
            dv = dv_h if dv is None else dv + dv_h
            dq_parts.append(tn(ds, all_keys) * HD ** (-0.5))
        dk_parts.append(dk)
        dv_parts.append(dv)
    dq_out[...] = jnp.concatenate(dq_parts, axis=1)
    joined = jnp.concatenate(dk_parts + dv_parts, axis=1)
    own_out[...] = joined[:rows]
    for d, out in enumerate(far_out):
        out[...] = joined[(d + 1) * rows : (d + 2) * rows].astype(BF)


def attend_back(idx, q, ag, lse, kv):
    rows = q.shape[0]
    outs = [shape((rows, HQ * HD), F32), shape((rows, 2 * HK * HD), F32)]
    outs += [shape((rows, 2 * HK * HD), BF) for _ in kv[1:]]
    return call(
        functools.partial(attend_back_kernel, len(kv)),
        outs,
        [IN_SMEM] + [IN_VMEM] * (3 + len(kv)),
        [],
        (idx, q, ag, lse) + tuple(kv),
        5 * 2 * rows * rows * len(kv) * HQ * HD * 4,
    )


def input_back_kernel(layer, far, idx, x, normed, dq, own_kv, *refs):
    far_kv = refs[:far]
    rg, a_own, a_got, v_own, v_got, cos, sin, og, ig_out, m_out, t_out, a_w, v_w, sems = refs[far:]
    own = idx[0] == layer
    first = idx[0] == 0
    fetch(own, a_own, a_got, a_w, sems.at[0])
    fetch(own, v_own, v_got, v_w, sems.at[1])
    kv = own_kv[...]
    for r in far_kv:
        kv = kv + r[...].astype(F32)
    half = HK * HD
    qk = jnp.concatenate([dq[...], kv[:, :half]], axis=1)
    qk_in = rot_back(qk, cos[...], sin[...]).astype(BF)
    v_in = kv[:, half:].astype(BF)
    rows, depth = x.shape
    width = (HQ + HK) * HD
    padded = jnp.concatenate([jnp.zeros((rows, HQ * HD), BF), v_in], axis=1)
    arrive(a_own, a_w, sems.at[0])
    arrive(v_own, v_w, sems.at[1])
    ng = nt(qk_in, a_w[:, :width]) + nt(padded, v_w[:, :width])
    z = x[...].astype(F32)
    gain = gain_row(a_w[:, width:])
    inv = norm_scale(z)
    weighted = ng * gain
    part = inv * weighted - z * (inv * inv * inv) * jnp.mean(z * weighted, axis=-1, keepdims=True)
    ig_out[...] = (rg[...] + part).astype(BF)
    nv = normed[...]
    qk_grad = jnp.concatenate([tn(nv, qk_in).astype(BF), gain_tile(ng * z * inv)], axis=1)
    lanes = lax.broadcasted_iota(jnp.int32, (depth, width), 1)
    v_grad = tn(nv, padded).astype(BF)
    ogv = og[...]
    merged = jnp.where(lanes < HQ * HD, ogv[:, :width], v_grad)
    vo_grad = jnp.concatenate([merged, ogv[:, width:]], axis=1)
    m_out[...] = jnp.where(first, qk_grad, vo_grad)
    t_out[...] = jnp.where(first, vo_grad, qk_grad)


def input_back(layer, idx, x, normed, dq, own_kv, far_kv, rg, weights, cos, sin, og):
    rows, depth = x.shape
    a_own, a_got, v_own, v_got = weights
    args = (idx, x, normed, dq, own_kv) + tuple(far_kv)
    args += (rg, a_own, a_got, v_own, v_got, cos, sin, og)
    return call(
        functools.partial(input_back_kernel, layer, len(far_kv)),
        (shape((rows, depth), BF), shape(a_own.shape, BF), shape(a_own.shape, BF)),
        [IN_SMEM] + [IN_VMEM] * (5 + len(far_kv)) + [ANYWHERE] * 4 + [IN_VMEM] * 3,
        [pltpu.VMEM(a_own.shape, BF), pltpu.VMEM(v_own.shape, BF), pltpu.SemaphoreType.DMA((2,))],
        args,
        2 * 2 * rows * depth * 1536,
    )


def crossed(value, axis, mask):
    count = lax.axis_size(axis)
    return lax.ppermute(value, axis, [(i, i ^ mask) for i in range(count)])


def shifted(value, distance):
    devices = range(lax.axis_size("ctx"))
    return lax.ppermute(value, "ctx", [(i, i + distance) for i in devices if i + distance in devices])


def other_core(value):
    return crossed(value, "section", 1)


def bits_of(count):
    return [b for b in range(count.bit_length() - 1)]


def gather_rows(piece, order):
    me = lax.axis_index("fsdp")
    count = lax.axis_size("fsdp")
    have = []
    value = piece
    for bit in order:
        got = crossed(value, "fsdp", 1 << bit)
        low = ((me >> bit) & 1) == 0
        place = sum(1 for b in have if b > bit)
        value = jnp.stack([jnp.where(low, value, got), jnp.where(low, got, value)], axis=place)
        have.append(bit)
    return value.reshape((count * piece.shape[0],) + piece.shape[1:])


def scatter_rows(value, order):
    me = lax.axis_index("fsdp")
    count = lax.axis_size("fsdp")
    bits = len(order)
    rows = value.shape[0] // count
    value = value.reshape((2,) * bits + (rows,) + value.shape[1:])
    left = sorted(order, reverse=True)
    for bit in order:
        mine = (me >> bit) & 1
        place = left.index(bit)
        send = lax.dynamic_index_in_dim(value, 1 - mine, place, keepdims=False)
        keep = lax.dynamic_index_in_dim(value, mine, place, keepdims=False)
        got = crossed(send, "fsdp", 1 << bit)
        value = (keep.astype(F32) + got.astype(F32)).astype(BF)
        left.remove(bit)
    return value


def body(
    inputs,
    positions,
    out_grad,
    attn_gain,
    query_proj,
    key_proj,
    value_proj,
    out_proj,
    mlp_gain,
    gate_proj,
    up_proj,
    down_proj,
):
    core = lax.axis_index("section")
    first = core == 0
    ctx = lax.axis_index("ctx")
    ctx_count = lax.axis_size("ctx")
    fsdp_count = lax.axis_size("fsdp")
    micro, seqs, block, depth = inputs.shape
    shard = query_proj.shape[1]
    rows = seqs * block
    idx = jnp.stack([core, ctx]).astype(jnp.int32)
    up_order = bits_of(fsdp_count)
    down_order = up_order[::-1]

    def pick(a, b):
        return jnp.where(first, a, b)

    def tile_of(gain):
        return jnp.broadcast_to(gain[0][:, None], (shard, LANES))

    a_piece = jnp.concatenate([query_proj[0], key_proj[0], tile_of(attn_gain)], axis=1)
    v_piece = jnp.concatenate([out_proj[0], value_proj[0], tile_of(mlp_gain)], axis=1)
    a_own = gather_rows(a_piece, up_order)
    v_own = gather_rows(v_piece, down_order)
    a_got = other_core(a_own)
    v_got = other_core(v_own)
    attn_w = (a_own, a_got, v_own, v_got)

    half = down_proj.shape[1] // 2
    g_keep = pick(gate_proj[0], up_proj[0])
    g_got = other_core(pick(up_proj[0], gate_proj[0]))
    d_keep = pick(down_proj[0, :half], down_proj[0, half:])
    d_got = other_core(pick(down_proj[0, half:], down_proj[0, :half]))
    g_mine = []
    g_theirs = []
    d_full = []
    for layer in range(2):
        g_piece = pick(g_keep, g_got) if layer == 0 else pick(g_got, g_keep)
        d_piece = pick(d_keep, d_got) if layer == 0 else pick(d_got, d_keep)
        mine = gather_rows(g_piece, up_order)
        g_mine.append(mine)
        g_theirs.append(other_core(mine))
        d_mine = gather_rows(d_piece, down_order).reshape(fsdp_count, half, depth)
        d_other = other_core(d_mine)
        full = jnp.stack([pick(d_mine, d_other), pick(d_other, d_mine)], axis=1)
        d_full.append(full.reshape(2 * fsdp_count * half, depth))

    places = lax.dynamic_index_in_dim(positions, core, 0, keepdims=False).reshape(rows)
    frequency = rope_base ** (-(jnp.arange(HD // 2, dtype=F32) * 2.0 / HD))
    angles = places.astype(F32)[:, None] * frequency
    cos = jnp.concatenate([jnp.cos(angles)] * 4, axis=-1)
    sin = jnp.concatenate([jnp.sin(angles)] * 4, axis=-1)

    x = lax.dynamic_index_in_dim(inputs, core, 0, keepdims=False).reshape(rows, depth)
    saved = []
    for layer in range(2):
        normed, q, kv_own = attn_in(layer, idx, x, attn_w, cos, sin)
        kv = [kv_own] + [shifted(kv_own, d) for d in range(1, ctx_count)]
        attn, lse = attend(idx, q, kv)
        y, resid, mn, gate, up, hid = mlp(
            layer, idx, x, attn, attn_w, g_mine[layer], g_theirs[layer], d_full[layer]
        )
        saved.append((x, normed, q, kv, attn, lse, resid, mn, gate, up, hid))
        x = y
    outs = [saved[1][0], x]

    e = lax.dynamic_index_in_dim(out_grad, core, 0, keepdims=False).reshape(rows, depth)
    entry = [None, None]
    finished = [None, None]
    for layer in (1, 0):
        x, normed, q, kv, attn, lse, resid, mn, gate, up, hid = saved[layer]
        gm, gt, rg, mix, ag, mg = mlp_back(
            layer, idx, e, resid, gate, up, g_mine[layer], g_theirs[layer], d_full[layer], attn_w
        )
        ggm, ggt, dg, og = mlp_grads(hid, e, mn, gm, gt, attn, mix, mg)
        back = attend_back(idx, q, ag, lse, kv)
        dq, own_kv = back[:2]
        far_kv = [shifted(part, -(d + 1)) for d, part in enumerate(back[2:])]
        e, a_mine, a_theirs = input_back(
            layer, idx, x, normed, dq, own_kv, far_kv, rg, attn_w, cos, sin, og
        )
        entry[layer] = e

        def joined(mine, theirs):
            got = other_core(theirs)
            return (mine.astype(F32) + got.astype(F32)).astype(BF)

        g_sum = scatter_rows(joined(ggm, ggt), up_order)
        dg = dg.reshape(fsdp_count, 2, half, depth)
        d_mine = lax.dynamic_index_in_dim(dg, core, 1, keepdims=False)
        d_theirs = lax.dynamic_index_in_dim(dg, 1 - core, 1, keepdims=False)
        d_sum = scatter_rows(joined(d_mine, d_theirs).reshape(fsdp_count * half, depth), down_order)
        a_sum = scatter_rows(joined(a_mine, a_theirs), up_order)
        finished[layer] = tuple(lax.psum(v, "ctx") for v in (g_sum, d_sum, a_sum))

    def own_layer(zero, one):
        keep = pick(zero, one)
        got = other_core(pick(one, zero))
        return (pick(keep, got), pick(got, keep))

    section_out = jnp.stack(own_layer(outs[0], outs[1])).reshape(1, micro, seqs, block, depth)
    input_grad = jnp.stack(own_layer(entry[0], entry[1])).reshape(1, micro, seqs, block, depth)
    gate_g, up_g = own_layer(finished[0][0], finished[1][0])
    down_g = jnp.concatenate(own_layer(finished[0][1], finished[1][1]), axis=0)
    qk_g, ov_g = own_layer(finished[0][2], finished[1][2])
    qw, kw = HQ * HD, HK * HD

    def out(v):
        return v.astype(F32)[None]

    return (
        section_out,
        input_grad,
        out(qk_g[:, qw + kw]),
        out(qk_g[:, :qw]),
        out(qk_g[:, qw : qw + kw]),
        out(ov_g[:, depth : depth + kw]),
        out(ov_g[:, :depth]),
        out(ov_g[:, depth + kw]),
        out(gate_g),
        out(up_g),
        out(down_g),
    )


def solution(mesh):
    rows = P(None, "fsdp", "ctx", None)
    both = P("section", None, "fsdp", "ctx", None)
    vec = P("section", "fsdp")
    mat = P("section", "fsdp", None)
    return jax.shard_map(
        body,
        mesh=mesh,
        in_specs=(rows, P(None, "fsdp", "ctx"), rows, vec, mat, mat, mat, mat, vec, mat, mat, mat),
        out_specs=(both, both, vec, mat, mat, mat, mat, vec, mat, mat, mat),
        check_vma=False,
    )
```

time: 1120 us -> 508 us (0.45)
  waiting for transfers between devices: 522 us -> 266 us
  local copies, waits for them, and re-layouts: 175 us -> 21.7 us
  Pallas kernels: 0 us -> 105 us
  matrix products: 99.6 us -> 0 us
  starting transfers between devices: 145 us -> 58.7 us
  blocking collectives: 63 us -> 0 us
  other arithmetic: 77.4 us -> 34.2 us
    unnamed x15 -> x1, waiting for transfers between devices: 132 us -> 0.02 us
    reduce_scatter x5 -> x0, waiting for transfers between devices: 120 us -> none  [the longest x1 35.5 us: body(): lax.psum_scatter(down_sum.astype(jnp.bfloat16), 'fsdp', scatter_dimension...]
    pallas_call x0 -> x14, Pallas kernels: none -> 105 us  [call(): pl.pallas_call(kernel, out_shape=tuple(outs), in_specs=in_specs, out_spec...]
    dot_general x49 -> x0, matrix products: 99.6 us -> none  [the longest x14 28.5 us: against(): lax.dot_general(former, latter, (((1,), (1,)), ((), ())), preferred_eleme...]
    all_gather x4 -> x0, waiting for transfers between devices: 94.9 us -> none  [the longest x1 64.8 us: body(): lax.all_gather(summed_part.astype(jnp.bfloat16), 'ctx', axis=0, tiled=True)]
    ppermute x34 -> x55, starting transfers between devices: 144 us -> 58.6 us  [the longest x12 33.5 us: shifted(): lax.ppermute(value, 'ctx', [(i, i + distance) for i in devices if i + dis...]
    psum x0 -> x1, waiting for transfers between devices: none -> 73.8 us  [body(): finished[layer] = tuple((lax.psum(v, 'ctx') for v in (g_sum, d_sum, a_sum)))]
    all_gather x5 -> x0, blocking collectives: 54.1 us -> none  [the longest x1 12.9 us: body(): lax.all_gather(value_proj[0], 'fsdp', axis=0, tiled=True)]
  transfers between devices with their start and end apart: 46 -> 56, of which waited for: 28 -> 23; matrix products, arithmetic and copies ran while one was open for 13% -> 9% of each run, Pallas kernels for 0% -> 16%
where the time goes in v1:
time: 508 us; the launch traced here: 501 us
  waiting for transfers between devices  266 us (52%)
  Pallas kernels  105 us (21%)
  starting transfers between devices  58.7 us (12%)
  other arithmetic  34.2 us (7%)
  local copies, waits for them, and re-layouts  21.7 us (4%)
  between operations  15.6 us (3%)
    ppermute x43, waiting for transfers between devices, crossed(): return lax.ppermute(value, axis, [(i, i ^ mask) for i in range(count)])  161 us
    pallas_call x14, Pallas kernels, call(): pl.pallas_call(kernel, out_shape=tuple(outs), in_specs=in_specs, out_spec...  105 us
    psum x1, waiting for transfers between devices, body(): finished[layer] = tuple((lax.psum(v, 'ctx') for v in (g_sum, d_sum, a_sum)))  73.8 us
    ppermute x12, starting transfers between devices, shifted(): lax.ppermute(value, 'ctx', [(i, i + distance) for i in devices if i + dis...  33.5 us
    ppermute x12, waiting for transfers between devices, shifted(): lax.ppermute(value, 'ctx', [(i, i + distance) for i in devices if i + dis...  31.3 us
    ppermute x43, starting transfers between devices, crossed(): return lax.ppermute(value, axis, [(i, i ^ mask) for i in range(count)])  25.2 us
  transfers between devices with their start and end apart: 56, of which 23 were waited for; matrix products, arithmetic and copies ran while one was open for 9% of the time, Pallas kernels for 16%

profile of v1, /device:TPU:0, one launch (start us, length us, event | category | flops | bytes accessed | tf_op | source)
XLA Modules:
  0.0 500.8 jit_solution(1111475715384946090)
XLA Ops:
  12.0 3.0 collective-permute-start.3
  15.2 1.6 collective-permute-start
  28.1 3.7 collective-permute-done.23
  34.4 1.6 collective-permute-start.20
  37.8 3.1 collective-permute-done.4
  41.7 4.8 collective-permute-done.1
  46.8 31.9 %collective-permute-done.10 = bf16[144,1536]{1,0:T(8,128)(2,1)S(1)} collective-permute-done((bf16[144,1536]{1,0:T(8,128)(2,1)S(1)}, bf16[144,1536]{1,0:T(8,128)(2,1)S(1)}, u32[]{:S(2)}, u32[]{:S(2)}) %collective-permute-start.10) | collective-permute-done | bytes 442400 | tf_op jit(solution)/shard_map/ppermute | solution.py:440
  79.7 1.6 collective-permute-start.21
  82.6 18.9 %collective-permute-done.11 = bf16[2,144,1536]{2,1,0:T(8,128)(2,1)S(1)} collective-permute-done((bf16[2,144,1536]{2,1,0:T(8,128)(2,1)S(1)}, bf16[2,144,1536]{2,1,0:T(8,128)(2,1)S(1)}, u32[]{:S(2)}, u32[]{:S(2)}) %collective-permute-start.11) | collective-permute-done | bytes 884768 | tf_op jit(solution)/shard_map/ppermute | solution.py:440
  101.8 18.3 %collective-permute-done.21 = bf16[2,144,1536]{2,1,0:T(8,128)(2,1)S(1)} collective-permute-done((bf16[2,144,1536]{2,1,0:T(8,128)(2,1)S(1)}, bf16[2,144,1536]{2,1,0:T(8,128)(2,1)S(1)}, u32[]{:S(2)}, u32[]{:S(2)}) %collective-permute-start.21) | collective-permute-done | bytes 884768 | tf_op jit(solution)/shard_map/ppermute | solution.py:440
  122.3 4.3 shard_map.203
  126.6 3.5 collective-permute-start.6
  132.3 4.5 collective-permute-start.7
  136.8 6.5 %collective-permute-start.8 = (bf16[256,384]{1,0:T(8,128)(2,1)S(1)}, bf16[256,384]{1,0:T(8,128)(2,1)S(1)}, u32[]{:S(2)}, u32[]{:S(2)}) collective-permute-start(bf16[256,384]{1,0:T(8,128)(2,1)S(1)} %copy-done.41), channel_id=1, source_target_pairs={{0,12},{1,13},{2,14},{3,15},{16,28},{17,29},{18,30},{19,31}} | collective-permute-start | bytes 589832 | tf_op jit(solution)/shard_map/ppermute | solution.py:445
  143.3 1.7 select_bitcast_fusion.3
  147.5 8.5 %shard_map.204 = (bf16[256,576]{1,0:T(8,128)(2,1)}, f32[16,256]{1,0:T(8,128)}) custom-call(s32[2]{0:T(128)} %pad_add_fusion.idx, bf16[256,576]{1,0:T(8,128)(2,1)} %get-tuple-element.69.q, bf16[256,384]{1,0:T(8,128)(2,1)} %get-tuple-element.70.refs_0_, bf16[256,384]{1,0:T(8,128)(2,1)} %copy-done.42, bf16[256,384]{1,0:T(8,128)(2,1)} %copy-done.43, ...), custom_call_target="tpu_custom_call" | custom-call | flops 2415919104 | bytes 1392648 | tf_op jit(solution)/shard_map/pallas_call | solution.py:48
  156.0 8.2 %shard_map.205 = (bf16[256,576]{1,0:T(8,128)(2,1)}, f32[256,576]{1,0:T(8,128)}, bf16[256,576]{1,0:T(8,128)(2,1)}, f32[256,1536]{1,0:T(8,128)}, f32[256,1536]{1,0:T(8,128)}, /*index=5*/bf16[256,1536]{1,0:T(8,128)(2,1)}) custom-call(s32[2]{0:T(128)} %pad_add_fusion.idx, bf16[256,576]{1,0:T(8,128)(2,1)} %bitcast.248, bf16[256,576]{1,0:T(8,128)(2,1)} %get-tuple-element.71.attn, ...), custom_call_target="tpu_custom_call" | custom-call | flops 1528823808 | bytes 13074440 | tf_op jit(solution)/shard_map/pallas_call | solution.py:48
  164.2 4.3 shard_map.206
  168.5 4.0 collective-permute-start.17
  172.5 5.3 %collective-permute-start.18 = (bf16[256,384]{1,0:T(8,128)(2,1)}, bf16[256,384]{1,0:T(8,128)(2,1)S(1)}, u32[]{:S(2)}, u32[]{:S(2)}) collective-permute-start(bf16[256,384]{1,0:T(8,128)(2,1)} %get-tuple-element.74.refs_0_), channel_id=1, source_target_pairs={{0,8},{4,12},{1,9},{5,13},{2,10},{6,14},{3,11},{7,15},{16,24},{20,... | collective-permute-start | bytes 589832 | tf_op jit(solution)/shard_map/ppermute | solution.py:445
  177.8 1.7 collective-permute-start.19
  181.6 1.8 collective-permute-done.18.refs_2_
  183.4 2.1 collective-permute-done.19.refs_3_
  186.2 8.5 %shard_map.207 = (bf16[256,576]{1,0:T(8,128)(2,1)}, f32[16,256]{1,0:T(8,128)}) custom-call(s32[2]{0:T(128)} %pad_add_fusion.idx, bf16[256,576]{1,0:T(8,128)(2,1)} %get-tuple-element.73.q, bf16[256,384]{1,0:T(8,128)(2,1)} %get-tuple-element.74.refs_0_, bf16[256,384]{1,0:T(8,128)(2,1)} %copy-done.45, bf16[256,384]{1,0:T(8,128)(2,1)} %copy-done.46, ...), custom_call_target="tpu_custom_call" | custom-call | flops 2415919104 | bytes 1392648 | tf_op jit(solution)/shard_map/pallas_call | solution.py:48
  194.7 8.2 %shard_map.208 = (bf16[256,576]{1,0:T(8,128)(2,1)}, f32[256,576]{1,0:T(8,128)}, bf16[256,576]{1,0:T(8,128)(2,1)}, f32[256,1536]{1,0:T(8,128)}, f32[256,1536]{1,0:T(8,128)}, /*index=5*/bf16[256,1536]{1,0:T(8,128)(2,1)}) custom-call(s32[2]{0:T(128)} %pad_add_fusion.idx, bf16[256,576]{1,0:T(8,128)(2,1)} %get-tuple-element.72.x, ...), custom_call_target="tpu_custom_call" | custom-call | flops 1528823808 | bytes 13074440 | tf_op jit(solution)/shard_map/pallas_call | solution.py:48
  202.8 8.3 %shard_map.209 = (bf16[256,1536]{1,0:T(8,128)(2,1)}, bf16[256,1536]{1,0:T(8,128)(2,1)}, f32[256,576]{1,0:T(8,128)}, bf16[256,576]{1,0:T(8,128)(2,1)}, bf16[256,5...) custom-call(s32[2]{0:T(128)} %pad_add_fusion.idx, bf16[256,576]{1,0:T(8,128)(2,1)} %bitcast.263, ...), custom_call_target="tpu_custom_call" | custom-call | flops 1528823808 | bytes 14303240 | tf_op jit(solution)/shard_map/pallas_call | solution.py:48
  211.1 11.0 %shard_map.210 = (f32[256,576]{1,0:T(8,128)}, f32[256,384]{1,0:T(8,128)}, bf16[256,384]{1,0:T(8,128)(2,1)}, bf16[256,384]{1,0:T(8,128)(2,1)}, bf16[256,384]{1,0:T(8,128)(2,1)}) custom-call(s32[2]{0:T(128)} %pad_add_fusion.idx, bf16[256,576]{1,0:T(8,128)(2,1)} %get-tuple-element.73.q, bf16[256,576]{1,0:T(8,128)(2,1)} %get-tuple-element.82.ag, ...), custom_call_target="tpu_custom_call" | custom-call | flops 6039797760 | bytes 2965512 | tf_op jit(solution)/shard_map/pallas_call | solution.py:48
  226.3 5.6 %shard_map.211 = (bf16[576,1536]{1,0:T(8,128)(2,1)}, bf16[576,1536]{1,0:T(8,128)(2,1)}, bf16[1536,576]{1,0:T(8,128)(2,1)}, bf16[576,896]{1,0:T(8,128)(2,1)}) custom-call(bf16[256,1536]{1,0:T(8,128)(2,1)} %get-tuple-element.90.hid, bf16[256,576]{1,0:T(8,128)(2,1)} %bitcast.264, bf16[256,576]{1,0:T(8,128)(2,1)} %get-tuple-element.91.mn, ...), custom_call_target="tpu_custom_call" | custom-call | flops 1528823808 | bytes 10027008 | tf_op jit(solution)/shard_map/pallas_call | solution.py:48
  231.8 2.2 dynamic-slice_bitcast_fusion
  234.1 11.1 %collective-permute-done.28.refs_1_ = bf16[256,384]{1,0:T(8,128)(2,1)S(1)} collective-permute-done((bf16[256,384]{1,0:T(8,128)(2,1)}, bf16[256,384]{1,0:T(8,128)(2,1)S(1)}, u32[]{:S(2)}, u32[]{:S(2)}) %collective-permute-start.28) | collective-permute-done | bytes 196640 | tf_op jit(solution)/shard_map/ppermute | solution.py:445
  246.0 6.6 %shard_map.212 = (bf16[256,576]{1,0:T(8,128)(2,1)}, bf16[576,896]{1,0:T(8,128)(2,1)}, bf16[576,896]{1,0:T(8,128)(2,1)}) custom-call(s32[2]{0:T(128)} %pad_add_fusion.idx, bf16[256,576]{1,0:T(8,128)(2,1)} %get-tuple-element.72.x, bf16[256,576]{1,0:T(8,128)(2,1)} %get-tuple-element.78.normed, f32[256,576]{1,0:T(8,128)} %get-tuple-element.84.dq, ...), custom_call_target="tpu_custom_call" | custom-call | flops 905969664 | bytes 10534920 | tf_op jit(solution)/shard_map/pallas_call | solution.py:48
  252.6 8.2 %shard_map.213 = (bf16[256,1536]{1,0:T(8,128)(2,1)}, bf16[256,1536]{1,0:T(8,128)(2,1)}, f32[256,576]{1,0:T(8,128)}, bf16[256,576]{1,0:T(8,128)(2,1)}, bf16[256,5...) custom-call(s32[2]{0:T(128)} %pad_add_fusion.idx, bf16[256,576]{1,0:T(8,128)(2,1)} %get-tuple-element.97.e, ...), custom_call_target="tpu_custom_call" | custom-call | flops 1528823808 | bytes 14303240 | tf_op jit(solution)/shard_map/pallas_call | solution.py:48
  260.8 5.6 %shard_map.215 = (bf16[576,1536]{1,0:T(8,128)(2,1)}, bf16[576,1536]{1,0:T(8,128)(2,1)}, bf16[1536,576]{1,0:T(8,128)(2,1)}, bf16[576,896]{1,0:T(8,128)(2,1)}) custom-call(bf16[256,1536]{1,0:T(8,128)(2,1)} %get-tuple-element.109.hid, bf16[256,576]{1,0:T(8,128)(2,1)} %get-tuple-element.97.e, bf16[256,576]{1,0:T(8,128)(2,1)} %get-tuple-element.110.mn, ...), custom_call_target="tpu_custom_call" | custom-call | flops 1528823808 | bytes 10027008 | tf_op jit(solution)/shard_map/pallas_call | solution.py:48
  266.4 2.3 dynamic-slice_bitcast_fusion.1
  268.7 11.1 %shard_map.214 = (f32[256,576]{1,0:T(8,128)}, f32[256,384]{1,0:T(8,128)}, bf16[256,384]{1,0:T(8,128)(2,1)}, bf16[256,384]{1,0:T(8,128)(2,1)}, bf16[256,384]{1,0:T(8,128)(2,1)}) custom-call(s32[2]{0:T(128)} %pad_add_fusion.idx, bf16[256,576]{1,0:T(8,128)(2,1)} %get-tuple-element.69.q, bf16[256,576]{1,0:T(8,128)(2,1)} %get-tuple-element.101.ag, ...), custom_call_target="tpu_custom_call" | custom-call | flops 6039797760 | bytes 2965512 | tf_op jit(solution)/shard_map/pallas_call | solution.py:48
  283.7 7.4 %collective-permute-done.30.refs_0_ = bf16[256,384]{1,0:T(8,128)(2,1)S(1)} collective-permute-done((bf16[256,384]{1,0:T(8,128)(2,1)}, bf16[256,384]{1,0:T(8,128)(2,1)S(1)}, u32[]{:S(2)}, u32[]{:S(2)}) %collective-permute-start.30) | collective-permute-done | bytes 196640 | tf_op jit(solution)/shard_map/ppermute | solution.py:445
  291.1 8.8 %collective-permute-done.31.refs_1_ = bf16[256,384]{1,0:T(8,128)(2,1)S(1)} collective-permute-done((bf16[256,384]{1,0:T(8,128)(2,1)}, bf16[256,384]{1,0:T(8,128)(2,1)S(1)}, u32[]{:S(2)}, u32[]{:S(2)}) %collective-permute-start.31) | collective-permute-done | bytes 196640 | tf_op jit(solution)/shard_map/ppermute | solution.py:445
  300.7 6.7 %shard_map.216 = (bf16[256,576]{1,0:T(8,128)(2,1)}, bf16[576,896]{1,0:T(8,128)(2,1)}, bf16[576,896]{1,0:T(8,128)(2,1)}) custom-call(s32[2]{0:T(128)} %pad_add_fusion.idx, bf16[256,576]{1,0:T(8,128)(2,1)} %bitcast.249, bf16[256,576]{1,0:T(8,128)(2,1)} %get-tuple-element.77.normed, f32[256,576]{1,0:T(8,128)} %get-tuple-element.103.dq, ...), custom_call_target="tpu_custom_call" | custom-call | flops 905969664 | bytes 10534920 | tf_op jit(solution)/shard_map/pallas_call | solution.py:48
  312.3 10.1 %collective-permute-done.52 = bf16[2,192,576]{2,1,0:T(8,128)(2,1)S(1)} collective-permute-done((bf16[2,192,576]{2,1,0:T(8,128)(2,1)S(1)}, bf16[2,192,576]{2,1,0:T(8,128)(2,1)S(1)}, u32[]{:S(2)}, u32[]{:S(2)}) %collective-permute-start.52) | collective-permute-done | bytes 442400 | tf_op jit(solution)/shard_map/ppermute | solution.py:440
  323.2 1.6 collective-permute-start.53
  325.1 7.0 %collective-permute-done.49 = bf16[2,192,576]{2,1,0:T(8,128)(2,1)S(1)} collective-permute-done((bf16[2,192,576]{2,1,0:T(8,128)(2,1)S(1)}, bf16[2,192,576]{2,1,0:T(8,128)(2,1)S(1)}, u32[]{:S(2)}, u32[]{:S(2)}) %collective-permute-start.49) | collective-permute-done | bytes 442400 | tf_op jit(solution)/shard_map/ppermute | solution.py:440
  332.8 9.6 %collective-permute-done.53 = bf16[192,576]{1,0:T(8,128)(2,1)S(1)} collective-permute-done((bf16[192,576]{1,0:T(8,128)(2,1)S(1)}, bf16[192,576]{1,0:T(8,128)(2,1)S(1)}, u32[]{:S(2)}, u32[]{:S(2)}) %collective-permute-start.53) | collective-permute-done | bytes 221216 | tf_op jit(solution)/shard_map/ppermute | solution.py:440
  344.5 11.6 %collective-permute-done.50 = bf16[192,576]{1,0:T(8,128)(2,1)S(1)} collective-permute-done((bf16[192,576]{1,0:T(8,128)(2,1)S(1)}, bf16[192,576]{1,0:T(8,128)(2,1)S(1)}, u32[]{:S(2)}, u32[]{:S(2)}) %collective-permute-start.50) | collective-permute-done | bytes 221216 | tf_op jit(solution)/shard_map/ppermute | solution.py:440
  361.5 3.0 collective-permute-done.36
  365.3 14.7 %collective-permute-done.45 = bf16[2,144,1536]{2,1,0:T(8,128)(2,1)S(1)} collective-permute-done((bf16[2,144,1536]{2,1,0:T(8,128)(2,1)S(1)}, bf16[2,144,1536]{2,1,0:T(8,128)(2,1)S(1)}, u32[]{:S(2)}, u32[]{:S(2)}) %collective-permute-start.45) | collective-permute-done | bytes 884768 | tf_op jit(solution)/shard_map/ppermute | solution.py:440
  380.8 14.5 %collective-permute-done.42 = bf16[2,144,1536]{2,1,0:T(8,128)(2,1)S(1)} collective-permute-done((bf16[2,144,1536]{2,1,0:T(8,128)(2,1)S(1)}, bf16[2,144,1536]{2,1,0:T(8,128)(2,1)S(1)}, u32[]{:S(2)}, u32[]{:S(2)}) %collective-permute-start.42) | collective-permute-done | bytes 884768 | tf_op jit(solution)/shard_map/ppermute | solution.py:440
  397.0 7.2 %collective-permute-done.43 = bf16[144,1536]{1,0:T(8,128)(2,1)S(1)} collective-permute-done((bf16[144,1536]{1,0:T(8,128)(2,1)S(1)}, bf16[144,1536]{1,0:T(8,128)(2,1)S(1)}, u32[]{:S(2)}, u32[]{:S(2)}) %collective-permute-start.43) | collective-permute-done | bytes 442400 | tf_op jit(solution)/shard_map/ppermute | solution.py:440
  409.3 73.8 %all-reduce.3.cloned.1.call-done = (bf16[144,896]{1,0:T(8,128)(2,1)}, bf16[144,896]{1,0:T(8,128)(2,1)}, bf16[144,1536]{1,0:T(8,128)(2,1)}, bf16[144,1536]{1,0:T(...) async-done(((bf16[144,896]{1,0:T(8,128)(2,1)}, bf16[144,896]{1,0:T(8,128)(2,1)}, bf16[144,1536]{1,0:T(8,128)(2,1)}, bf16[144,1536]{1,0:T(8,128)(2,1)}, ...) | async-done | bytes 1843216 | tf_op jit(solution)/shard_map/psum | solution.py:593
  (283 shorter events, 75.6 us)
Async XLA Ops:
  7.2 475.9 %all-reduce.3.cloned.1.call-start = ((), (), s32[]{:S(2)}) async-start(), calls=%async_computation | async-start | bytes 3784704 | tf_op jit(solution)/shard_map/psum | solution.py:593
  9.7 12.1 %collective-permute-start.13 = (bf16[192,576]{1,0:T(8,128)(2,1)}, bf16[192,576]{1,0:T(8,128)(2,1)}, u32[]{:S(2)}, u32[]{:S(2)}) collective-permute-start(bf16[192,576]{1,0:T(8,128)(2,1)} %select_bitcast_fusion.35), channel_id=1, source_target_pairs={{0,16},{16,0},{1,17},{17,1},{2,18},{18,2},{3,19},{19,3},{4,20},{20... | collective-permute-start | bytes 663560 | tf_op jit(solution)/shard_map/ppermute | solution.py:440
  11.0 22.3 %collective-permute-start.9 = (bf16[144,1536]{1,0:T(8,128)(2,1)}, bf16[144,1536]{1,0:T(8,128)(2,1)}, u32[]{:S(2)}, u32[]{:S(2)}) collective-permute-start(bf16[144,1536]{1,0:T(8,128)(2,1)} %select_bitcast_fusion.20), channel_id=1, source_target_pairs={{0,16},{16,0},{1,17},{17,1},{2,18},{18,2},{3,19},{19,3},{4,20},{20... | collective-permute-start | bytes 1327112 | tf_op jit(solution)/shard_map/ppermute | solution.py:440
  12.0 12.9 %collective-permute-start.3 = (bf16[144,896]{1,0:T(8,128)(2,1)}, bf16[144,896]{1,0:T(8,128)(2,1)}, u32[]{:S(2)}, u32[]{:S(2)}) collective-permute-start(bf16[144,896]{1,0:T(8,128)(2,1)} %pad_maximum_fusion.15), channel_id=1, source_target_pairs={{0,2},{1,3},{2,0},{3,1},{4,6},{5,7},{6,4},{7,5},{8,10},{9,11},{10,... | collective-permute-start | bytes 774152 | tf_op jit(solution)/shard_map/ppermute | solution.py:440
  15.2 11.5 %collective-permute-start = (bf16[144,896]{1,0:T(8,128)(2,1)S(1)}, bf16[144,896]{1,0:T(8,128)(2,1)}, u32[]{:S(2)}, u32[]{:S(2)}) collective-permute-start(bf16[144,896]{1,0:T(8,128)(2,1)S(1)} %pad_maximum_fusion.14), channel_id=1, source_target_pairs={{0,1},{1,0},{2,3},{3,2},{4,5},{5,4},{6,7},{7,6},{8,9},{9,8},{10,11... | collective-permute-start | bytes 774152 | tf_op jit(solution)/shard_map/ppermute | solution.py:440
  22.8 9.0 %collective-permute-start.23 = (bf16[192,576]{1,0:T(8,128)(2,1)S(1)}, bf16[192,576]{1,0:T(8,128)(2,1)S(1)}, u32[]{:S(2)}, u32[]{:S(2)}) collective-permute-start(bf16[192,576]{1,0:T(8,128)(2,1)S(1)} %get-tuple-element.187), channel_id=1, source_target_pairs={{0,2},{1,3},{2,0},{3,1},{4,6},{5,7},{6,4},{7,5},{8,10},{9,11},{10,... | collective-permute-start | bytes 663560 | tf_op jit(solution)/shard_map/ppermute | solution.py:440
  23.4 13.7 %collective-permute-start.14 = (bf16[192,576]{1,0:T(8,128)(2,1)S(1)}, bf16[192,576]{1,0:T(8,128)(2,1)S(1)}, u32[]{:S(2)}, u32[]{:S(2)}) collective-permute-start(bf16[192,576]{1,0:T(8,128)(2,1)S(1)} %get-tuple-element.188), channel_id=1, source_target_pairs={{0,2},{1,3},{2,0},{3,1},{4,6},{5,7},{6,4},{7,5},{8,10},{9,11},{10,... | collective-permute-start | bytes 663560 | tf_op jit(solution)/shard_map/ppermute | solution.py:440
  26.1 14.8 %collective-permute-start.4 = (bf16[2,144,896]{2,1,0:T(8,128)(2,1)S(1)}, bf16[2,144,896]{2,1,0:T(8,128)(2,1)S(1)}, u32[]{:S(2)}, u32[]{:S(2)}) collective-permute-start(bf16[2,144,896]{2,1,0:T(8,128)(2,1)S(1)} %pad_maximum_fusion.11), channel_id=1, source_target_pairs={{0,1},{1,0},{2,3},{3,2},{4,5},{5,4},{6,7},{7,6},{8,9},{9,8},{10,11... | collective-permute-start | bytes 1548296 | tf_op jit(solution)/shard_map/ppermute | solution.py:440
  27.9 18.6 %collective-permute-start.1 = (bf16[2,144,896]{2,1,0:T(8,128)(2,1)S(1)}, bf16[2,144,896]{2,1,0:T(8,128)(2,1)S(1)}, u32[]{:S(2)}, u32[]{:S(2)}) collective-permute-start(bf16[2,144,896]{2,1,0:T(8,128)(2,1)S(1)} %pad_maximum_fusion.10), channel_id=1, source_target_pairs={{0,2},{1,3},{2,0},{3,1},{4,6},{5,7},{6,4},{7,5},{8,10},{9,11},{10,... | collective-permute-start | bytes 1548296 | tf_op jit(solution)/shard_map/ppermute | solution.py:440
  32.7 97.4 %collective-permute-start.24 = (bf16[2,192,576]{2,1,0:T(8,128)(2,1)}, bf16[2,192,576]{2,1,0:T(8,128)(2,1)}, u32[]{:S(2)}, u32[]{:S(2)}) collective-permute-start(bf16[2,192,576]{2,1,0:T(8,128)(2,1)} %pad_maximum_fusion.13), channel_id=1, source_target_pairs={{0,1},{1,0},{2,3},{3,2},{4,5},{5,4},{6,7},{7,6},{8,9},{9,8},{10,11... | collective-permute-start | bytes 1327112 | tf_op jit(solution)/shard_map/ppermute | solution.py:440
  34.4 44.6 %collective-permute-start.20 = (bf16[144,1536]{1,0:T(8,128)(2,1)S(1)}, bf16[144,1536]{1,0:T(8,128)(2,1)S(1)}, u32[]{:S(2)}, u32[]{:S(2)}) collective-permute-start(bf16[144,1536]{1,0:T(8,128)(2,1)S(1)} %get-tuple-element.165), channel_id=1, source_target_pairs={{0,1},{1,0},{2,3},{3,2},{4,5},{5,4},{6,7},{7,6},{8,9},{9,8},{10,11... | collective-permute-start | bytes 1327112 | tf_op jit(solution)/shard_map/ppermute | solution.py:440
  37.2 42.5 %collective-permute-start.15 = (bf16[2,192,576]{2,1,0:T(8,128)(2,1)S(1)}, bf16[2,192,576]{2,1,0:T(8,128)(2,1)S(1)}, u32[]{:S(2)}, u32[]{:S(2)}) collective-permute-start(bf16[2,192,576]{2,1,0:T(8,128)(2,1)S(1)} %pad_maximum_fusion.12), channel_id=1, source_target_pairs={{0,1},{1,0},{2,3},{3,2},{4,5},{5,4},{6,7},{7,6},{8,9},{9,8},{10,11... | collective-permute-start | bytes 1327112 | tf_op jit(solution)/shard_map/ppermute | solution.py:440
  40.9 37.9 %collective-permute-start.10 = (bf16[144,1536]{1,0:T(8,128)(2,1)S(1)}, bf16[144,1536]{1,0:T(8,128)(2,1)S(1)}, u32[]{:S(2)}, u32[]{:S(2)}) collective-permute-start(bf16[144,1536]{1,0:T(8,128)(2,1)S(1)} %get-tuple-element.166), channel_id=1, source_target_pairs={{0,1},{1,0},{2,3},{3,2},{4,5},{5,4},{6,7},{7,6},{8,9},{9,8},{10,11... | collective-permute-start | bytes 1327112 | tf_op jit(solution)/shard_map/ppermute | solution.py:440
  46.5 73.8 %collective-permute-start.5 = (bf16[576,896]{1,0:T(8,128)(2,1)S(1)}, bf16[576,896]{1,0:T(8,128)(2,1)S(1)}, u32[]{:S(2)}, u32[]{:S(2)}) collective-permute-start(bf16[576,896]{1,0:T(8,128)(2,1)S(1)} %bitcast.219), channel_id=1, source_target_pairs={{0,16},{16,0},{1,17},{17,1},{2,18},{18,2},{3,19},{19,3},{4,20},{20... | collective-permute-start | bytes 3096584 | tf_op jit(solution)/shard_map/ppermute | solution.py:440
  78.8 42.2 %collective-permute-start.2 = (bf16[576,896]{1,0:T(8,128)(2,1)S(1)}, bf16[576,896]{1,0:T(8,128)(2,1)S(1)}, u32[]{:S(2)}, u32[]{:S(2)}) collective-permute-start(bf16[576,896]{1,0:T(8,128)(2,1)S(1)} %bitcast.228), channel_id=1, source_target_pairs={{0,16},{16,0},{1,17},{17,1},{2,18},{18,2},{3,19},{19,3},{4,20},{20... | collective-permute-start | bytes 3096584 | tf_op jit(solution)/shard_map/ppermute | solution.py:440
  78.9 22.5 %collective-permute-start.11 = (bf16[2,144,1536]{2,1,0:T(8,128)(2,1)S(1)}, bf16[2,144,1536]{2,1,0:T(8,128)(2,1)S(1)}, u32[]{:S(2)}, u32[]{:S(2)}) collective-permute-start(bf16[2,144,1536]{2,1,0:T(8,128)(2,1)S(1)} %pad_maximum_fusion.8), channel_id=1, source_target_pairs={{0,2},{1,3},{2,0},{3,1},{4,6},{5,7},{6,4},{7,5},{8,10},{9,11},{10,... | collective-permute-start | bytes 2654216 | tf_op jit(solution)/shard_map/ppermute | solution.py:440
  79.7 40.3 %collective-permute-start.21 = (bf16[2,144,1536]{2,1,0:T(8,128)(2,1)S(1)}, bf16[2,144,1536]{2,1,0:T(8,128)(2,1)S(1)}, u32[]{:S(2)}, u32[]{:S(2)}) collective-permute-start(bf16[2,144,1536]{2,1,0:T(8,128)(2,1)S(1)} %pad_maximum_fusion.9), channel_id=1, source_target_pairs={{0,2},{1,3},{2,0},{3,1},{4,6},{5,7},{6,4},{7,5},{8,10},{9,11},{10,... | collective-permute-start | bytes 2654216 | tf_op jit(solution)/shard_map/ppermute | solution.py:440
  101.4 30.2 %collective-permute-start.16 = (bf16[4,192,576]{2,1,0:T(8,128)(2,1)}, bf16[4,192,576]{2,1,0:T(8,128)(2,1)}, u32[]{:S(2)}, u32[]{:S(2)}) collective-permute-start(bf16[4,192,576]{2,1,0:T(8,128)(2,1)} %bitcast.32), channel_id=1, source_target_pairs={{0,16},{16,0},{1,17},{17,1},{2,18},{18,2},{3,19},{19,3},{4,20},{20... | collective-permute-start | bytes 2654216 | tf_op jit(solution)/shard_map/ppermute | solution.py:440
  120.0 36.0 %collective-permute-start.12 = (bf16[576,1536]{1,0:T(8,128)(2,1)S(1)}, bf16[576,1536]{1,0:T(8,128)(2,1)}, u32[]{:S(2)}, u32[]{:S(2)}) collective-permute-start(bf16[576,1536]{1,0:T(8,128)(2,1)S(1)} %bitcast.237), channel_id=1, source_target_pairs={{0,16},{16,0},{1,17},{17,1},{2,18},{18,2},{3,19},{19,3},{4,20},{20... | collective-permute-start | bytes 5308424 | tf_op jit(solution)/shard_map/ppermute | solution.py:440
  120.4 74.3 %collective-permute-start.22 = (bf16[576,1536]{1,0:T(8,128)(2,1)S(1)}, bf16[576,1536]{1,0:T(8,128)(2,1)}, u32[]{:S(2)}, u32[]{:S(2)}) collective-permute-start(bf16[576,1536]{1,0:T(8,128)(2,1)S(1)} %bitcast.240), channel_id=1, source_target_pairs={{0,16},{16,0},{1,17},{17,1},{2,18},{18,2},{3,19},{19,3},{4,20},{20... | collective-permute-start | bytes 5308424 | tf_op jit(solution)/shard_map/ppermute | solution.py:440
  126.6 10.1 %collective-permute-start.6 = (bf16[256,384]{1,0:T(8,128)(2,1)}, bf16[256,384]{1,0:T(8,128)(2,1)S(1)}, u32[]{:S(2)}, u32[]{:S(2)}) collective-permute-start(bf16[256,384]{1,0:T(8,128)(2,1)} %get-tuple-element.70.refs_0_), channel_id=1, source_target_pairs={{0,4},{4,8},{8,12},{1,5},{5,9},{9,13},{2,6},{6,10},{10,14},{3,7},{... | collective-permute-start | bytes 589832 | tf_op jit(solution)/shard_map/ppermute | solution.py:445
  131.6 47.9 %collective-permute-start.25 = (bf16[4,192,576]{2,1,0:T(8,128)(2,1)S(1)}, bf16[4,192,576]{2,1,0:T(8,128)(2,1)S(1)}, u32[]{:S(2)}, u32[]{:S(2)}) collective-permute-start(bf16[4,192,576]{2,1,0:T(8,128)(2,1)S(1)} %bitcast.258), channel_id=1, source_target_pairs={{0,16},{16,0},{1,17},{17,1},{2,18},{18,2},{3,19},{19,3},{4,20},{20... | collective-permute-start | bytes 2654216 | tf_op jit(solution)/shard_map/ppermute | solution.py:440
  132.3 14.5 %collective-permute-start.7 = (bf16[256,384]{1,0:T(8,128)(2,1)S(1)}, bf16[256,384]{1,0:T(8,128)(2,1)S(1)}, u32[]{:S(2)}, u32[]{:S(2)}) collective-permute-start(bf16[256,384]{1,0:T(8,128)(2,1)S(1)} %copy-done.41), channel_id=1, source_target_pairs={{0,8},{4,12},{1,9},{5,13},{2,10},{6,14},{3,11},{7,15},{16,24},{20,... | collective-permute-start | bytes 589832 | tf_op jit(solution)/shard_map/ppermute | solution.py:445
  136.8 10.0 %collective-permute-start.8 = (bf16[256,384]{1,0:T(8,128)(2,1)S(1)}, bf16[256,384]{1,0:T(8,128)(2,1)S(1)}, u32[]{:S(2)}, u32[]{:S(2)}) collective-permute-start(bf16[256,384]{1,0:T(8,128)(2,1)S(1)} %copy-done.41), channel_id=1, source_target_pairs={{0,12},{1,13},{2,14},{3,15},{16,28},{17,29},{18,30},{19,31}} | collective-permute-start | bytes 589832 | tf_op jit(solution)/shard_map/ppermute | solution.py:445
  168.5 13.1 %collective-permute-start.17 = (bf16[256,384]{1,0:T(8,128)(2,1)}, bf16[256,384]{1,0:T(8,128)(2,1)S(1)}, u32[]{:S(2)}, u32[]{:S(2)}) collective-permute-start(bf16[256,384]{1,0:T(8,128)(2,1)} %get-tuple-element.74.refs_0_), channel_id=1, source_target_pairs={{0,4},{4,8},{8,12},{1,5},{5,9},{9,13},{2,6},{6,10},{10,14},{3,7},{... | collective-permute-start | bytes 589832 | tf_op jit(solution)/shard_map/ppermute | solution.py:445
  172.5 10.9 %collective-permute-start.18 = (bf16[256,384]{1,0:T(8,128)(2,1)}, bf16[256,384]{1,0:T(8,128)(2,1)S(1)}, u32[]{:S(2)}, u32[]{:S(2)}) collective-permute-start(bf16[256,384]{1,0:T(8,128)(2,1)} %get-tuple-element.74.refs_0_), channel_id=1, source_target_pairs={{0,8},{4,12},{1,9},{5,13},{2,10},{6,14},{3,11},{7,15},{16,24},{20,... | collective-permute-start | bytes 589832 | tf_op jit(solution)/shard_map/ppermute | solution.py:445
  222.2 11.9 %collective-permute-start.27 = (bf16[256,384]{1,0:T(8,128)(2,1)}, bf16[256,384]{1,0:T(8,128)(2,1)S(1)}, u32[]{:S(2)}, u32[]{:S(2)}) collective-permute-start(bf16[256,384]{1,0:T(8,128)(2,1)} %get-tuple-element.86), channel_id=1, source_target_pairs={{4,0},{8,4},{12,8},{5,1},{9,5},{13,9},{6,2},{10,6},{14,10},{7,3},{... | collective-permute-start | bytes 589832 | tf_op jit(solution)/shard_map/ppermute | solution.py:445
  223.4 21.8 %collective-permute-start.28 = (bf16[256,384]{1,0:T(8,128)(2,1)}, bf16[256,384]{1,0:T(8,128)(2,1)S(1)}, u32[]{:S(2)}, u32[]{:S(2)}) collective-permute-start(bf16[256,384]{1,0:T(8,128)(2,1)} %get-tuple-element.87), channel_id=1, source_target_pairs={{8,0},{12,4},{9,1},{13,5},{10,2},{14,6},{11,3},{15,7},{24,16},{28,... | collective-permute-start | bytes 589832 | tf_op jit(solution)/shard_map/ppermute | solution.py:445
  224.7 20.5 %collective-permute-start.29 = (bf16[256,384]{1,0:T(8,128)(2,1)}, bf16[256,384]{1,0:T(8,128)(2,1)S(1)}, u32[]{:S(2)}, u32[]{:S(2)}) collective-permute-start(bf16[256,384]{1,0:T(8,128)(2,1)} %get-tuple-element.88), channel_id=1, source_target_pairs={{12,0},{13,1},{14,2},{15,3},{28,16},{29,17},{30,18},{31,19}} | collective-permute-start | bytes 589832 | tf_op jit(solution)/shard_map/ppermute | solution.py:445
  234.1 73.4 %collective-permute-start.51 = (bf16[4,192,576]{2,1,0:T(8,128)(2,1)}, bf16[4,192,576]{2,1,0:T(8,128)(2,1)S(1)}, u32[]{:S(2)}, u32[]{:S(2)}) collective-permute-start(bf16[4,192,576]{2,1,0:T(8,128)(2,1)} %dynamic-slice_bitcast_fusion), channel_id=1, source_target_pairs={{0,16},{16,0},{1,17},{17,1},{2,18},{18,2},{3,19},{19,3},{4,20},{20... | collective-permute-start | bytes 2654216 | tf_op jit(solution)/shard_map/ppermute | solution.py:440
  268.7 39.6 %collective-permute-start.48 = (bf16[4,192,576]{2,1,0:T(8,128)(2,1)}, bf16[4,192,576]{2,1,0:T(8,128)(2,1)}, u32[]{:S(2)}, u32[]{:S(2)}) collective-permute-start(bf16[4,192,576]{2,1,0:T(8,128)(2,1)} %dynamic-slice_bitcast_fusion.1), channel_id=1, source_target_pairs={{0,16},{16,0},{1,17},{17,1},{2,18},{18,2},{3,19},{19,3},{4,20},{20... | collective-permute-start | bytes 2654216 | tf_op jit(solution)/shard_map/ppermute | solution.py:440
  279.8 11.3 %collective-permute-start.30 = (bf16[256,384]{1,0:T(8,128)(2,1)}, bf16[256,384]{1,0:T(8,128)(2,1)S(1)}, u32[]{:S(2)}, u32[]{:S(2)}) collective-permute-start(bf16[256,384]{1,0:T(8,128)(2,1)} %get-tuple-element.105), channel_id=1, source_target_pairs={{4,0},{8,4},{12,8},{5,1},{9,5},{13,9},{6,2},{10,6},{14,10},{7,3},{... | collective-permute-start | bytes 589832 | tf_op jit(solution)/shard_map/ppermute | solution.py:445
  281.1 18.8 %collective-permute-start.31 = (bf16[256,384]{1,0:T(8,128)(2,1)}, bf16[256,384]{1,0:T(8,128)(2,1)S(1)}, u32[]{:S(2)}, u32[]{:S(2)}) collective-permute-start(bf16[256,384]{1,0:T(8,128)(2,1)} %get-tuple-element.106), channel_id=1, source_target_pairs={{8,0},{12,4},{9,1},{13,5},{10,2},{14,6},{11,3},{15,7},{24,16},{28,... | collective-permute-start | bytes 589832 | tf_op jit(solution)/shard_map/ppermute | solution.py:445
  282.4 17.5 %collective-permute-start.32 = (bf16[256,384]{1,0:T(8,128)(2,1)}, bf16[256,384]{1,0:T(8,128)(2,1)S(1)}, u32[]{:S(2)}, u32[]{:S(2)}) collective-permute-start(bf16[256,384]{1,0:T(8,128)(2,1)} %get-tuple-element.107), channel_id=1, source_target_pairs={{12,0},{13,1},{14,2},{15,3},{28,16},{29,17},{30,18},{31,19}} | collective-permute-start | bytes 589832 | tf_op jit(solution)/shard_map/ppermute | solution.py:445
  291.1 19.4 %collective-permute-start.37 = (bf16[576,896]{1,0:T(8,128)(2,1)}, bf16[576,896]{1,0:T(8,128)(2,1)S(1)}, u32[]{:S(2)}, u32[]{:S(2)}) collective-permute-start(bf16[576,896]{1,0:T(8,128)(2,1)} %get-tuple-element.120), channel_id=1, source_target_pairs={{0,16},{16,0},{1,17},{17,1},{2,18},{18,2},{3,19},{19,3},{4,20},{20... | collective-permute-start | bytes 3096584 | tf_op jit(solution)/shard_map/ppermute | solution.py:440
  299.9 56.8 %collective-permute-start.44 = (bf16[576,1536]{1,0:T(8,128)(2,1)}, bf16[576,1536]{1,0:T(8,128)(2,1)S(1)}, u32[]{:S(2)}, u32[]{:S(2)}) collective-permute-start(bf16[576,1536]{1,0:T(8,128)(2,1)} %get-tuple-element.124), channel_id=1, source_target_pairs={{0,16},{16,0},{1,17},{17,1},{2,18},{18,2},{3,19},{19,3},{4,20},{20... | collective-permute-start | bytes 5308424 | tf_op jit(solution)/shard_map/ppermute | solution.py:440
  299.9 58.8 %collective-permute-start.41 = (bf16[576,1536]{1,0:T(8,128)(2,1)}, bf16[576,1536]{1,0:T(8,128)(2,1)S(1)}, u32[]{:S(2)}, u32[]{:S(2)}) collective-permute-start(bf16[576,1536]{1,0:T(8,128)(2,1)} %get-tuple-element.122), channel_id=1, source_target_pairs={{0,16},{16,0},{1,17},{17,1},{2,18},{18,2},{3,19},{19,3},{4,20},{20... | collective-permute-start | bytes 5308424 | tf_op jit(solution)/shard_map/ppermute | solution.py:440
  307.5 15.7 %collective-permute-start.34 = (bf16[576,896]{1,0:T(8,128)(2,1)}, bf16[576,896]{1,0:T(8,128)(2,1)S(1)}, u32[]{:S(2)}, u32[]{:S(2)}) collective-permute-start(bf16[576,896]{1,0:T(8,128)(2,1)} %get-tuple-element.118), channel_id=1, source_target_pairs={{0,16},{16,0},{1,17},{17,1},{2,18},{18,2},{3,19},{19,3},{4,20},{20... | collective-permute-start | bytes 3096584 | tf_op jit(solution)/shard_map/ppermute | solution.py:440
  308.3 14.1 %collective-permute-start.52 = (bf16[2,192,576]{2,1,0:T(8,128)(2,1)S(1)}, bf16[2,192,576]{2,1,0:T(8,128)(2,1)S(1)}, u32[]{:S(2)}, u32[]{:S(2)}) collective-permute-start(bf16[2,192,576]{2,1,0:T(8,128)(2,1)S(1)} %dynamic-slice_bitcast_fusion.6), channel_id=1, source_target_pairs={{0,2},{1,3},{2,0},{3,1},{4,6},{5,7},{6,4},{7,5},{8,10},{9,11},{10,... | collective-permute-start | bytes 1327112 | tf_op jit(solution)/shard_map/ppermute | solution.py:440
  310.5 21.6 %collective-permute-start.49 = (bf16[2,192,576]{2,1,0:T(8,128)(2,1)S(1)}, bf16[2,192,576]{2,1,0:T(8,128)(2,1)S(1)}, u32[]{:S(2)}, u32[]{:S(2)}) collective-permute-start(bf16[2,192,576]{2,1,0:T(8,128)(2,1)S(1)} %dynamic-slice_bitcast_fusion.7), channel_id=1, source_target_pairs={{0,2},{1,3},{2,0},{3,1},{4,6},{5,7},{6,4},{7,5},{8,10},{9,11},{10,... | collective-permute-start | bytes 1327112 | tf_op jit(solution)/shard_map/ppermute | solution.py:440
  322.5 21.2 %collective-permute-start.38 = (bf16[2,144,896]{2,1,0:T(8,128)(2,1)S(1)}, bf16[2,144,896]{2,1,0:T(8,128)(2,1)S(1)}, u32[]{:S(2)}, u32[]{:S(2)}) collective-permute-start(bf16[2,144,896]{2,1,0:T(8,128)(2,1)S(1)} %dynamic-slice_bitcast_fusion.4), channel_id=1, source_target_pairs={{0,1},{1,0},{2,3},{3,2},{4,5},{5,4},{6,7},{7,6},{8,9},{9,8},{10,11... | collective-permute-start | bytes 1548296 | tf_op jit(solution)/shard_map/ppermute | solution.py:440
  323.2 19.2 %collective-permute-start.53 = (bf16[192,576]{1,0:T(8,128)(2,1)S(1)}, bf16[192,576]{1,0:T(8,128)(2,1)S(1)}, u32[]{:S(2)}, u32[]{:S(2)}) collective-permute-start(bf16[192,576]{1,0:T(8,128)(2,1)S(1)} %dynamic-slice_bitcast_fusion.12), channel_id=1, source_target_pairs={{0,1},{1,0},{2,3},{3,2},{4,5},{5,4},{6,7},{7,6},{8,9},{9,8},{10,11... | collective-permute-start | bytes 663560 | tf_op jit(solution)/shard_map/ppermute | solution.py:440
  332.1 25.8 %collective-permute-start.35 = (bf16[2,144,896]{2,1,0:T(8,128)(2,1)S(1)}, bf16[2,144,896]{2,1,0:T(8,128)(2,1)S(1)}, u32[]{:S(2)}, u32[]{:S(2)}) collective-permute-start(bf16[2,144,896]{2,1,0:T(8,128)(2,1)S(1)} %dynamic-slice_bitcast_fusion.5), channel_id=1, source_target_pairs={{0,1},{1,0},{2,3},{3,2},{4,5},{5,4},{6,7},{7,6},{8,9},{9,8},{10,11... | collective-permute-start | bytes 1548296 | tf_op jit(solution)/shard_map/ppermute | solution.py:440
  342.4 13.6 %collective-permute-start.50 = (bf16[192,576]{1,0:T(8,128)(2,1)S(1)}, bf16[192,576]{1,0:T(8,128)(2,1)S(1)}, u32[]{:S(2)}, u32[]{:S(2)}) collective-permute-start(bf16[192,576]{1,0:T(8,128)(2,1)S(1)} %dynamic-slice_bitcast_fusion.13), channel_id=1, source_target_pairs={{0,1},{1,0},{2,3},{3,2},{4,5},{5,4},{6,7},{7,6},{8,9},{9,8},{10,11... | collective-permute-start | bytes 663560 | tf_op jit(solution)/shard_map/ppermute | solution.py:440
  343.9 16.9 %collective-permute-start.39 = (bf16[144,896]{1,0:T(8,128)(2,1)S(1)}, bf16[144,896]{1,0:T(8,128)(2,1)S(1)}, u32[]{:S(2)}, u32[]{:S(2)}) collective-permute-start(bf16[144,896]{1,0:T(8,128)(2,1)S(1)} %dynamic-slice_bitcast_fusion.10), channel_id=1, source_target_pairs={{0,2},{1,3},{2,0},{3,1},{4,6},{5,7},{6,4},{7,5},{8,10},{9,11},{10,... | collective-permute-start | bytes 774152 | tf_op jit(solution)/shard_map/ppermute | solution.py:440
  357.3 22.6 %collective-permute-start.45 = (bf16[2,144,1536]{2,1,0:T(8,128)(2,1)S(1)}, bf16[2,144,1536]{2,1,0:T(8,128)(2,1)S(1)}, u32[]{:S(2)}, u32[]{:S(2)}) collective-permute-start(bf16[2,144,1536]{2,1,0:T(8,128)(2,1)S(1)} %dynamic-slice_bitcast_fusion.2), channel_id=1, source_target_pairs={{0,1},{1,0},{2,3},{3,2},{4,5},{5,4},{6,7},{7,6},{8,9},{9,8},{10,11... | collective-permute-start | bytes 2654216 | tf_op jit(solution)/shard_map/ppermute | solution.py:440
  359.3 36.0 %collective-permute-start.42 = (bf16[2,144,1536]{2,1,0:T(8,128)(2,1)S(1)}, bf16[2,144,1536]{2,1,0:T(8,128)(2,1)S(1)}, u32[]{:S(2)}, u32[]{:S(2)}) collective-permute-start(bf16[2,144,1536]{2,1,0:T(8,128)(2,1)S(1)} %dynamic-slice_bitcast_fusion.3), channel_id=1, source_target_pairs={{0,1},{1,0},{2,3},{3,2},{4,5},{5,4},{6,7},{7,6},{8,9},{9,8},{10,11... | collective-permute-start | bytes 2654216 | tf_op jit(solution)/shard_map/ppermute | solution.py:440
  380.3 15.8 %collective-permute-start.46 = (bf16[144,1536]{1,0:T(8,128)(2,1)S(1)}, bf16[144,1536]{1,0:T(8,128)(2,1)S(1)}, u32[]{:S(2)}, u32[]{:S(2)}) collective-permute-start(bf16[144,1536]{1,0:T(8,128)(2,1)S(1)} %dynamic-slice_bitcast_fusion.8), channel_id=1, source_target_pairs={{0,2},{1,3},{2,0},{3,1},{4,6},{5,7},{6,4},{7,5},{8,10},{9,11},{10,... | collective-permute-start | bytes 1327112 | tf_op jit(solution)/shard_map/ppermute | solution.py:440
  (56 other events, 303.0 us)
Sparse Core Ops, SparseCore 0:
  405.2 77.8 all-reduce.2

commit v2 on v1

--- a/solution.py
+++ b/solution.py
@@ -42,7 +42,15 @@
     return jax.ShapeDtypeStruct(dims, kind)
 
 
-def call(kernel, outs, in_specs, scratch, args, flops):
+def call(kernel, outs, in_specs, scratch, args, flops, after=()):
+    count = len(args)
+    late = len(after)
+    inner = kernel
+
+    def kernel(*refs):
+        inner(*refs[:count], *refs[count + late :])
+
+    in_specs = list(in_specs) + [ANYWHERE] * late
     moved = sum(a.size * a.dtype.itemsize for a in args)
     moved += sum(o.size * o.dtype.itemsize for o in outs)
     return pl.pallas_call(
@@ -52,8 +60,8 @@
         out_specs=tuple(IN_VMEM for _ in outs),
         scratch_shapes=scratch,
         compiler_params=pltpu.CompilerParams(vmem_limit_bytes=VMEM_LIMIT),
-        cost_estimate=pl.CostEstimate(flops=flops, bytes_accessed=moved, transcendentals=0),
-    )(*args)
+        cost_estimate=pl.CostEstimate(flops=flops // 1000, bytes_accessed=moved // 1000, transcendentals=0),
+    )(*args, *after)
 
 
 def fetch(flag, yes_ref, no_ref, target, sem):
@@ -68,6 +76,22 @@
 
 def arrive(ref, target, sem):
     pltpu.make_async_copy(ref, target, sem).wait()
+
+
+def fetch_down(parts, core, mine, theirs, target, sem):
+    if parts == 0:
+        pltpu.make_async_copy(mine, target, sem).start()
+        return
+    half = mine.shape[0] // parts
+    for i in range(parts):
+        rows = pl.ds(i * half, half)
+        for source, place in ((mine, core), (theirs, 1 - core)):
+            start = pl.multiple_of((2 * i + place) * half, half)
+            pltpu.make_async_copy(source.at[rows], target.at[pl.ds(start, half)], sem).start()
+
+
+def arrive_down(target, sem):
+    pltpu.make_async_copy(target, target, sem).wait()
 
 
 def norm_scale(z):
@@ -128,7 +152,7 @@
     kv_out[...] = jnp.concatenate([qk[:, HQ * HD :].astype(BF), value.astype(BF)], axis=1)
 
 
-def attn_in(layer, idx, x, weights, cos, sin):
+def attn_in(layer, idx, x, weights, cos, sin, after=()):
     rows, depth = x.shape
     a_own, a_got, v_own, v_got = weights
     args = (idx, x, a_own, a_got, v_own, v_got, cos, sin)
@@ -139,6 +163,7 @@
         [pltpu.VMEM(a_own.shape, BF), pltpu.VMEM(v_own.shape, BF), pltpu.SemaphoreType.DMA((2,))],
         args,
         2 * rows * depth * 1536,
+        after,
     )
 
 
@@ -186,7 +211,7 @@
     attn_out[...] = jnp.concatenate(pieces, axis=1)
 
 
-def attend(idx, q, kv):
+def attend(idx, q, kv, after=()):
     rows = q.shape[0]
     return call(
         functools.partial(attend_kernel, len(kv)),
@@ -195,13 +220,15 @@
         [],
         (idx, q) + tuple(kv),
         2 * 2 * rows * rows * len(kv) * HQ * HD * 4,
-    )
-
-
-def mlp_kernel(layer, idx, x, attn, v_own, v_got, g_m, g_t, d, y_out, resid_out, mn_out, gate_out, up_out, hid_out, v_w, sems):
+        after,
+    )
+
+
+def mlp_kernel(layer, parts, idx, x, attn, v_own, v_got, g_m, g_t, d_m, d_t, y_out, resid_out, mn_out, gate_out, up_out, hid_out, v_w, d_w, sems):
     own = idx[0] == layer
     first = idx[0] == 0
     fetch(own, v_own, v_got, v_w, sems.at[0])
+    fetch_down(parts, idx[0], d_m, d_t, d_w, sems.at[1])
     arrive(v_own, v_w, sems.at[0])
     width = HQ * HD
     depth = x.shape[1]
@@ -218,16 +245,17 @@
     up_out[...] = up
     hid = (gate * jax.nn.sigmoid(gate) * up).astype(BF)
     hid_out[...] = hid
-    y_out[...] = (resid + nn(hid, d[...])).astype(BF)
-
-
-def mlp(layer, idx, x, attn, weights, g_m, g_t, d):
+    arrive_down(d_w, sems.at[1])
+    y_out[...] = (resid + nn(hid, d_w[:, :depth])).astype(BF)
+
+
+def mlp(layer, parts, idx, x, attn, weights, g_m, g_t, d_m, d_t, after=()):
     rows, depth = x.shape
     _, _, v_own, v_got = weights
     ff = g_m.shape[1]
-    args = (idx, x, attn, v_own, v_got, g_m, g_t, d)
+    args = (idx, x, attn, v_own, v_got, g_m, g_t, d_m, d_t)
     return call(
-        functools.partial(mlp_kernel, layer),
+        functools.partial(mlp_kernel, layer, parts),
         (
             shape((rows, depth), BF),
             shape((rows, depth), F32),
@@ -236,19 +264,26 @@
             shape((rows, ff), F32),
             shape((rows, ff), BF),
         ),
-        [IN_SMEM, IN_VMEM, IN_VMEM] + [ANYWHERE] * 2 + [IN_VMEM] * 3,
-        [pltpu.VMEM(v_own.shape, BF), pltpu.SemaphoreType.DMA((1,))],
+        [IN_SMEM, IN_VMEM, IN_VMEM] + [ANYWHERE] * 2 + [IN_VMEM] * 2 + [ANYWHERE] * 2,
+        [
+            pltpu.VMEM(v_own.shape, BF),
+            pltpu.VMEM((ff, d_m.shape[1]), BF),
+            pltpu.SemaphoreType.DMA((2,)),
+        ],
         args,
         2 * rows * depth * (3 * ff + depth),
-    )
-
-
-def mlp_back_kernel(layer, idx, e, resid, gate, up, g_m, g_t, d, v_own, v_got, gm_out, gt_out, rg_out, mix_out, ag_out, mg_out, v_w, sems):
+        after,
+    )
+
+
+def mlp_back_kernel(layer, parts, idx, e, resid, gate, up, g_m, g_t, d_m, d_t, v_own, v_got, gm_out, gt_out, rg_out, mix_out, ag_out, mg_out, v_w, d_w, sems):
     own = idx[0] == layer
     first = idx[0] == 0
+    fetch_down(parts, idx[0], d_m, d_t, d_w, sems.at[1])
     fetch(own, v_own, v_got, v_w, sems.at[0])
     low = e[...]
-    hg = nt(low, d[...])
+    arrive_down(d_w, sems.at[1])
+    hg = nt(low, d_w[:, : e.shape[1]])
     gv = gate[...]
     sig = jax.nn.sigmoid(gv)
     g_in = (hg * up[...] * sig * (1.0 + gv * (1.0 - sig))).astype(BF)
@@ -274,13 +309,13 @@
     ag_out[...] = nt(mix, v_w[:, :depth]).astype(BF)
 
 
-def mlp_back(layer, idx, e, resid, gate, up, g_m, g_t, d, weights):
+def mlp_back(layer, parts, idx, e, resid, gate, up, g_m, g_t, d_m, d_t, weights, after=()):
     rows, depth = e.shape
     _, _, v_own, v_got = weights
     ff = g_m.shape[1]
-    args = (idx, e, resid, gate, up, g_m, g_t, d, v_own, v_got)
+    args = (idx, e, resid, gate, up, g_m, g_t, d_m, d_t, v_own, v_got)
     return call(
-        functools.partial(mlp_back_kernel, layer),
+        functools.partial(mlp_back_kernel, layer, parts),
         (
             shape((rows, ff), BF),
             shape((rows, ff), BF),
@@ -289,40 +324,168 @@
             shape((rows, HQ * HD), BF),
             shape((depth, LANES), BF),
         ),
-        [IN_SMEM] + [IN_VMEM] * 7 + [ANYWHERE] * 2,
-        [pltpu.VMEM(v_own.shape, BF), pltpu.SemaphoreType.DMA((1,))],
+        [IN_SMEM] + [IN_VMEM] * 6 + [ANYWHERE] * 4,
+        [
+            pltpu.VMEM(v_own.shape, BF),
+            pltpu.VMEM((ff, d_m.shape[1]), BF),
+            pltpu.SemaphoreType.DMA((2,)),
+        ],
         args,
         2 * rows * depth * (3 * ff + depth),
-    )
-
-
-def mlp_grads_kernel(hid, e, mn, gm, gt, attn, mix, mg, ggm_out, ggt_out, dg_out, og_out):
+        after,
+    )
+
+
+def padded_rows(count, step=16):
+    return count + -count % step
+
+
+class Packing:
+    def __init__(self, shard, half, ff, depth):
+        self.shard = shard
+        self.half = half
+        self.shard_step = padded_rows(shard)
+        self.half_step = padded_rows(half)
+        self.gate_tiles = ff // LANES
+        self.down_tiles = padded_rows(depth, LANES) // LANES
+        self.out_tiles = (self.down_tiles + 1) // 2
+        self.down_at = self.gate_tiles * self.shard_step
+        self.out_at = self.down_at + self.down_tiles * self.half_step
+        used = self.out_at + self.out_tiles * self.shard_step
+        self.used = used
+        self.rows = self.down_at + padded_rows(used - self.down_at, 64)
+        self.entry_tiles = (HQ + 2 * HK + 1) * HD // LANES // 2
+        self.entry_rows = self.entry_tiles * self.shard_step
+
+
+def tile(value, at):
+    return value[:, at * LANES : (at + 1) * LANES]
+
+
+def mlp_grads_kernel(pack, idx, hid, e, mn, gm, gt, attn, mix, mg, m_out, t_out):
+    parts = m_out.shape[0]
+    first = idx[0] == 0
+    depth = mn.shape[1]
+    shard, half = pack.shard, pack.half
     mnv = mn[...]
-    ggm_out[...] = tn(mnv, gm[...]).astype(BF)
-    ggt_out[...] = tn(mnv, gt[...]).astype(BF)
-    dg_out[...] = tn(hid[...], e[...]).astype(BF)
-    depth = mn.shape[1]
-    width = (HQ + HK) * HD
-    og_out[...] = jnp.zeros_like(og_out)
-    og_out[:, :depth] = tn(attn[...], mix[...]).astype(BF)
-    og_out[:, width:] = mg[...]
-
-
-def mlp_grads(hid, e, mn, gm, gt, attn, mix, mg):
+    fill = pack.down_tiles * LANES - depth
+    down = tn(hid[...], e[...]).astype(BF)
+    down = jnp.concatenate([down, jnp.zeros((down.shape[0], fill), BF)], axis=1)
+    outward = tn(attn[...], mix[...]).astype(BF)
+    outward = jnp.concatenate([outward, mg[:, :fill]], axis=1)
+    blank = jnp.zeros((shard, LANES), BF)
+    for out, side, low in ((m_out, gm, first), (t_out, gt, jnp.logical_not(first))):
+        gate = tn(mnv, side[...]).astype(BF)
+        for f in range(parts):
+            rows = slice(f * shard, (f + 1) * shard)
+            for k in range(pack.gate_tiles):
+                at = k * pack.shard_step
+                out[f, at : at + shard, :] = tile(gate[rows], k)
+            low_half = down[2 * f * half : (2 * f + 1) * half]
+            high_half = down[(2 * f + 1) * half : (2 * f + 2) * half]
+            own_half = jnp.where(low, low_half, high_half)
+            for k in range(pack.down_tiles):
+                at = pack.down_at + k * pack.half_step
+                out[f, at : at + half, :] = tile(own_half, k)
+            for k in range(pack.out_tiles):
+                at = pack.out_at + k * pack.shard_step
+                other = k + pack.out_tiles
+                high = tile(outward[rows], other) if other < pack.down_tiles else blank
+                out[f, at : at + shard, :] = jnp.where(low, tile(outward[rows], k), high)
+            if pack.used < pack.rows:
+                out[f, pack.used :, :] = jnp.zeros((pack.rows - pack.used, LANES), BF)
+
+
+def mlp_grads(pack, parts, idx, hid, e, mn, gm, gt, attn, mix, mg, after=()):
     rows, depth = e.shape
     ff = gm.shape[1]
     return call(
-        mlp_grads_kernel,
+        functools.partial(mlp_grads_kernel, pack),
+        (shape((parts, pack.rows, LANES), BF), shape((parts, pack.rows, LANES), BF)),
+        [IN_SMEM] + [IN_VMEM] * 8,
+        [],
+        (idx, hid, e, mn, gm, gt, attn, mix, mg),
+        2 * rows * depth * (3 * ff + depth),
+        after,
+    )
+
+
+def halves(idx, zero, one, got):
+    first = idx[0] == 0
+    keep = jnp.where(first, zero[...], one[...])
+    other = got[...]
+    return jnp.where(first, keep, other), jnp.where(first, other, keep)
+
+
+def unpack_mlp_kernel(pack, idx, zero, one, got, gate_out, up_out, down_out, o_out, gain_out):
+    shard, half = pack.shard, pack.half
+    both = halves(idx, zero, one, got)
+    for value, out in zip(both, (gate_out, up_out)):
+        for k in range(pack.gate_tiles):
+            at = k * pack.shard_step
+            out[:, k * LANES : (k + 1) * LANES] = value[at : at + shard].astype(F32)
+    depth = down_out.shape[1]
+    for side, value in enumerate(both):
+        tiles = []
+        for k in range(pack.down_tiles):
+            at = pack.down_at + k * pack.half_step
+            tiles.append(value[at : at + half])
+        wide_rows = jnp.concatenate(tiles, axis=1)[:, :depth]
+        down_out[side * half : (side + 1) * half, :] = wide_rows.astype(F32)
+    tiles = []
+    for k in range(pack.down_tiles):
+        at = pack.out_at + (k % pack.out_tiles) * pack.shard_step
+        tiles.append(both[k // pack.out_tiles][at : at + shard])
+    o_out[...] = jnp.concatenate(tiles, axis=1)[:, :depth].astype(F32)
+    gain_out[...] = tiles[-1].astype(F32)
+
+
+def unpack_mlp(pack, idx, zero, one, got, ff, depth):
+    return call(
+        functools.partial(unpack_mlp_kernel, pack),
         (
-            shape((depth, ff), BF),
-            shape((depth, ff), BF),
-            shape((ff, depth), BF),
-            shape((depth, (HQ + HK) * HD + LANES), BF),
+            shape((pack.shard, ff), F32),
+            shape((pack.shard, ff), F32),
+            shape((2 * pack.half, depth), F32),
+            shape((pack.shard, depth), F32),
+            shape((pack.shard, LANES), F32),
         ),
-        [IN_VMEM] * 8,
+        [IN_SMEM] + [IN_VMEM] * 3,
         [],
-        (hid, e, mn, gm, gt, attn, mix, mg),
-        2 * rows * depth * (3 * ff + depth),
+        (idx, zero, one, got),
+        1000,
+    )
+
+
+def unpack_entry_kernel(pack, idx, zero, one, got, q_out, k_out, v_out, gain_out):
+    shard = pack.shard
+    tiles = []
+    for value in halves(idx, zero, one, got):
+        for k in range(pack.entry_tiles):
+            at = k * pack.shard_step
+            tiles.append(value[at : at + shard])
+    full = jnp.concatenate(tiles, axis=1).astype(F32)
+    qw, kw = HQ * HD, HK * HD
+    q_out[...] = full[:, :qw]
+    k_out[...] = full[:, qw : qw + kw]
+    v_out[...] = full[:, qw + kw : qw + 2 * kw]
+    gain_out[...] = tiles[-1].astype(F32)
+
+
+def unpack_entry(pack, idx, zero, one, got):
+    qw, kw = HQ * HD, HK * HD
+    return call(
+        functools.partial(unpack_entry_kernel, pack),
+        (
+            shape((pack.shard, qw), F32),
+            shape((pack.shard, kw), F32),
+            shape((pack.shard, kw), F32),
+            shape((pack.shard, LANES), F32),
+        ),
+        [IN_SMEM] + [IN_VMEM] * 3,
+        [],
+        (idx, zero, one, got),
+        1000,
     )
 
 
@@ -369,7 +532,7 @@
         out[...] = joined[(d + 1) * rows : (d + 2) * rows].astype(BF)
 
 
-def attend_back(idx, q, ag, lse, kv):
+def attend_back(idx, q, ag, lse, kv, after=()):
     rows = q.shape[0]
     outs = [shape((rows, HQ * HD), F32), shape((rows, 2 * HK * HD), F32)]
     outs += [shape((rows, 2 * HK * HD), BF) for _ in kv[1:]]
@@ -380,12 +543,13 @@
         [],
         (idx, q, ag, lse) + tuple(kv),
         5 * 2 * rows * rows * len(kv) * HQ * HD * 4,
-    )
-
-
-def input_back_kernel(layer, far, idx, x, normed, dq, own_kv, *refs):
+        after,
+    )
+
+
+def input_back_kernel(layer, pack, far, idx, x, normed, dq, own_kv, *refs):
     far_kv = refs[:far]
-    rg, a_own, a_got, v_own, v_got, cos, sin, og, ig_out, m_out, t_out, a_w, v_w, sems = refs[far:]
+    rg, a_own, a_got, v_own, v_got, cos, sin, ig_out, m_out, t_out, a_w, v_w, sems = refs[far:]
     own = idx[0] == layer
     first = idx[0] == 0
     fetch(own, a_own, a_got, a_w, sems.at[0])
@@ -410,28 +574,39 @@
     part = inv * weighted - z * (inv * inv * inv) * jnp.mean(z * weighted, axis=-1, keepdims=True)
     ig_out[...] = (rg[...] + part).astype(BF)
     nv = normed[...]
-    qk_grad = jnp.concatenate([tn(nv, qk_in).astype(BF), gain_tile(ng * z * inv)], axis=1)
-    lanes = lax.broadcasted_iota(jnp.int32, (depth, width), 1)
-    v_grad = tn(nv, padded).astype(BF)
-    ogv = og[...]
-    merged = jnp.where(lanes < HQ * HD, ogv[:, :width], v_grad)
-    vo_grad = jnp.concatenate([merged, ogv[:, width:]], axis=1)
-    m_out[...] = jnp.where(first, qk_grad, vo_grad)
-    t_out[...] = jnp.where(first, vo_grad, qk_grad)
-
-
-def input_back(layer, idx, x, normed, dq, own_kv, far_kv, rg, weights, cos, sin, og):
+    grads = jnp.concatenate(
+        [
+            tn(nv, qk_in).astype(BF),
+            tn(nv, v_in).astype(BF),
+            gain_tile(ng * z * inv)[:, :HD],
+        ],
+        axis=1,
+    )
+    shard = pack.shard
+    for f in range(m_out.shape[0]):
+        piece = grads[f * shard : (f + 1) * shard]
+        for k in range(pack.entry_tiles):
+            at = k * pack.shard_step
+            low = tile(piece, k)
+            high = tile(piece, k + pack.entry_tiles)
+            m_out[f, at : at + shard, :] = jnp.where(first, low, high)
+            t_out[f, at : at + shard, :] = jnp.where(first, high, low)
+
+
+def input_back(layer, pack, parts, idx, x, normed, dq, own_kv, far_kv, rg, weights, cos, sin, after=()):
     rows, depth = x.shape
     a_own, a_got, v_own, v_got = weights
     args = (idx, x, normed, dq, own_kv) + tuple(far_kv)
-    args += (rg, a_own, a_got, v_own, v_got, cos, sin, og)
+    args += (rg, a_own, a_got, v_own, v_got, cos, sin)
+    packed = (parts, pack.entry_rows, LANES)
     return call(
-        functools.partial(input_back_kernel, layer, len(far_kv)),
-        (shape((rows, depth), BF), shape(a_own.shape, BF), shape(a_own.shape, BF)),
-        [IN_SMEM] + [IN_VMEM] * (5 + len(far_kv)) + [ANYWHERE] * 4 + [IN_VMEM] * 3,
+        functools.partial(input_back_kernel, layer, pack, len(far_kv)),
+        (shape((rows, depth), BF), shape(packed, BF), shape(packed, BF)),
+        [IN_SMEM] + [IN_VMEM] * (5 + len(far_kv)) + [ANYWHERE] * 4 + [IN_VMEM] * 2,
         [pltpu.VMEM(a_own.shape, BF), pltpu.VMEM(v_own.shape, BF), pltpu.SemaphoreType.DMA((2,))],
         args,
         2 * 2 * rows * depth * 1536,
+        after,
     )
 
 
@@ -453,36 +628,99 @@
     return [b for b in range(count.bit_length() - 1)]
 
 
-def gather_rows(piece, order):
+def held(value, *deps):
+    return lax.optimization_barrier((value,) + deps)[0]
+
+
+def gather_step(value, have, bit, wait):
     me = lax.axis_index("fsdp")
+    got = crossed(value, "fsdp", 1 << bit)
+    if wait:
+        got = held(got, *wait)
+    low = ((me >> bit) & 1) == 0
+    place = sum(1 for b in have if b > bit)
+    return jnp.stack([jnp.where(low, value, got), jnp.where(low, got, value)], axis=place)
+
+
+def gather_some(values, orders, first, last, wait=()):
+    for step in range(first, last):
+        late = wait if step == last - 1 else ()
+        values = [gather_step(v, o[:step], o[step], late) for v, o in zip(values, orders)]
+    return values
+
+
+def whole_rows(value):
+    return value.reshape((value.size // value.shape[-1],) + value.shape[-1:])
+
+
+def cut(value, left, bit):
+    mine = (lax.axis_index("fsdp") >> bit) & 1
+    place = sorted(left, reverse=True).index(bit)
+    send = lax.dynamic_index_in_dim(value, 1 - mine, place, keepdims=False)
+    keep = lax.dynamic_index_in_dim(value, mine, place, keepdims=False)
+    return send, keep
+
+
+def added(halves, bit, wait=()):
+    send, keep = halves
+    got = crossed(send, "fsdp", 1 << bit)
+    if wait:
+        got = held(got, *wait)
+    return (keep.astype(F32) + got.astype(F32)).astype(BF)
+
+
+def first_cut(value, order):
     count = lax.axis_size("fsdp")
-    have = []
-    value = piece
-    for bit in order:
-        got = crossed(value, "fsdp", 1 << bit)
-        low = ((me >> bit) & 1) == 0
-        place = sum(1 for b in have if b > bit)
-        value = jnp.stack([jnp.where(low, value, got), jnp.where(low, got, value)], axis=place)
-        have.append(bit)
-    return value.reshape((count * piece.shape[0],) + piece.shape[1:])
-
-
-def scatter_rows(value, order):
-    me = lax.axis_index("fsdp")
-    count = lax.axis_size("fsdp")
-    bits = len(order)
-    rows = value.shape[0] // count
-    value = value.reshape((2,) * bits + (rows,) + value.shape[1:])
-    left = sorted(order, reverse=True)
-    for bit in order:
-        mine = (me >> bit) & 1
-        place = left.index(bit)
-        send = lax.dynamic_index_in_dim(value, 1 - mine, place, keepdims=False)
-        keep = lax.dynamic_index_in_dim(value, mine, place, keepdims=False)
-        got = crossed(send, "fsdp", 1 << bit)
-        value = (keep.astype(F32) + got.astype(F32)).astype(BF)
-        left.remove(bit)
+    value = value.reshape((2,) * len(order) + (value.shape[0] // count,) + value.shape[1:])
+    return cut(value, order, order[0])
+
+
+def scatter_rest(value, order, wait=()):
+    for step in range(1, len(order)):
+        late = wait if step == len(order) - 1 else ()
+        value = added(cut(value, order[step:], order[step]), order[step], late)
     return value
+
+
+def sum_over_ctx(value):
+    count = lax.axis_size("ctx")
+    if count & (count - 1):
+        return lax.psum(value, "ctx")
+    for bit in bits_of(count):
+        value = (value.astype(F32) + crossed(value, "ctx", 1 << bit).astype(F32)).astype(BF)
+    return value
+
+
+def ctx_begin(value, wait=()):
+    me = lax.axis_index("ctx") & 1
+    size = value.shape[0] // 2
+    send = lax.dynamic_slice_in_dim(value, (1 - me) * size, size, 0)
+    keep = lax.dynamic_slice_in_dim(value, me * size, size, 0)
+    got = crossed(send, "ctx", 1)
+    if wait:
+        got = held(got, *wait)
+    return (keep.astype(F32) + got.astype(F32)).astype(BF)
+
+
+def ctx_middle(value, wait=()):
+    for bit in bits_of(lax.axis_size("ctx"))[1:]:
+        value = added_over_ctx(value, bit, wait)
+    return value
+
+
+def ctx_end(value, wait=()):
+    low = (lax.axis_index("ctx") & 1) == 0
+    got = crossed(value, "ctx", 1)
+    if wait:
+        got = held(got, *wait)
+    return jnp.concatenate([jnp.where(low, value, got), jnp.where(low, got, value)], axis=0)
+
+
+def added_over_ctx(value, bit, wait):
+    got = crossed(value, "ctx", 1 << bit)
+    if wait:
+        got = held(got, *wait)
+    return (value.astype(F32) + got.astype(F32)).astype(BF)
 
 
 def body(
@@ -519,8 +757,10 @@
 
     a_piece = jnp.concatenate([query_proj[0], key_proj[0], tile_of(attn_gain)], axis=1)
     v_piece = jnp.concatenate([out_proj[0], value_proj[0], tile_of(mlp_gain)], axis=1)
-    a_own = gather_rows(a_piece, up_order)
-    v_own = gather_rows(v_piece, down_order)
+    steps = len(up_order)
+    a_own, v_own = gather_some([a_piece, v_piece], [up_order, down_order], 0, steps)
+    a_own = whole_rows(a_own)
+    v_own = whole_rows(v_own)
     a_got = other_core(a_own)
     v_got = other_core(v_own)
     attn_w = (a_own, a_got, v_own, v_got)
@@ -528,21 +768,23 @@
     half = down_proj.shape[1] // 2
     g_keep = pick(gate_proj[0], up_proj[0])
     g_got = other_core(pick(up_proj[0], gate_proj[0]))
-    d_keep = pick(down_proj[0, :half], down_proj[0, half:])
-    d_got = other_core(pick(down_proj[0, half:], down_proj[0, :half]))
-    g_mine = []
-    g_theirs = []
-    d_full = []
-    for layer in range(2):
+    wide_down = jnp.pad(down_proj[0], ((0, 0), (0, -depth % LANES)))
+    d_keep = pick(wide_down[:half], wide_down[half:])
+    d_got = other_core(pick(wide_down[half:], wide_down[:half]))
+    def feed_forward_pieces(layer):
         g_piece = pick(g_keep, g_got) if layer == 0 else pick(g_got, g_keep)
         d_piece = pick(d_keep, d_got) if layer == 0 else pick(d_got, d_keep)
-        mine = gather_rows(g_piece, up_order)
-        g_mine.append(mine)
-        g_theirs.append(other_core(mine))
-        d_mine = gather_rows(d_piece, down_order).reshape(fsdp_count, half, depth)
-        d_other = other_core(d_mine)
-        full = jnp.stack([pick(d_mine, d_other), pick(d_other, d_mine)], axis=1)
-        d_full.append(full.reshape(2 * fsdp_count * half, depth))
+        return [g_piece, d_piece]
+
+    parts_of_down = fsdp_count if half % 16 == 0 else 0
+
+    def down_halves(mine, theirs):
+        if parts_of_down:
+            return (mine, theirs)
+        mine, theirs = [v.reshape(fsdp_count, half, -1) for v in (mine, theirs)]
+        full = jnp.stack([pick(mine, theirs), pick(theirs, mine)], axis=1)
+        full = whole_rows(full)
+        return (full, full)
 
     places = lax.dynamic_index_in_dim(positions, core, 0, keepdims=False).reshape(rows)
     frequency = rope_base ** (-(jnp.arange(HD // 2, dtype=F32) * 2.0 / HD))
@@ -552,73 +794,136 @@
 
     x = lax.dynamic_index_in_dim(inputs, core, 0, keepdims=False).reshape(rows, depth)
     saved = []
+    ff_w = [None, None]
     for layer in range(2):
         normed, q, kv_own = attn_in(layer, idx, x, attn_w, cos, sin)
         kv = [kv_own] + [shifted(kv_own, d) for d in range(1, ctx_count)]
+        orders = [up_order, down_order] if layer == 0 else [down_order, up_order]
+        if layer == 0:
+            parts = lax.optimization_barrier(tuple(feed_forward_pieces(0)) + (a_own, v_own))[:2]
+        parts = gather_some(parts, orders, 0, 1, (normed,))
+        if layer == 1:
+            parts = lax.optimization_barrier(tuple(parts) + (normed,))[:2]
+        g_all, d_all = gather_some(parts, orders, 1, steps)
         attn, lse = attend(idx, q, kv)
-        y, resid, mn, gate, up, hid = mlp(
-            layer, idx, x, attn, attn_w, g_mine[layer], g_theirs[layer], d_full[layer]
-        )
+        g_all, d_all, attn = lax.optimization_barrier((whole_rows(g_all), whole_rows(d_all), attn))
+        ff_w[layer] = (g_all, other_core(g_all)) + down_halves(d_all, other_core(d_all))
+        if layer == 0:
+            parts = lax.optimization_barrier(tuple(feed_forward_pieces(1)) + (g_all, d_all))[:2]
+        y, resid, mn, gate, up, hid = mlp(layer, parts_of_down, idx, x, attn, attn_w, *ff_w[layer])
         saved.append((x, normed, q, kv, attn, lse, resid, mn, gate, up, hid))
         x = y
     outs = [saved[1][0], x]
 
+    pack = Packing(shard, half, gate_proj.shape[2], depth)
+
+    def joined(mine, theirs):
+        got = other_core(theirs)
+        return (mine.astype(F32) + got.astype(F32)).astype(BF)
+
     e = lax.dynamic_index_in_dim(out_grad, core, 0, keepdims=False).reshape(rows, depth)
     entry = [None, None]
-    finished = [None, None]
-    for layer in (1, 0):
+    def feed_forward_back(layer, e, after, between):
         x, normed, q, kv, attn, lse, resid, mn, gate, up, hid = saved[layer]
         gm, gt, rg, mix, ag, mg = mlp_back(
-            layer, idx, e, resid, gate, up, g_mine[layer], g_theirs[layer], d_full[layer], attn_w
+            layer, parts_of_down, idx, e, resid, gate, up, *ff_w[layer], attn_w, after
         )
-        ggm, ggt, dg, og = mlp_grads(hid, e, mn, gm, gt, attn, mix, mg)
-        back = attend_back(idx, q, ag, lse, kv)
-        dq, own_kv = back[:2]
+        done = between(ag) if between else ()
+        first = tuple(d[0] if isinstance(d, tuple) else d for d in done)
+        mine, theirs = mlp_grads(pack, fsdp_count, idx, hid, e, mn, gm, gt, attn, mix, mg, first)
+        result = (rg, ag, joined(mine, theirs))
+        return result + (done,) if between else result
+
+    def attention_back(layer, ag, after):
+        x, normed, q, kv, attn, lse, resid, mn, gate, up, hid = saved[layer]
+        back = attend_back(idx, q, ag, lse, kv, after)
         far_kv = [shifted(part, -(d + 1)) for d, part in enumerate(back[2:])]
-        e, a_mine, a_theirs = input_back(
-            layer, idx, x, normed, dq, own_kv, far_kv, rg, attn_w, cos, sin, og
+        return back[0], back[1], far_kv
+
+    def entry_back(layer, dq, own_kv, far_kv, rg, after):
+        x, normed = saved[layer][:2]
+        e, mine, theirs = input_back(
+            layer, pack, fsdp_count, idx, x, normed, dq, own_kv, far_kv, rg, attn_w, cos, sin, after
         )
         entry[layer] = e
-
-        def joined(mine, theirs):
-            got = other_core(theirs)
-            return (mine.astype(F32) + got.astype(F32)).astype(BF)
-
-        g_sum = scatter_rows(joined(ggm, ggt), up_order)
-        dg = dg.reshape(fsdp_count, 2, half, depth)
-        d_mine = lax.dynamic_index_in_dim(dg, core, 1, keepdims=False)
-        d_theirs = lax.dynamic_index_in_dim(dg, 1 - core, 1, keepdims=False)
-        d_sum = scatter_rows(joined(d_mine, d_theirs).reshape(fsdp_count * half, depth), down_order)
-        a_sum = scatter_rows(joined(a_mine, a_theirs), up_order)
-        finished[layer] = tuple(lax.psum(v, "ctx") for v in (g_sum, d_sum, a_sum))
+        return e, joined(mine, theirs)
+
+    orders = (up_order, down_order)
+
+    def start(value, at):
+        return [first_cut(value[:, :at], up_order), first_cut(value[:, at:], down_order)]
+
+    def sends(cuts):
+        return tuple(c[0] for c in cuts)
+
+    def first_sums(cuts, wait):
+        return [added(c, o[0], wait) for c, o in zip(cuts, orders)]
+
+    def last_sums(values, wait):
+        values = [scatter_rest(v, o, wait) for v, o in zip(values, orders)]
+        return jnp.concatenate(values, axis=1)[0]
+
+    middle = pack.down_at
+    entry_middle = pack.entry_rows // 2
+    rg, ag, m1 = feed_forward_back(1, e, (), ())
+    m1 = start(m1, middle)
+    dq, own_kv, far_kv = attention_back(1, ag, sends(m1))
+    e, a1 = entry_back(1, dq, own_kv, far_kv, rg, ())
+    m1 = first_sums(m1, (e,))
+
+    def between(ag):
+        return (last_sums(m1, (ag,)), *start(a1, entry_middle))
+
+    rg, ag, m0, m1 = feed_forward_back(0, e, tuple(m1), between)
+    m0 = start(m0, middle)
+    m1, a1 = m1[0], list(m1[1:])
+    m1 = ctx_begin(m1, (m0[0][0],))
+    a1 = first_sums(a1, (m0[0][0],))
+    dq, own_kv, far_kv = attention_back(0, ag, sends(m0) + tuple(a1) + (m1,))
+    a1 = last_sums(a1, (dq,))
+    m0 = first_sums(m0, (dq,))
+    m1 = ctx_middle(m1, (far_kv[-1],))
+    e, a0 = entry_back(0, dq, own_kv, far_kv, rg, (a1, m1) + tuple(m0))
+    a0 = start(a0, entry_middle)
+    late = sends(a0)[0]
+    m0 = jnp.concatenate([last_sums(m0, (e,)), a1], axis=0)
+    m0 = ctx_begin(m0, (late,))
+    a0 = first_sums(a0, ())
+    m1 = ctx_end(m1, tuple(a0))
+    a0 = last_sums(a0, ())
+    m0 = ctx_end(ctx_middle(m0, (a0,)))
+    a0 = sum_over_ctx(a0)
+    m0, a1 = m0[: pack.rows], m0[pack.rows :]
 
     def own_layer(zero, one):
         keep = pick(zero, one)
         got = other_core(pick(one, zero))
         return (pick(keep, got), pick(got, keep))
 
+    outs[0], outs[1], entry[0], entry[1], _ = lax.optimization_barrier(
+        (outs[0], outs[1], entry[0], entry[1], late)
+    )
     section_out = jnp.stack(own_layer(outs[0], outs[1])).reshape(1, micro, seqs, block, depth)
     input_grad = jnp.stack(own_layer(entry[0], entry[1])).reshape(1, micro, seqs, block, depth)
-    gate_g, up_g = own_layer(finished[0][0], finished[1][0])
-    down_g = jnp.concatenate(own_layer(finished[0][1], finished[1][1]), axis=0)
-    qk_g, ov_g = own_layer(finished[0][2], finished[1][2])
-    qw, kw = HQ * HD, HK * HD
-
-    def out(v):
-        return v.astype(F32)[None]
+    ff = gate_proj.shape[2]
+    m_got = other_core(pick(m1, m0))
+    gate_g, up_g, down_g, out_g, mlp_gain_g = unpack_mlp(pack, idx, m0, m1, m_got, ff, depth)
+    a_got = other_core(pick(a1, a0))
+    query_g, key_g, value_g, attn_gain_g = unpack_entry(pack, idx, a0, a1, a_got)
+    spare = LANES - HD
 
     return (
         section_out,
         input_grad,
-        out(qk_g[:, qw + kw]),
-        out(qk_g[:, :qw]),
-        out(qk_g[:, qw : qw + kw]),
-        out(ov_g[:, depth : depth + kw]),
-        out(ov_g[:, :depth]),
-        out(ov_g[:, depth + kw]),
-        out(gate_g),
-        out(up_g),
-        out(down_g),
+        attn_gain_g[:, spare][None],
+        query_g[None],
+        key_g[None],
+        value_g[None],
+        out_g[None],
+        mlp_gain_g[:, spare][None],
+        gate_g[None],
+        up_g[None],
+        down_g[None],
     )
 
 

time: 508 us -> 394 us (0.78)
  waiting for transfers between devices: 266 us -> 129 us
  between operations: 15.6 us -> 2.55 us
  starting transfers between devices: 58.7 us -> 70.6 us
  other arithmetic: 34.2 us -> 43.3 us
  local copies, waits for them, and re-layouts: 21.7 us -> 30.6 us
  Pallas kernels: 105 us -> 112 us
    psum x1 -> x0, waiting for transfers between devices: 73.8 us -> none  [body(): finished[layer] = tuple((lax.psum(v, 'ctx') for v in (g_sum, d_sum, a_sum)))]
    ppermute x43 -> x52, waiting for transfers between devices: 161 us -> 92.1 us  [crossed(): return lax.ppermute(value, axis, [(i, i ^ mask) for i in range(count)])]
    ppermute x43 -> x52, starting transfers between devices: 25.2 us -> 39.7 us  [crossed(): return lax.ppermute(value, axis, [(i, i ^ mask) for i in range(count)])]
    unnamed x101 -> x142, local copies, waits for them, and re-layouts: 9.23 us -> 20.1 us
    pallas_call x14 -> x16, Pallas kernels: 105 us -> 112 us  [call(): pl.pallas_call(kernel, out_shape=tuple(outs), in_specs=in_specs, out_spec...]
    another operation x28 -> x24, other arithmetic: 9.86 us -> 3.47 us  [gather_step(): jnp.stack([jnp.where(low, value, got), jnp.where(low, got, value)], axis=...]
    ppermute x12, waiting for transfers between devices: 31.3 us -> 36.9 us  [shifted(): lax.ppermute(value, 'ctx', [(i, i + distance) for i in devices if i + dis...]
    convert_element_type x15 -> x21, other arithmetic: 7.26 us -> 11.1 us  [the longest x16 7.21 us: added(): return (keep.astype(F32) + got.astype(F32)).astype(BF)]
  transfers between devices with their start and end apart: 56 -> 64, of which waited for: 23 -> 27; matrix products, arithmetic and copies ran while one was open for 9% -> 12% of each run, Pallas kernels for 16% -> 20%
where the time goes in v2:
time: 394 us; the launch traced here: 388 us
  waiting for transfers between devices  129 us (33%)
  Pallas kernels  112 us (28%)
  starting transfers between devices  70.6 us (18%)
  other arithmetic  43.3 us (11%)
  local copies, waits for them, and re-layouts  30.6 us (8%)
    pallas_call x16, Pallas kernels, call(): pl.pallas_call(kernel, out_shape=tuple(outs), in_specs=in_specs, out_spec...  112 us
    ppermute x52, waiting for transfers between devices, crossed(): return lax.ppermute(value, axis, [(i, i ^ mask) for i in range(count)])  92.1 us
    ppermute x52, starting transfers between devices, crossed(): return lax.ppermute(value, axis, [(i, i ^ mask) for i in range(count)])  39.7 us
    ppermute x12, waiting for transfers between devices, shifted(): lax.ppermute(value, 'ctx', [(i, i + distance) for i in devices if i + dis...  36.9 us
    ppermute x12, starting transfers between devices, shifted(): lax.ppermute(value, 'ctx', [(i, i + distance) for i in devices if i + dis...  30.9 us
    unnamed x142, local copies, waits for them, and re-layouts  20.1 us
    select_n x8, other arithmetic, pick(): return jnp.where(first, a, b)  8.41 us
  transfers between devices with their start and end apart: 64, of which 27 were waited for; matrix products, arithmetic and copies ran while one was open for 12% of the time, Pallas kernels for 20%

profile of v2, /device:TPU:0, one launch (start us, length us, event | category | flops | bytes accessed | tf_op | source)
XLA Modules:
  0.0 388.5 jit_solution(10504750830027616948)
XLA Ops:
  2.6 3.0 collective-permute-start.4
  17.1 9.5 %collective-permute-done.5 = bf16[2,144,896]{2,1,0:T(8,128)(2,1)S(1)} collective-permute-done((bf16[2,144,896]{2,1,0:T(8,128)(2,1)S(1)}, bf16[2,144,896]{2,1,0:T(8,128)(2,1)S(1)}, u32[]{:S(2)}, u32[]{:S(2)}) %collective-permute-start.5) | collective-permute-done | bytes 516128 | tf_op jit(solution)/shard_map/ppermute | solution.py:615
  28.4 2.3 broadcast_select_fusion.10
  35.9 2.4 pad_maximum_fusion.17
  41.3 4.3 %shard_map.203 = (bf16[256,576]{1,0:T(8,128)(2,1)}, bf16[256,576]{1,0:T(8,128)(2,1)}, bf16[256,384]{1,0:T(8,128)(2,1)}) custom-call(s32[2]{0:T(128)} %pad_add_fusion.refs_0_, bf16[256,576]{1,0:T(8,128)(2,1)} %bitcast.237, bf16[576,896]{1,0:T(8,128)(2,1)} %bitcast.213, bf16[576,896]{1,0:T(8,128)(2,1)} %collective-permute-done.7.refs_3_.refs_10_, ...), custom_call_target="tpu_custom_call" | custom-call | flops 452984 | bytes 5472 | tf_op jit(solution)/shard_map/pallas_call | solution.py:56
  47.5 3.8 collective-permute-done.6
  52.8 3.5 collective-permute-start.12
  56.3 4.5 %collective-permute-start.13 = (bf16[256,384]{1,0:T(8,128)(2,1)S(1)}, bf16[256,384]{1,0:T(8,128)(2,1)S(1)}, u32[]{:S(2)}, u32[]{:S(2)}) collective-permute-start(bf16[256,384]{1,0:T(8,128)(2,1)S(1)} %copy-done.42), channel_id=1, source_target_pairs={{0,8},{4,12},{1,9},{5,13},{2,10},{6,14},{3,11},{7,15},{16,24},{20,... | collective-permute-start | bytes 589832 | tf_op jit(solution)/shard_map/ppermute | solution.py:620
  62.3 3.5 collective-permute-done.13.refs_4_.refs_6_
  65.8 2.1 collective-permute-done.14.refs_5_.refs_7_
  68.6 8.5 %shard_map.204 = (bf16[256,576]{1,0:T(8,128)(2,1)}, f32[16,256]{1,0:T(8,128)}) custom-call(s32[2]{0:T(128)} %pad_add_fusion.refs_0_, bf16[256,576]{1,0:T(8,128)(2,1)} %get-tuple-element.116.refs_1_, bf16[256,384]{1,0:T(8,128)(2,1)} %get-tuple-element.117.refs_2_.refs_4_, bf16[256,384]{1,0:T(8,128)(2,1)} %copy-done.43, bf16[256,384]{1,0:T(8,128)(2,1)} %copy-done.44, ...), custom_call_target="tpu_custom_call" | custom-call | flops 2415919 | bytes 1392 | tf_op jit(solution)/shard_map/pallas_call | solution.py:56
  85.2 7.9 %shard_map.205 = (bf16[256,576]{1,0:T(8,128)(2,1)}, f32[256,576]{1,0:T(8,128)}, bf16[256,576]{1,0:T(8,128)(2,1)}, f32[256,1536]{1,0:T(8,128)}, f32[256,1536]{1,0:T(8,128)}, /*index=5*/bf16[256,1536]{1,0:T(8,128)(2,1)}) custom-call(s32[2]{0:T(128)} %pad_add_fusion.refs_0_, bf16[256,576]{1,0:T(8,128)(2,1)} %bitcast.238, ...), custom_call_target="tpu_custom_call" | custom-call | flops 1528823 | bytes 13271 | tf_op jit(solution)/shard_map/pallas_call | solution.py:56
  93.1 4.3 %shard_map.206 = (bf16[256,576]{1,0:T(8,128)(2,1)}, bf16[256,576]{1,0:T(8,128)(2,1)}, bf16[256,384]{1,0:T(8,128)(2,1)}) custom-call(s32[2]{0:T(128)} %pad_add_fusion.refs_0_, bf16[256,576]{1,0:T(8,128)(2,1)} %get-tuple-element.193.refs_1_, bf16[576,896]{1,0:T(8,128)(2,1)} %bitcast.214, bf16[576,896]{1,0:T(8,128)(2,1)} %collective-permute-done.7.refs_3_.refs_10_, ...), custom_call_target="tpu_custom_call" | custom-call | flops 452984 | bytes 5472 | tf_op jit(solution)/shard_map/pallas_call | solution.py:56
  100.0 6.5 %collective-permute-start.21 = (bf16[256,384]{1,0:T(8,128)(2,1)S(1)}, bf16[256,384]{1,0:T(8,128)(2,1)S(1)}, u32[]{:S(2)}, u32[]{:S(2)}) collective-permute-start(bf16[256,384]{1,0:T(8,128)(2,1)S(1)} %copy-done.46), channel_id=1, source_target_pairs={{0,4},{4,8},{8,12},{1,5},{5,9},{9,13},{2,6},{6,10},{10,14},{3,7},{... | collective-permute-start | bytes 589832 | tf_op jit(solution)/shard_map/ppermute | solution.py:620
  106.5 5.3 %collective-permute-start.22 = (bf16[256,384]{1,0:T(8,128)(2,1)S(1)}, bf16[256,384]{1,0:T(8,128)(2,1)S(1)}, u32[]{:S(2)}, u32[]{:S(2)}) collective-permute-start(bf16[256,384]{1,0:T(8,128)(2,1)S(1)} %copy-done.46), channel_id=1, source_target_pairs={{0,8},{4,12},{1,9},{5,13},{2,10},{6,14},{3,11},{7,15},{16,24},{20,... | collective-permute-start | bytes 589832 | tf_op jit(solution)/shard_map/ppermute | solution.py:620
  113.3 3.8 collective-permute-done.22.refs_4_.refs_6_
  117.1 2.5 collective-permute-done.23.refs_5_.refs_7_
  120.3 8.5 %shard_map.207 = (bf16[256,576]{1,0:T(8,128)(2,1)}, f32[16,256]{1,0:T(8,128)}) custom-call(s32[2]{0:T(128)} %pad_add_fusion.refs_0_, bf16[256,576]{1,0:T(8,128)(2,1)} %get-tuple-element.130.refs_1_, bf16[256,384]{1,0:T(8,128)(2,1)} %get-tuple-element.131.refs_2_.refs_4_, bf16[256,384]{1,0:T(8,128)(2,1)} %copy-done.47, bf16[256,384]{1,0:T(8,128)(2,1)} %copy-done.48, ...), custom_call_target="tpu_custom_call" | custom-call | flops 2415919 | bytes 1392 | tf_op jit(solution)/shard_map/pallas_call | solution.py:56
  131.2 3.6 collective-permute-done.25.refs_8_
  134.8 8.0 %shard_map.208 = (bf16[256,576]{1,0:T(8,128)(2,1)}, f32[256,576]{1,0:T(8,128)}, bf16[256,576]{1,0:T(8,128)(2,1)}, f32[256,1536]{1,0:T(8,128)}, f32[256,1536]{1,0:T(8,128)}, /*index=5*/bf16[256,1536]{1,0:T(8,128)(2,1)}) custom-call(s32[2]{0:T(128)} %pad_add_fusion.refs_0_, bf16[256,576]{1,0:T(8,128)(2,1)} %get-tuple-element.193.refs_1_, ...), custom_call_target="tpu_custom_call" | custom-call | flops 1528823 | bytes 13271 | tf_op jit(solution)/shard_map/pallas_call | solution.py:56
  142.8 9.3 %shard_map.209 = (bf16[256,1536]{1,0:T(8,128)(2,1)}, bf16[256,1536]{1,0:T(8,128)(2,1)}, f32[256,576]{1,0:T(8,128)}, bf16[256,576]{1,0:T(8,128)(2,1)}, bf16[256,5...) custom-call(s32[2]{0:T(128)} %pad_add_fusion.refs_0_, bf16[256,576]{1,0:T(8,128)(2,1)} %bitcast.242, ...), custom_call_target="tpu_custom_call" | custom-call | flops 1528823 | bytes 14499 | tf_op jit(solution)/shard_map/pallas_call | solution.py:56
  152.1 6.7 %shard_map.210 = (bf16[4,3136,128]{2,1,0:T(8,128)(2,1)}, bf16[4,3136,128]{2,1,0:T(8,128)(2,1)}) custom-call(s32[2]{0:T(128)} %pad_add_fusion.refs_0_, bf16[256,1536]{1,0:T(8,128)(2,1)} %get-tuple-element.142.refs_1_, bf16[256,576]{1,0:T(8,128)(2,1)} %bitcast.243, bf16[256,576]{1,0:T(8,128)(2,1)} %get-tuple-element.143.refs_3_, ...), custom_call_target="tpu_custom_call" | custom-call | flops 1528823 | bytes 10108 | tf_op jit(solution)/shard_map/pallas_call | solution.py:56
  158.9 5.8 %collective-permute-done.26 = bf16[4,3136,128]{2,1,0:T(8,128)(2,1)S(1)} collective-permute-done((bf16[4,3136,128]{2,1,0:T(8,128)(2,1)}, bf16[4,3136,128]{2,1,0:T(8,128)(2,1)S(1)}, u32[]{:S(2)}, u32[]{:S(2)}) %collective-permute-start.26) | collective-permute-done | bytes 3211296 | tf_op jit(solution)/shard_map/ppermute | solution.py:615
  166.4 3.7 add_convert_fusion.1
  176.1 11.0 %shard_map.211 = (f32[256,576]{1,0:T(8,128)}, f32[256,384]{1,0:T(8,128)}, bf16[256,384]{1,0:T(8,128)(2,1)}, bf16[256,384]{1,0:T(8,128)(2,1)}, bf16[256,384]{1,0:T(8,128)(2,1)}) custom-call(s32[2]{0:T(128)} %pad_add_fusion.refs_0_, bf16[256,576]{1,0:T(8,128)(2,1)} %get-tuple-element.130.refs_1_, bf16[256,576]{1,0:T(8,128)(2,1)} %get-tuple-element.140.refs_2_, ...), custom_call_target="tpu_custom_call" | custom-call | flops 6039797 | bytes 2965 | tf_op jit(solution)/shard_map/pallas_call | solution.py:56
  191.6 6.4 %collective-permute-done.27.refs_5_ = bf16[256,384]{1,0:T(8,128)(2,1)S(1)} collective-permute-done((bf16[256,384]{1,0:T(8,128)(2,1)}, bf16[256,384]{1,0:T(8,128)(2,1)S(1)}, u32[]{:S(2)}, u32[]{:S(2)}) %collective-permute-start.27) | collective-permute-done | bytes 196640 | tf_op jit(solution)/shard_map/ppermute | solution.py:620
  198.0 13.8 %collective-permute-done.28.refs_6_ = bf16[256,384]{1,0:T(8,128)(2,1)S(1)} collective-permute-done((bf16[256,384]{1,0:T(8,128)(2,1)}, bf16[256,384]{1,0:T(8,128)(2,1)S(1)}, u32[]{:S(2)}, u32[]{:S(2)}) %collective-permute-start.28) | collective-permute-done | bytes 196640 | tf_op jit(solution)/shard_map/ppermute | solution.py:620
  212.6 5.9 %shard_map.212 = (bf16[256,576]{1,0:T(8,128)(2,1)}, bf16[4,576,128]{2,1,0:T(8,128)(2,1)}, bf16[4,576,128]{2,1,0:T(8,128)(2,1)}) custom-call(s32[2]{0:T(128)} %pad_add_fusion.refs_0_, bf16[256,576]{1,0:T(8,128)(2,1)} %get-tuple-element.193.refs_1_, bf16[256,576]{1,0:T(8,128)(2,1)} %get-tuple-element.124.refs_2_, f32[256,576]{1,0:T(8,128)} %get-tuple-element.150.refs_3_, ...), custom_call_target="tpu_custom_call" | custom-call | flops 905969 | bytes 8617 | tf_op jit(solution)/shard_map/pallas_call | solution.py:56
  223.6 9.3 %shard_map.213 = (bf16[256,1536]{1,0:T(8,128)(2,1)}, bf16[256,1536]{1,0:T(8,128)(2,1)}, f32[256,576]{1,0:T(8,128)}, bf16[256,576]{1,0:T(8,128)(2,1)}, bf16[256,5...) custom-call(s32[2]{0:T(128)} %pad_add_fusion.refs_0_, bf16[256,576]{1,0:T(8,128)(2,1)} %get-tuple-element.196.refs_1_.refs_2_, ...), custom_call_target="tpu_custom_call" | custom-call | flops 1528823 | bytes 14499 | tf_op jit(solution)/shard_map/pallas_call | solution.py:56
  233.0 2.1 collective-permute-done.32
  237.2 6.3 %shard_map.214 = (bf16[4,3136,128]{2,1,0:T(8,128)(2,1)}, bf16[4,3136,128]{2,1,0:T(8,128)(2,1)}) custom-call(s32[2]{0:T(128)} %pad_add_fusion.refs_0_, bf16[256,1536]{1,0:T(8,128)(2,1)} %get-tuple-element.164.refs_1_, bf16[256,576]{1,0:T(8,128)(2,1)} %get-tuple-element.196.refs_1_.refs_2_, bf16[256,576]{1,0:T(8,128)(2,1)} %get-tuple-element.165.refs_3_, ...), custom_call_target="tpu_custom_call" | custom-call | flops 1528823 | bytes 10108 | tf_op jit(solution)/shard_map/pallas_call | solution.py:56
  246.7 2.9 collective-permute-done.35
  249.6 3.7 add_convert_fusion
  254.9 2.9 collective-permute-done.38
  262.5 10.9 %shard_map.215 = (f32[256,576]{1,0:T(8,128)}, f32[256,384]{1,0:T(8,128)}, bf16[256,384]{1,0:T(8,128)(2,1)}, bf16[256,384]{1,0:T(8,128)(2,1)}, bf16[256,384]{1,0:T(8,128)(2,1)}) custom-call(s32[2]{0:T(128)} %pad_add_fusion.refs_0_, bf16[256,576]{1,0:T(8,128)(2,1)} %get-tuple-element.116.refs_1_, bf16[256,576]{1,0:T(8,128)(2,1)} %get-tuple-element.162.refs_2_, ...), custom_call_target="tpu_custom_call" | custom-call | flops 6039797 | bytes 2965 | tf_op jit(solution)/shard_map/pallas_call | solution.py:56
  275.3 3.8 collective-permute-done.42
  280.9 2.6 collective-permute-done.43
  288.2 2.7 collective-permute-start.62
  293.2 2.3 collective-permute-done.39.refs_5_
  295.5 2.4 collective-permute-done.40.refs_6_
  298.6 5.9 %shard_map.216 = (bf16[256,576]{1,0:T(8,128)(2,1)}, bf16[4,576,128]{2,1,0:T(8,128)(2,1)}, bf16[4,576,128]{2,1,0:T(8,128)(2,1)}) custom-call(s32[2]{0:T(128)} %pad_add_fusion.refs_0_, bf16[256,576]{1,0:T(8,128)(2,1)} %bitcast.239, bf16[256,576]{1,0:T(8,128)(2,1)} %get-tuple-element.112.refs_2_, f32[256,576]{1,0:T(8,128)} %get-tuple-element.179.refs_3_, ...), custom_call_target="tpu_custom_call" | custom-call | flops 905969 | bytes 8617 | tf_op jit(solution)/shard_map/pallas_call | solution.py:56
  307.8 9.7 %collective-permute-done.56 = bf16[1,1728,128]{2,1,0:T(8,128)(2,1)S(1)} collective-permute-done((bf16[1,1728,128]{2,1,0:T(8,128)(2,1)S(1)}, bf16[1,1728,128]{2,1,0:T(8,128)(2,1)S(1)}, u32[]{:S(2)}, u32[]{:S(2)}) %collective-permute-start.56) | collective-permute-done | bytes 442400 | tf_op jit(solution)/shard_map/ppermute | solution.py:615
  322.6 3.7 collective-permute-done.50
  329.0 2.5 collective-permute-done.58
  334.6 20.9 %collective-permute-done.59 = bf16[1856,128]{1,0:T(8,128)(2,1)S(1)} collective-permute-done((bf16[1856,128]{1,0:T(8,128)(2,1)S(1)}, bf16[1856,128]{1,0:T(8,128)(2,1)S(1)}, u32[]{:S(2)}, u32[]{:S(2)}) %collective-permute-start.59) | collective-permute-done | bytes 475168 | tf_op jit(solution)/shard_map/ppermute | solution.py:615
  357.7 13.0 %collective-permute-done.60 = bf16[1856,128]{1,0:T(8,128)(2,1)S(1)} collective-permute-done((bf16[1856,128]{1,0:T(8,128)(2,1)S(1)}, bf16[1856,128]{1,0:T(8,128)(2,1)S(1)}, u32[]{:S(2)}, u32[]{:S(2)}) %collective-permute-start.60) | collective-permute-done | bytes 475168 | tf_op jit(solution)/shard_map/ppermute | solution.py:615
  381.2 3.7 shard_map.218
  384.8 2.5 copy.57
  (348 shorter events, 111.8 us)
Async XLA Ops:
  2.6 10.0 %collective-permute-start.4 = (bf16[144,896]{1,0:T(8,128)(2,1)S(1)}, bf16[144,896]{1,0:T(8,128)(2,1)S(1)}, u32[]{:S(2)}, u32[]{:S(2)}) collective-permute-start(bf16[144,896]{1,0:T(8,128)(2,1)S(1)} %pad_maximum_fusion.16), channel_id=1, source_target_pairs={{0,2},{1,3},{2,0},{3,1},{4,6},{5,7},{6,4},{7,5},{8,10},{9,11},{10,... | collective-permute-start | bytes 774152 | tf_op jit(solution)/shard_map/ppermute | solution.py:615
  11.2 17.0 %collective-permute-start.1 = (bf16[192,640]{1,0:T(8,128)(2,1)}, bf16[192,640]{1,0:T(8,128)(2,1)}, u32[]{:S(2)}, u32[]{:S(2)}) collective-permute-start(bf16[192,640]{1,0:T(8,128)(2,1)} %broadcast_select_fusion.12), channel_id=1, source_target_pairs={{0,16},{16,0},{1,17},{17,1},{2,18},{18,2},{3,19},{19,3},{4,20},{20... | collective-permute-start | bytes 737288 | tf_op jit(solution)/shard_map/ppermute | solution.py:615
  12.1 18.6 %collective-permute-start = (bf16[144,1536]{1,0:T(8,128)(2,1)}, bf16[144,1536]{1,0:T(8,128)(2,1)}, u32[]{:S(2)}, u32[]{:S(2)}) collective-permute-start(bf16[144,1536]{1,0:T(8,128)(2,1)} %select_bitcast_fusion.16), channel_id=1, source_target_pairs={{0,16},{16,0},{1,17},{17,1},{2,18},{18,2},{3,19},{19,3},{4,20},{20... | collective-permute-start | bytes 1327112 | tf_op jit(solution)/shard_map/ppermute | solution.py:615
  12.9 13.7 %collective-permute-start.5 = (bf16[2,144,896]{2,1,0:T(8,128)(2,1)S(1)}, bf16[2,144,896]{2,1,0:T(8,128)(2,1)S(1)}, u32[]{:S(2)}, u32[]{:S(2)}) collective-permute-start(bf16[2,144,896]{2,1,0:T(8,128)(2,1)S(1)} %pad_maximum_fusion.12), channel_id=1, source_target_pairs={{0,1},{1,0},{2,3},{3,2},{4,5},{5,4},{6,7},{7,6},{8,9},{9,8},{10,11... | collective-permute-start | bytes 1548296 | tf_op jit(solution)/shard_map/ppermute | solution.py:615
  15.6 12.4 %collective-permute-start.3 = (bf16[2,144,896]{2,1,0:T(8,128)(2,1)S(1)}, bf16[2,144,896]{2,1,0:T(8,128)(2,1)S(1)}, u32[]{:S(2)}, u32[]{:S(2)}) collective-permute-start(bf16[2,144,896]{2,1,0:T(8,128)(2,1)S(1)} %pad_maximum_fusion.11), channel_id=1, source_target_pairs={{0,2},{1,3},{2,0},{3,1},{4,6},{5,7},{6,4},{7,5},{8,10},{9,11},{10,... | collective-permute-start | bytes 1548296 | tf_op jit(solution)/shard_map/ppermute | solution.py:615
  27.0 13.4 %collective-permute-start.8 = (bf16[576,896]{1,0:T(8,128)(2,1)S(1)}, bf16[576,896]{1,0:T(8,128)(2,1)S(1)}, u32[]{:S(2)}, u32[]{:S(2)}) collective-permute-start(bf16[576,896]{1,0:T(8,128)(2,1)S(1)} %bitcast.203), channel_id=1, source_target_pairs={{0,16},{16,0},{1,17},{17,1},{2,18},{18,2},{3,19},{19,3},{4,20},{20... | collective-permute-start | bytes 3096584 | tf_op jit(solution)/shard_map/ppermute | solution.py:615
  28.2 12.2 %collective-permute-start.7 = (bf16[576,896]{1,0:T(8,128)(2,1)S(1)}, bf16[576,896]{1,0:T(8,128)(2,1)}, u32[]{:S(2)}, u32[]{:S(2)}) collective-permute-start(bf16[576,896]{1,0:T(8,128)(2,1)S(1)} %bitcast.212), channel_id=1, source_target_pairs={{0,16},{16,0},{1,17},{17,1},{2,18},{18,2},{3,19},{19,3},{4,20},{20... | collective-permute-start | bytes 3096584 | tf_op jit(solution)/shard_map/ppermute | solution.py:615
  32.7 12.9 %collective-permute-start.10 = (bf16[192,640]{1,0:T(8,128)(2,1)}, bf16[192,640]{1,0:T(8,128)(2,1)}, u32[]{:S(2)}, u32[]{:S(2)}) collective-permute-start(bf16[192,640]{1,0:T(8,128)(2,1)} %get-tuple-element.114), channel_id=1, source_target_pairs={{0,2},{1,3},{2,0},{3,1},{4,6},{5,7},{6,4},{7,5},{8,10},{9,11},{10,... | collective-permute-start | bytes 737288 | tf_op jit(solution)/shard_map/ppermute | solution.py:615
  38.3 13.0 %collective-permute-start.6 = (bf16[144,1536]{1,0:T(8,128)(2,1)S(1)}, bf16[144,1536]{1,0:T(8,128)(2,1)S(1)}, u32[]{:S(2)}, u32[]{:S(2)}) collective-permute-start(bf16[144,1536]{1,0:T(8,128)(2,1)S(1)} %copy-done.34), channel_id=1, source_target_pairs={{0,1},{1,0},{2,3},{3,2},{4,5},{5,4},{6,7},{7,6},{8,9},{9,8},{10,11... | collective-permute-start | bytes 1327112 | tf_op jit(solution)/shard_map/ppermute | solution.py:615
  46.8 30.3 %collective-permute-start.11 = (bf16[2,192,640]{2,1,0:T(8,128)(2,1)S(1)}, bf16[2,192,640]{2,1,0:T(8,128)(2,1)S(1)}, u32[]{:S(2)}, u32[]{:S(2)}) collective-permute-start(bf16[2,192,640]{2,1,0:T(8,128)(2,1)S(1)} %pad_maximum_fusion.13), channel_id=1, source_target_pairs={{0,1},{1,0},{2,3},{3,2},{4,5},{5,4},{6,7},{7,6},{8,9},{9,8},{10,11... | collective-permute-start | bytes 1474568 | tf_op jit(solution)/shard_map/ppermute | solution.py:615
  51.5 26.0 %collective-permute-start.9 = (bf16[2,144,1536]{2,1,0:T(8,128)(2,1)S(1)}, bf16[2,144,1536]{2,1,0:T(8,128)(2,1)S(1)}, u32[]{:S(2)}, u32[]{:S(2)}) collective-permute-start(bf16[2,144,1536]{2,1,0:T(8,128)(2,1)S(1)} %pad_maximum_fusion.7), channel_id=1, source_target_pairs={{0,2},{1,3},{2,0},{3,1},{4,6},{5,7},{6,4},{7,5},{8,10},{9,11},{10,... | collective-permute-start | bytes 2654216 | tf_op jit(solution)/shard_map/ppermute | solution.py:615
  52.8 9.5 %collective-permute-start.12 = (bf16[256,384]{1,0:T(8,128)(2,1)S(1)}, bf16[256,384]{1,0:T(8,128)(2,1)S(1)}, u32[]{:S(2)}, u32[]{:S(2)}) collective-permute-start(bf16[256,384]{1,0:T(8,128)(2,1)S(1)} %copy-done.42), channel_id=1, source_target_pairs={{0,4},{4,8},{8,12},{1,5},{5,9},{9,13},{2,6},{6,10},{10,14},{3,7},{... | collective-permute-start | bytes 589832 | tf_op jit(solution)/shard_map/ppermute | solution.py:620
  56.3 9.5 %collective-permute-start.13 = (bf16[256,384]{1,0:T(8,128)(2,1)S(1)}, bf16[256,384]{1,0:T(8,128)(2,1)S(1)}, u32[]{:S(2)}, u32[]{:S(2)}) collective-permute-start(bf16[256,384]{1,0:T(8,128)(2,1)S(1)} %copy-done.42), channel_id=1, source_target_pairs={{0,8},{4,12},{1,9},{5,13},{2,10},{6,14},{3,11},{7,15},{16,24},{20,... | collective-permute-start | bytes 589832 | tf_op jit(solution)/shard_map/ppermute | solution.py:620
  78.8 18.6 %collective-permute-start.18 = (bf16[192,640]{1,0:T(8,128)(2,1)S(1)}, bf16[192,640]{1,0:T(8,128)(2,1)S(1)}, u32[]{:S(2)}, u32[]{:S(2)}) collective-permute-start(bf16[192,640]{1,0:T(8,128)(2,1)S(1)} %copy-done.40), channel_id=1, source_target_pairs={{0,1},{1,0},{2,3},{3,2},{4,5},{5,4},{6,7},{7,6},{8,9},{9,8},{10,11... | collective-permute-start | bytes 737288 | tf_op jit(solution)/shard_map/ppermute | solution.py:615
  80.5 17.0 %collective-permute-start.17 = (bf16[144,1536]{1,0:T(8,128)(2,1)S(1)}, bf16[144,1536]{1,0:T(8,128)(2,1)S(1)}, u32[]{:S(2)}, u32[]{:S(2)}) collective-permute-start(bf16[144,1536]{1,0:T(8,128)(2,1)S(1)} %copy-done.33), channel_id=1, source_target_pairs={{0,2},{1,3},{2,0},{3,1},{4,6},{5,7},{6,4},{7,5},{8,10},{9,11},{10,... | collective-permute-start | bytes 1327112 | tf_op jit(solution)/shard_map/ppermute | solution.py:615
  97.7 31.1 %collective-permute-start.20 = (bf16[2,192,640]{2,1,0:T(8,128)(2,1)S(1)}, bf16[2,192,640]{2,1,0:T(8,128)(2,1)S(1)}, u32[]{:S(2)}, u32[]{:S(2)}) collective-permute-start(bf16[2,192,640]{2,1,0:T(8,128)(2,1)S(1)} %pad_maximum_fusion.14), channel_id=1, source_target_pairs={{0,2},{1,3},{2,0},{3,1},{4,6},{5,7},{6,4},{7,5},{8,10},{9,11},{10,... | collective-permute-start | bytes 1474568 | tf_op jit(solution)/shard_map/ppermute | solution.py:615
  98.3 30.7 %collective-permute-start.19 = (bf16[2,144,1536]{2,1,0:T(8,128)(2,1)S(1)}, bf16[2,144,1536]{2,1,0:T(8,128)(2,1)S(1)}, u32[]{:S(2)}, u32[]{:S(2)}) collective-permute-start(bf16[2,144,1536]{2,1,0:T(8,128)(2,1)S(1)} %pad_maximum_fusion.8), channel_id=1, source_target_pairs={{0,1},{1,0},{2,3},{3,2},{4,5},{5,4},{6,7},{7,6},{8,9},{9,8},{10,11... | collective-permute-start | bytes 2654216 | tf_op jit(solution)/shard_map/ppermute | solution.py:615
  100.0 13.3 %collective-permute-start.21 = (bf16[256,384]{1,0:T(8,128)(2,1)S(1)}, bf16[256,384]{1,0:T(8,128)(2,1)S(1)}, u32[]{:S(2)}, u32[]{:S(2)}) collective-permute-start(bf16[256,384]{1,0:T(8,128)(2,1)S(1)} %copy-done.46), channel_id=1, source_target_pairs={{0,4},{4,8},{8,12},{1,5},{5,9},{9,13},{2,6},{6,10},{10,14},{3,7},{... | collective-permute-start | bytes 589832 | tf_op jit(solution)/shard_map/ppermute | solution.py:620
  106.5 10.6 %collective-permute-start.22 = (bf16[256,384]{1,0:T(8,128)(2,1)S(1)}, bf16[256,384]{1,0:T(8,128)(2,1)S(1)}, u32[]{:S(2)}, u32[]{:S(2)}) collective-permute-start(bf16[256,384]{1,0:T(8,128)(2,1)S(1)} %copy-done.46), channel_id=1, source_target_pairs={{0,8},{4,12},{1,9},{5,13},{2,10},{6,14},{3,11},{7,15},{16,24},{20,... | collective-permute-start | bytes 589832 | tf_op jit(solution)/shard_map/ppermute | solution.py:620
  111.8 7.9 %collective-permute-start.23 = (bf16[256,384]{1,0:T(8,128)(2,1)S(1)}, bf16[256,384]{1,0:T(8,128)(2,1)S(1)}, u32[]{:S(2)}, u32[]{:S(2)}) collective-permute-start(bf16[256,384]{1,0:T(8,128)(2,1)S(1)} %copy-done.46), channel_id=1, source_target_pairs={{0,12},{1,13},{2,14},{3,15},{16,28},{17,29},{18,30},{19,31}} | collective-permute-start | bytes 589832 | tf_op jit(solution)/shard_map/ppermute | solution.py:620
  172.2 46.4 %collective-permute-start.31 = (bf16[2,1,1408,128]{3,2,1,0:T(8,128)(2,1)}, bf16[2,1,1408,128]{3,2,1,0:T(8,128)(2,1)}, u32[]{:S(2)}, u32[]{:S(2)}) collective-permute-start(bf16[2,1,1408,128]{3,2,1,0:T(8,128)(2,1)} %dynamic-slice_bitcast_fusion.3.refs_9_), channel_id=1, source_target_pairs={{0,2},{1,3},{2,0},{3,1},{4,6},{5,7},{6,4},{7,5},{8,10},{9,11},{10,... | collective-permute-start | bytes 2162696 | tf_op jit(solution)/shard_map/ppermute | solution.py:615
  187.0 11.0 %collective-permute-start.27 = (bf16[256,384]{1,0:T(8,128)(2,1)}, bf16[256,384]{1,0:T(8,128)(2,1)S(1)}, u32[]{:S(2)}, u32[]{:S(2)}) collective-permute-start(bf16[256,384]{1,0:T(8,128)(2,1)} %get-tuple-element.152), channel_id=1, source_target_pairs={{4,0},{8,4},{12,8},{5,1},{9,5},{13,9},{6,2},{10,6},{14,10},{7,3},{... | collective-permute-start | bytes 589832 | tf_op jit(solution)/shard_map/ppermute | solution.py:620
  188.3 23.5 %collective-permute-start.28 = (bf16[256,384]{1,0:T(8,128)(2,1)}, bf16[256,384]{1,0:T(8,128)(2,1)S(1)}, u32[]{:S(2)}, u32[]{:S(2)}) collective-permute-start(bf16[256,384]{1,0:T(8,128)(2,1)} %get-tuple-element.153), channel_id=1, source_target_pairs={{8,0},{12,4},{9,1},{13,5},{10,2},{14,6},{11,3},{15,7},{24,16},{28,... | collective-permute-start | bytes 589832 | tf_op jit(solution)/shard_map/ppermute | solution.py:620
  189.6 22.2 %collective-permute-start.29 = (bf16[256,384]{1,0:T(8,128)(2,1)}, bf16[256,384]{1,0:T(8,128)(2,1)S(1)}, u32[]{:S(2)}, u32[]{:S(2)}) collective-permute-start(bf16[256,384]{1,0:T(8,128)(2,1)} %get-tuple-element.154), channel_id=1, source_target_pairs={{12,0},{13,1},{14,2},{15,3},{28,16},{29,17},{30,18},{31,19}} | collective-permute-start | bytes 589832 | tf_op jit(solution)/shard_map/ppermute | solution.py:620
  191.1 31.3 %collective-permute-start.30 = (bf16[2,1,1728,128]{3,2,1,0:T(8,128)(2,1)S(1)}, bf16[2,1,1728,128]{3,2,1,0:T(8,128)(2,1)S(1)}, u32[]{:S(2)}, u32[]{:S(2)}) collective-permute-start(bf16[2,1,1728,128]{3,2,1,0:T(8,128)(2,1)S(1)} %copy-done.25), channel_id=1, source_target_pairs={{0,1},{1,0},{2,3},{3,2},{4,5},{5,4},{6,7},{7,6},{8,9},{9,8},{10,11... | collective-permute-start | bytes 2654216 | tf_op jit(solution)/shard_map/ppermute | solution.py:615
  220.1 12.8 %collective-permute-start.33 = (bf16[1,1408,128]{2,1,0:T(8,128)(2,1)S(1)}, bf16[1,1408,128]{2,1,0:T(8,128)(2,1)S(1)}, u32[]{:S(2)}, u32[]{:S(2)}) collective-permute-start(bf16[1,1408,128]{2,1,0:T(8,128)(2,1)S(1)} %dynamic-slice_bitcast_fusion.7), channel_id=1, source_target_pairs={{0,1},{1,0},{2,3},{3,2},{4,5},{5,4},{6,7},{7,6},{8,9},{9,8},{10,11... | collective-permute-start | bytes 1081352 | tf_op jit(solution)/shard_map/ppermute | solution.py:615
  222.7 12.4 %collective-permute-start.32 = (bf16[1,1728,128]{2,1,0:T(8,128)(2,1)S(1)}, bf16[1,1728,128]{2,1,0:T(8,128)(2,1)S(1)}, u32[]{:S(2)}, u32[]{:S(2)}) collective-permute-start(bf16[1,1728,128]{2,1,0:T(8,128)(2,1)S(1)} %dynamic-slice_bitcast_fusion.5), channel_id=1, source_target_pairs={{0,2},{1,3},{2,0},{3,1},{4,6},{5,7},{6,4},{7,5},{8,10},{9,11},{10,... | collective-permute-start | bytes 1327112 | tf_op jit(solution)/shard_map/ppermute | solution.py:615
  243.5 14.3 %collective-permute-start.37 = (bf16[2,1,288,128]{3,2,1,0:T(8,128)(2,1)S(1)}, bf16[2,1,288,128]{3,2,1,0:T(8,128)(2,1)S(1)}, u32[]{:S(2)}, u32[]{:S(2)}) collective-permute-start(bf16[2,1,288,128]{3,2,1,0:T(8,128)(2,1)S(1)} %copy-done.53), channel_id=1, source_target_pairs={{0,2},{1,3},{2,0},{3,1},{4,6},{5,7},{6,4},{7,5},{8,10},{9,11},{10,... | collective-permute-start | bytes 442376 | tf_op jit(solution)/shard_map/ppermute | solution.py:615
  244.1 14.4 %collective-permute-start.36 = (bf16[2,1,288,128]{3,2,1,0:T(8,128)(2,1)S(1)}, bf16[2,1,288,128]{3,2,1,0:T(8,128)(2,1)S(1)}, u32[]{:S(2)}, u32[]{:S(2)}) collective-permute-start(bf16[2,1,288,128]{3,2,1,0:T(8,128)(2,1)S(1)} %copy-done.52), channel_id=1, source_target_pairs={{0,1},{1,0},{2,3},{3,2},{4,5},{5,4},{6,7},{7,6},{8,9},{9,8},{10,11... | collective-permute-start | bytes 442376 | tf_op jit(solution)/shard_map/ppermute | solution.py:615
  246.7 11.1 %collective-permute-start.38 = (bf16[1568,128]{1,0:T(8,128)(2,1)S(1)}, bf16[1568,128]{1,0:T(8,128)(2,1)S(1)}, u32[]{:S(2)}, u32[]{:S(2)}) collective-permute-start(bf16[1568,128]{1,0:T(8,128)(2,1)S(1)} %fusion.15), channel_id=1, source_target_pairs={{0,4},{4,0},{8,12},{12,8},{1,5},{5,1},{9,13},{13,9},{2,6},{6,2},{1... | collective-permute-start | bytes 1204232 | tf_op jit(solution)/shard_map/ppermute | solution.py:615
  253.6 38.4 %collective-permute-start.45 = (bf16[2,1,1728,128]{3,2,1,0:T(8,128)(2,1)S(1)}, bf16[2,1,1728,128]{3,2,1,0:T(8,128)(2,1)S(1)}, u32[]{:S(2)}, u32[]{:S(2)}) collective-permute-start(bf16[2,1,1728,128]{3,2,1,0:T(8,128)(2,1)S(1)} %dynamic-slice_bitcast_fusion.refs_8_), channel_id=1, source_target_pairs={{0,1},{1,0},{2,3},{3,2},{4,5},{5,4},{6,7},{7,6},{8,9},{9,8},{10,11... | collective-permute-start | bytes 2654216 | tf_op jit(solution)/shard_map/ppermute | solution.py:615
  258.6 32.3 %collective-permute-start.46 = (bf16[2,1,1408,128]{3,2,1,0:T(8,128)(2,1)S(1)}, bf16[2,1,1408,128]{3,2,1,0:T(8,128)(2,1)S(1)}, u32[]{:S(2)}, u32[]{:S(2)}) collective-permute-start(bf16[2,1,1408,128]{3,2,1,0:T(8,128)(2,1)S(1)} %dynamic-slice_bitcast_fusion.2.refs_9_), channel_id=1, source_target_pairs={{0,2},{1,3},{2,0},{3,1},{4,6},{5,7},{6,4},{7,5},{8,10},{9,11},{10,... | collective-permute-start | bytes 2162696 | tf_op jit(solution)/shard_map/ppermute | solution.py:615
  261.8 25.3 %collective-permute-start.44 = (bf16[1568,128]{1,0:T(8,128)(2,1)S(1)}, bf16[1568,128]{1,0:T(8,128)(2,1)S(1)}, u32[]{:S(2)}, u32[]{:S(2)}) collective-permute-start(bf16[1568,128]{1,0:T(8,128)(2,1)S(1)} %fusion.7.refs_12_), channel_id=1, source_target_pairs={{0,8},{4,12},{8,0},{12,4},{1,9},{5,13},{9,1},{13,5},{2,10},{6,14},... | collective-permute-start | bytes 1204232 | tf_op jit(solution)/shard_map/ppermute | solution.py:615
  273.5 12.1 %collective-permute-start.41 = (bf16[256,384]{1,0:T(8,128)(2,1)}, bf16[256,384]{1,0:T(8,128)(2,1)S(1)}, u32[]{:S(2)}, u32[]{:S(2)}) collective-permute-start(bf16[256,384]{1,0:T(8,128)(2,1)} %get-tuple-element.183), channel_id=1, source_target_pairs={{12,0},{13,1},{14,2},{15,3},{28,16},{29,17},{30,18},{31,19}} | collective-permute-start | bytes 589832 | tf_op jit(solution)/shard_map/ppermute | solution.py:620
  283.5 12.0 %collective-permute-start.39 = (bf16[256,384]{1,0:T(8,128)(2,1)}, bf16[256,384]{1,0:T(8,128)(2,1)S(1)}, u32[]{:S(2)}, u32[]{:S(2)}) collective-permute-start(bf16[256,384]{1,0:T(8,128)(2,1)} %get-tuple-element.181), channel_id=1, source_target_pairs={{4,0},{8,4},{12,8},{5,1},{9,5},{13,9},{6,2},{10,6},{14,10},{7,3},{... | collective-permute-start | bytes 589832 | tf_op jit(solution)/shard_map/ppermute | solution.py:620
  285.5 12.4 %collective-permute-start.40 = (bf16[256,384]{1,0:T(8,128)(2,1)}, bf16[256,384]{1,0:T(8,128)(2,1)S(1)}, u32[]{:S(2)}, u32[]{:S(2)}) collective-permute-start(bf16[256,384]{1,0:T(8,128)(2,1)} %get-tuple-element.182), channel_id=1, source_target_pairs={{8,0},{12,4},{9,1},{13,5},{10,2},{14,6},{11,3},{15,7},{24,16},{28,... | collective-permute-start | bytes 589832 | tf_op jit(solution)/shard_map/ppermute | solution.py:620
  288.2 39.0 %collective-permute-start.62 = (bf16[1568,128]{1,0:T(8,128)(2,1)S(1)}, bf16[1568,128]{1,0:T(8,128)(2,1)S(1)}, u32[]{:S(2)}, u32[]{:S(2)}) collective-permute-start(bf16[1568,128]{1,0:T(8,128)(2,1)S(1)} %add_convert_fusion.6.refs_16_), channel_id=1, source_target_pairs={{0,4},{4,0},{8,12},{12,8},{1,5},{5,1},{9,13},{13,9},{2,6},{6,2},{1... | collective-permute-start | bytes 1204232 | tf_op jit(solution)/shard_map/ppermute | solution.py:615
  291.2 15.5 %collective-permute-start.57 = (bf16[1,1408,128]{2,1,0:T(8,128)(2,1)S(1)}, bf16[1,1408,128]{2,1,0:T(8,128)(2,1)S(1)}, u32[]{:S(2)}, u32[]{:S(2)}) collective-permute-start(bf16[1,1408,128]{2,1,0:T(8,128)(2,1)S(1)} %dynamic-slice_bitcast_fusion.6), channel_id=1, source_target_pairs={{0,1},{1,0},{2,3},{3,2},{4,5},{5,4},{6,7},{7,6},{8,9},{9,8},{10,11... | collective-permute-start | bytes 1081352 | tf_op jit(solution)/shard_map/ppermute | solution.py:615
  304.5 16.2 %collective-permute-start.47 = (bf16[4,576,128]{2,1,0:T(8,128)(2,1)}, bf16[4,576,128]{2,1,0:T(8,128)(2,1)S(1)}, u32[]{:S(2)}, u32[]{:S(2)}) collective-permute-start(bf16[4,576,128]{2,1,0:T(8,128)(2,1)} %get-tuple-element.192), channel_id=1, source_target_pairs={{0,16},{16,0},{1,17},{17,1},{2,18},{18,2},{3,19},{19,3},{4,20},{20... | collective-permute-start | bytes 1769480 | tf_op jit(solution)/shard_map/ppermute | solution.py:615
  304.7 12.8 %collective-permute-start.56 = (bf16[1,1728,128]{2,1,0:T(8,128)(2,1)S(1)}, bf16[1,1728,128]{2,1,0:T(8,128)(2,1)S(1)}, u32[]{:S(2)}, u32[]{:S(2)}) collective-permute-start(bf16[1,1728,128]{2,1,0:T(8,128)(2,1)S(1)} %dynamic-slice_bitcast_fusion.4), channel_id=1, source_target_pairs={{0,2},{1,3},{2,0},{3,1},{4,6},{5,7},{6,4},{7,5},{8,10},{9,11},{10,... | collective-permute-start | bytes 1327112 | tf_op jit(solution)/shard_map/ppermute | solution.py:615
  318.8 12.7 %collective-permute-start.58 = (bf16[1856,128]{1,0:T(8,128)(2,1)S(1)}, bf16[1856,128]{1,0:T(8,128)(2,1)S(1)}, u32[]{:S(2)}, u32[]{:S(2)}) collective-permute-start(bf16[1856,128]{1,0:T(8,128)(2,1)S(1)} %fusion.10), channel_id=1, source_target_pairs={{0,4},{4,0},{8,12},{12,8},{1,5},{5,1},{9,13},{13,9},{2,6},{6,2},{1... | collective-permute-start | bytes 1425416 | tf_op jit(solution)/shard_map/ppermute | solution.py:615
  322.4 33.3 %collective-permute-start.49 = (bf16[256,576]{1,0:T(8,128)(2,1)S(1)}, bf16[256,576]{1,0:T(8,128)(2,1)S(1)}, u32[]{:S(2)}, u32[]{:S(2)}) collective-permute-start(bf16[256,576]{1,0:T(8,128)(2,1)S(1)} %broadcast_select_fusion.6), channel_id=1, source_target_pairs={{0,16},{16,0},{1,17},{17,1},{2,18},{18,2},{3,19},{19,3},{4,20},{20... | collective-permute-start | bytes 884744 | tf_op jit(solution)/shard_map/ppermute | solution.py:615
  326.3 46.1 %collective-permute-start.48 = (bf16[256,576]{1,0:T(8,128)(2,1)S(1)}, bf16[256,576]{1,0:T(8,128)(2,1)S(1)}, u32[]{:S(2)}, u32[]{:S(2)}) collective-permute-start(bf16[256,576]{1,0:T(8,128)(2,1)S(1)} %broadcast_select_fusion.8), channel_id=1, source_target_pairs={{0,16},{16,0},{1,17},{17,1},{2,18},{18,2},{3,19},{19,3},{4,20},{20... | collective-permute-start | bytes 884744 | tf_op jit(solution)/shard_map/ppermute | solution.py:615
  332.6 22.9 %collective-permute-start.59 = (bf16[1856,128]{1,0:T(8,128)(2,1)S(1)}, bf16[1856,128]{1,0:T(8,128)(2,1)S(1)}, u32[]{:S(2)}, u32[]{:S(2)}) collective-permute-start(bf16[1856,128]{1,0:T(8,128)(2,1)S(1)} %add_convert_fusion.5), channel_id=1, source_target_pairs={{0,8},{4,12},{8,0},{12,4},{1,9},{5,13},{9,1},{13,5},{2,10},{6,14},... | collective-permute-start | bytes 1425416 | tf_op jit(solution)/shard_map/ppermute | solution.py:615
  332.8 23.1 %collective-permute-start.54 = (bf16[576,128]{1,0:T(8,128)(2,1)S(1)}, bf16[576,128]{1,0:T(8,128)(2,1)S(1)}, u32[]{:S(2)}, u32[]{:S(2)}) collective-permute-start(bf16[576,128]{1,0:T(8,128)(2,1)S(1)} %maximum_bitcast_fusion.4), channel_id=1, source_target_pairs={{0,4},{4,0},{8,12},{12,8},{1,5},{5,1},{9,13},{13,9},{2,6},{6,2},{1... | collective-permute-start | bytes 442376 | tf_op jit(solution)/shard_map/ppermute | solution.py:615
  355.7 15.0 %collective-permute-start.60 = (bf16[1856,128]{1,0:T(8,128)(2,1)S(1)}, bf16[1856,128]{1,0:T(8,128)(2,1)S(1)}, u32[]{:S(2)}, u32[]{:S(2)}) collective-permute-start(bf16[1856,128]{1,0:T(8,128)(2,1)S(1)} %add_convert_fusion.4), channel_id=1, source_target_pairs={{0,4},{4,0},{8,12},{12,8},{1,5},{5,1},{9,13},{13,9},{2,6},{6,2},{1... | collective-permute-start | bytes 1425416 | tf_op jit(solution)/shard_map/ppermute | solution.py:615
  355.9 16.5 %collective-permute-start.55 = (bf16[576,128]{1,0:T(8,128)(2,1)S(1)}, bf16[576,128]{1,0:T(8,128)(2,1)S(1)}, u32[]{:S(2)}, u32[]{:S(2)}) collective-permute-start(bf16[576,128]{1,0:T(8,128)(2,1)S(1)} %add_convert_fusion.8), channel_id=1, source_target_pairs={{0,8},{4,12},{8,0},{12,4},{1,9},{5,13},{9,1},{13,5},{2,10},{6,14},... | collective-permute-start | bytes 442376 | tf_op jit(solution)/shard_map/ppermute | solution.py:615
  372.3 8.0 %collective-permute-start.63 = (bf16[3136,128]{1,0:T(8,128)(2,1)S(1)}, bf16[3136,128]{1,0:T(8,128)(2,1)S(1)}, u32[]{:S(2)}, u32[]{:S(2)}) collective-permute-start(bf16[3136,128]{1,0:T(8,128)(2,1)S(1)} %get-tuple-element.244), channel_id=1, source_target_pairs={{0,16},{16,0},{1,17},{17,1},{2,18},{18,2},{3,19},{19,3},{4,20},{20... | collective-permute-start | bytes 2408456 | tf_op jit(solution)/shard_map/ppermute | solution.py:615
  (85 other events, 362.9 us)

commit v3 on v2

--- a/solution.py
+++ b/solution.py
@@ -19,7 +19,7 @@
 
 BF = jnp.bfloat16
 F32 = jnp.float32
-VMEM_LIMIT = 56 * 1024 * 1024
+MIB = 1024 * 1024
 
 IN_VMEM = pl.BlockSpec(memory_space=pltpu.VMEM)
 IN_SMEM = pl.BlockSpec(memory_space=pltpu.SMEM)
@@ -42,7 +42,7 @@
     return jax.ShapeDtypeStruct(dims, kind)
 
 
-def call(kernel, outs, in_specs, scratch, args, flops, after=()):
+def call(kernel, outs, in_specs, scratch, args, flops, after=(), limit=56):
     count = len(args)
     late = len(after)
     inner = kernel
@@ -59,7 +59,7 @@
         in_specs=in_specs,
         out_specs=tuple(IN_VMEM for _ in outs),
         scratch_shapes=scratch,
-        compiler_params=pltpu.CompilerParams(vmem_limit_bytes=VMEM_LIMIT),
+        compiler_params=pltpu.CompilerParams(vmem_limit_bytes=limit * MIB),
         cost_estimate=pl.CostEstimate(flops=flops // 1000, bytes_accessed=moved // 1000, transcendentals=0),
     )(*args, *after)
 
@@ -164,6 +164,7 @@
         args,
         2 * rows * depth * 1536,
         after,
+        limit=40,
     )
 
 
@@ -221,6 +222,7 @@
         (idx, q) + tuple(kv),
         2 * 2 * rows * rows * len(kv) * HQ * HD * 4,
         after,
+        limit=40,
     )
 
 
@@ -273,6 +275,7 @@
         args,
         2 * rows * depth * (3 * ff + depth),
         after,
+        limit=40,
     )
 
 
@@ -333,6 +336,7 @@
         args,
         2 * rows * depth * (3 * ff + depth),
         after,
+        limit=40,
     )
 
 
@@ -407,6 +411,7 @@
         (idx, hid, e, mn, gm, gt, attn, mix, mg),
         2 * rows * depth * (3 * ff + depth),
         after,
+        limit=40,
     )
 
 
@@ -691,11 +696,16 @@
     return value
 
 
-def ctx_begin(value, wait=()):
+def ctx_cut(value):
     me = lax.axis_index("ctx") & 1
     size = value.shape[0] // 2
     send = lax.dynamic_slice_in_dim(value, (1 - me) * size, size, 0)
     keep = lax.dynamic_slice_in_dim(value, me * size, size, 0)
+    return send, keep
+
+
+def ctx_begin(halves, wait=()):
+    send, keep = halves
     got = crossed(send, "ctx", 1)
     if wait:
         got = held(got, *wait)
@@ -817,8 +827,10 @@
 
     pack = Packing(shard, half, gate_proj.shape[2], depth)
 
-    def joined(mine, theirs):
+    def joined(mine, theirs, wait=()):
         got = other_core(theirs)
+        if wait:
+            got = held(got, *wait)
         return (mine.astype(F32) + got.astype(F32)).astype(BF)
 
     e = lax.dynamic_index_in_dim(out_grad, core, 0, keepdims=False).reshape(rows, depth)
@@ -828,11 +840,9 @@
         gm, gt, rg, mix, ag, mg = mlp_back(
             layer, parts_of_down, idx, e, resid, gate, up, *ff_w[layer], attn_w, after
         )
-        done = between(ag) if between else ()
-        first = tuple(d[0] if isinstance(d, tuple) else d for d in done)
-        mine, theirs = mlp_grads(pack, fsdp_count, idx, hid, e, mn, gm, gt, attn, mix, mg, first)
-        result = (rg, ag, joined(mine, theirs))
-        return result + (done,) if between else result
+        done = tuple(between(ag)) if between else ()
+        mine, theirs = mlp_grads(pack, fsdp_count, idx, hid, e, mn, gm, gt, attn, mix, mg, done)
+        return rg, ag, mine, theirs
 
     def attention_back(layer, ag, after):
         x, normed, q, kv, attn, lse, resid, mn, gate, up, hid = saved[layer]
@@ -846,7 +856,7 @@
             layer, pack, fsdp_count, idx, x, normed, dq, own_kv, far_kv, rg, attn_w, cos, sin, after
         )
         entry[layer] = e
-        return e, joined(mine, theirs)
+        return e, mine, theirs
 
     orders = (up_order, down_order)
 
@@ -863,37 +873,44 @@
         values = [scatter_rest(v, o, wait) for v, o in zip(values, orders)]
         return jnp.concatenate(values, axis=1)[0]
 
+    def next_cuts(values):
+        return [cut(v, o[1:], o[1]) for v, o in zip(values, orders)] if steps > 1 else [values]
+
     middle = pack.down_at
     entry_middle = pack.entry_rows // 2
-    rg, ag, m1 = feed_forward_back(1, e, (), ())
-    m1 = start(m1, middle)
-    dq, own_kv, far_kv = attention_back(1, ag, sends(m1))
-    e, a1 = entry_back(1, dq, own_kv, far_kv, rg, ())
+    rg, ag, mine, theirs = feed_forward_back(1, e, (), None)
+    dq, own_kv, far_kv = attention_back(1, ag, (mine,))
+    m1 = start(joined(mine, theirs, (dq,)), middle)
+    e, a_mine, a_theirs = entry_back(1, dq, own_kv, far_kv, rg, sends(m1))
     m1 = first_sums(m1, (e,))
 
     def between(ag):
-        return (last_sums(m1, (ag,)), *start(a1, entry_middle))
-
-    rg, ag, m0, m1 = feed_forward_back(0, e, tuple(m1), between)
-    m0 = start(m0, middle)
-    m1, a1 = m1[0], list(m1[1:])
-    m1 = ctx_begin(m1, (m0[0][0],))
-    a1 = first_sums(a1, (m0[0][0],))
-    dq, own_kv, far_kv = attention_back(0, ag, sends(m0) + tuple(a1) + (m1,))
-    a1 = last_sums(a1, (dq,))
+        m1_cut.extend(ctx_cut(last_sums(m1, (ag,))))
+        return m1_cut[:1]
+
+    m1_cut = []
+    rg, ag, mine, theirs = feed_forward_back(0, e, tuple(m1), between)
+    m0 = start(joined(mine, theirs), middle)
+    m1 = ctx_begin(m1_cut, (m0[0][0],))
+    dq, own_kv, far_kv = attention_back(0, ag, sends(m0) + (m1,))
+    a1 = start(joined(a_mine, a_theirs, (dq,)), entry_middle)
     m0 = first_sums(m0, (dq,))
     m1 = ctx_middle(m1, (far_kv[-1],))
-    e, a0 = entry_back(0, dq, own_kv, far_kv, rg, (a1, m1) + tuple(m0))
-    a0 = start(a0, entry_middle)
+    e, a_mine, a_theirs = entry_back(
+        0, dq, own_kv, far_kv, rg, sends(next_cuts(m0)) + sends(a1) + (m1,)
+    )
+    a0 = start(joined(a_mine, a_theirs), entry_middle)
     late = sends(a0)[0]
-    m0 = jnp.concatenate([last_sums(m0, (e,)), a1], axis=0)
-    m0 = ctx_begin(m0, (late,))
-    a0 = first_sums(a0, ())
-    m1 = ctx_end(m1, tuple(a0))
-    a0 = last_sums(a0, ())
-    m0 = ctx_end(ctx_middle(m0, (a0,)))
-    a0 = sum_over_ctx(a0)
-    m0, a1 = m0[: pack.rows], m0[pack.rows :]
+    m0 = ctx_cut(last_sums(m0, (late,)))
+    a1 = first_sums(a1, (m0[0],))
+    a0 = first_sums(a0, (m0[0],))
+    m0 = ctx_begin(m0, tuple(a0))
+    a1 = last_sums(a1, (m0,))
+    a0 = last_sums(a0, (m0,))
+    m1 = ctx_end(m1, (a0,))
+    a0 = sum_over_ctx(jnp.concatenate([a0, a1], axis=0))
+    m0 = ctx_end(ctx_middle(m0))
+    a0, a1 = a0[: pack.entry_rows], a0[pack.entry_rows :]
 
     def own_layer(zero, one):
         keep = pick(zero, one)

time: 394 us -> 374 us (0.949)
  Pallas kernels: 112 us -> 99.1 us
  starting transfers between devices: 70.6 us -> 65.3 us
  local copies, waits for them, and re-layouts: 30.6 us -> 34.7 us
    pallas_call x16, Pallas kernels: 112 us -> 99.1 us  [call(): pl.pallas_call(kernel, out_shape=tuple(outs), in_specs=in_specs, out_spec...]
    ppermute x52, waiting for transfers between devices: 92.1 us -> 83 us  [crossed(): return lax.ppermute(value, axis, [(i, i ^ mask) for i in range(count)])]
    ppermute x12, waiting for transfers between devices: 36.9 us -> 43.4 us  [shifted(): lax.ppermute(value, 'ctx', [(i, i + distance) for i in devices if i + dis...]
    ppermute x52, starting transfers between devices: 39.7 us -> 34.6 us  [crossed(): return lax.ppermute(value, axis, [(i, i ^ mask) for i in range(count)])]
    unnamed x142 -> x206, local copies, waits for them, and re-layouts: 20.1 us -> 21.2 us
  transfers between devices with their start and end apart: 64 -> 64, of which waited for: 27 -> 25; matrix products, arithmetic and copies ran while one was open for 12% -> 13% of each run, Pallas kernels for 20% -> 18%
where the time goes in v3:
time: 374 us; the launch traced here: 368 us
  waiting for transfers between devices  126 us (34%)
  Pallas kernels  99.1 us (26%)
  starting transfers between devices  65.3 us (17%)
  other arithmetic  40.2 us (11%)
  local copies, waits for them, and re-layouts  34.7 us (9%)
    pallas_call x16, Pallas kernels, call(): pl.pallas_call(kernel, out_shape=tuple(outs), in_specs=in_specs, out_spec...  99.1 us
    ppermute x52, waiting for transfers between devices, crossed(): return lax.ppermute(value, axis, [(i, i ^ mask) for i in range(count)])  83 us
    ppermute x12, waiting for transfers between devices, shifted(): lax.ppermute(value, 'ctx', [(i, i + distance) for i in devices if i + dis...  43.4 us
    ppermute x52, starting transfers between devices, crossed(): return lax.ppermute(value, axis, [(i, i ^ mask) for i in range(count)])  34.6 us
    ppermute x12, starting transfers between devices, shifted(): lax.ppermute(value, 'ctx', [(i, i + distance) for i in devices if i + dis...  30.7 us
    unnamed x206, local copies, waits for them, and re-layouts  21.2 us
    select_n x8, other arithmetic, pick(): return jnp.where(first, a, b)  8.33 us
    convert_element_type x4, other arithmetic, joined(): return (mine.astype(F32) + got.astype(F32)).astype(BF)  8 us
  transfers between devices with their start and end apart: 64, of which 25 were waited for; matrix products, arithmetic and copies ran while one was open for 13% of the time, Pallas kernels for 18%

profile of v3, /device:TPU:0, one launch (start us, length us, event | category | flops | bytes accessed | tf_op | source)
XLA Modules:
  0.0 368.4 jit_solution(17727398976961488925)
XLA Ops:
  2.6 3.0 collective-permute-start.4
  18.2 8.4 %collective-permute-done.5 = bf16[2,144,896]{2,1,0:T(8,128)(2,1)S(1)} collective-permute-done((bf16[2,144,896]{2,1,0:T(8,128)(2,1)S(1)}, bf16[2,144,896]{2,1,0:T(8,128)(2,1)S(1)}, u32[]{:S(2)}, u32[]{:S(2)}) %collective-permute-start.5) | collective-permute-done | bytes 516128 | tf_op jit(solution)/shard_map/ppermute | solution.py:620
  27.1 1.9 collective-permute-done.3
  29.4 2.3 broadcast_select_fusion.10
  31.6 2.0 bitcast_select_fusion
  39.5 2.8 shard_map.203
  44.6 6.7 %collective-permute-done.6 = bf16[144,1536]{1,0:T(8,128)(2,1)S(1)} collective-permute-done((bf16[144,1536]{1,0:T(8,128)(2,1)}, bf16[144,1536]{1,0:T(8,128)(2,1)S(1)}, u32[]{:S(2)}, u32[]{:S(2)}) %collective-permute-start.6) | collective-permute-done | bytes 442400 | tf_op jit(solution)/shard_map/ppermute | solution.py:620
  53.0 3.5 collective-permute-start.12
  56.5 4.5 %collective-permute-start.13 = (bf16[256,384]{1,0:T(8,128)(2,1)S(1)}, bf16[256,384]{1,0:T(8,128)(2,1)S(1)}, u32[]{:S(2)}, u32[]{:S(2)}) collective-permute-start(bf16[256,384]{1,0:T(8,128)(2,1)S(1)} %get-tuple-element.122.refs_2_.refs_4_), channel_id=1, source_target_pairs={{0,8},{4,12},{1,9},{5,13},{2,10},{6,14},{3,11},{7,15},{16,24},{20,... | collective-permute-start | bytes 589832 | tf_op jit(solution)/shard_map/ppermute | solution.py:625
  62.5 3.4 collective-permute-done.13.refs_4_.refs_6_
  65.9 2.1 collective-permute-done.14.refs_5_.refs_7_
  68.0 7.0 %shard_map.204 = (bf16[256,576]{1,0:T(8,128)(2,1)S(1)}, f32[16,256]{1,0:T(8,128)S(1)}) custom-call(s32[2]{0:T(128)S(1)} %pad_add_fusion.refs_0_, bf16[256,576]{1,0:T(8,128)(2,1)S(1)} %get-tuple-element.121.refs_1_, bf16[256,384]{1,0:T(8,128)(2,1)S(1)} %get-tuple-element.122.refs_2_.refs_4_, bf16[256,384]{1,0:T(8,128)(2,1)S(1)} %collective-permute-done.12.refs_3_.refs_5_, ...), custom_call_target="tpu_custom_call" | custom-call | flops 2415919 | bytes 1392 | tf_op jit(solution)/shard_map/pallas_call | solution.py:56
  79.1 2.1 collective-permute-done.16.refs_8_
  81.3 6.4 %shard_map.205 = (bf16[256,576]{1,0:T(8,128)(2,1)S(1)}, f32[256,576]{1,0:T(8,128)S(1)}, bf16[256,576]{1,0:T(8,128)(2,1)S(1)}, f32[256,1536]{1,0:T(8,128)S(1)}, f...) custom-call(s32[2]{0:T(128)S(1)} %pad_add_fusion.refs_0_, bf16[256,576]{1,0:T(8,128)(2,1)S(1)} %bitcast.229, ...), custom_call_target="tpu_custom_call" | custom-call | flops 1528823 | bytes 13271 | tf_op jit(solution)/shard_map/pallas_call | solution.py:56
  88.6 3.9 %shard_map.206 = (bf16[256,576]{1,0:T(8,128)(2,1)S(1)}, bf16[256,576]{1,0:T(8,128)(2,1)S(1)}, bf16[256,384]{1,0:T(8,128)(2,1)S(1)}) custom-call(s32[2]{0:T(128)S(1)} %pad_add_fusion.refs_0_, bf16[256,576]{1,0:T(8,128)(2,1)S(1)} %get-tuple-element.196.refs_1_, bf16[576,896]{1,0:T(8,128)(2,1)S(1)} %bitcast.215, ...), custom_call_target="tpu_custom_call" | custom-call | flops 452984 | bytes 5472 | tf_op jit(solution)/shard_map/pallas_call | solution.py:56
  95.4 6.4 %collective-permute-start.21 = (bf16[256,384]{1,0:T(8,128)(2,1)S(1)}, bf16[256,384]{1,0:T(8,128)(2,1)S(1)}, u32[]{:S(2)}, u32[]{:S(2)}) collective-permute-start(bf16[256,384]{1,0:T(8,128)(2,1)S(1)} %get-tuple-element.136.refs_2_.refs_4_), channel_id=1, source_target_pairs={{0,4},{4,8},{8,12},{1,5},{5,9},{9,13},{2,6},{6,10},{10,14},{3,7},{... | collective-permute-start | bytes 589832 | tf_op jit(solution)/shard_map/ppermute | solution.py:625
  101.8 5.3 %collective-permute-start.22 = (bf16[256,384]{1,0:T(8,128)(2,1)S(1)}, bf16[256,384]{1,0:T(8,128)(2,1)S(1)}, u32[]{:S(2)}, u32[]{:S(2)}) collective-permute-start(bf16[256,384]{1,0:T(8,128)(2,1)S(1)} %get-tuple-element.136.refs_2_.refs_4_), channel_id=1, source_target_pairs={{0,8},{4,12},{1,9},{5,13},{2,10},{6,14},{3,11},{7,15},{16,24},{20,... | collective-permute-start | bytes 589832 | tf_op jit(solution)/shard_map/ppermute | solution.py:625
  108.9 2.9 collective-permute-done.22.refs_4_.refs_6_
  111.8 2.1 collective-permute-done.23.refs_5_.refs_7_
  113.9 7.0 %shard_map.207 = (bf16[256,576]{1,0:T(8,128)(2,1)S(1)}, f32[16,256]{1,0:T(8,128)S(1)}) custom-call(s32[2]{0:T(128)S(1)} %pad_add_fusion.refs_0_, bf16[256,576]{1,0:T(8,128)(2,1)S(1)} %get-tuple-element.135.refs_1_, bf16[256,384]{1,0:T(8,128)(2,1)S(1)} %get-tuple-element.136.refs_2_.refs_4_, bf16[256,384]{1,0:T(8,128)(2,1)S(1)} %collective-permute-done.21.refs_3_.refs_5_, ...), custom_call_target="tpu_custom_call" | custom-call | flops 2415919 | bytes 1392 | tf_op jit(solution)/shard_map/pallas_call | solution.py:56
  123.8 1.9 copy.50
  125.6 2.5 collective-permute-done.25.refs_8_
  129.7 6.6 %shard_map.208 = (bf16[256,576]{1,0:T(8,128)(2,1)S(1)}, f32[256,576]{1,0:T(8,128)S(1)}, bf16[256,576]{1,0:T(8,128)(2,1)S(1)}, f32[256,1536]{1,0:T(8,128)S(1)}, f...) custom-call(s32[2]{0:T(128)S(1)} %copy-done.57, bf16[256,576]{1,0:T(8,128)(2,1)S(1)} %get-tuple-element.196.refs_1_, ...), custom_call_target="tpu_custom_call" | custom-call | flops 1528823 | bytes 13271 | tf_op jit(solution)/shard_map/pallas_call | solution.py:56
  136.3 8.1 %shard_map.209 = (bf16[256,1536]{1,0:T(8,128)(2,1)S(1)}, bf16[256,1536]{1,0:T(8,128)(2,1)S(1)}, f32[256,576]{1,0:T(8,128)S(1)}, bf16[256,576]{1,0:T(8,128)(2,1)S...) custom-call(s32[2]{0:T(128)S(1)} %copy-done.57, bf16[256,576]{1,0:T(8,128)(2,1)S(1)} %bitcast.230, ...), custom_call_target="tpu_custom_call" | custom-call | flops 1528823 | bytes 14499 | tf_op jit(solution)/shard_map/pallas_call | solution.py:56
  146.0 4.3 %shard_map.210 = (bf16[4,3136,128]{2,1,0:T(8,128)(2,1)S(1)}, bf16[4,3136,128]{2,1,0:T(8,128)(2,1)}) custom-call(s32[2]{0:T(128)S(1)} %copy-done.57, bf16[256,1536]{1,0:T(8,128)(2,1)S(1)} %get-tuple-element.147.refs_1_, bf16[256,576]{1,0:T(8,128)(2,1)S(1)} %bitcast.231, bf16[256,576]{1,0:T(8,128)(2,1)S(1)} %get-tuple-element.148.refs_3_, ...), custom_call_target="tpu_custom_call" | custom-call | flops 1528823 | bytes 10108 | tf_op jit(solution)/shard_map/pallas_call | solution.py:56
  152.1 11.4 %shard_map.211 = (f32[256,576]{1,0:T(8,128)}, f32[256,384]{1,0:T(8,128)}, bf16[256,384]{1,0:T(8,128)(2,1)}, bf16[256,384]{1,0:T(8,128)(2,1)}, bf16[256,384]{1,0:T(8,128)(2,1)}) custom-call(s32[2]{0:T(128)} %copy-done.56, bf16[256,576]{1,0:T(8,128)(2,1)} %copy-done.29, bf16[256,576]{1,0:T(8,128)(2,1)} %copy-done.53, f32[16,256]{1,0:T(8,128)} %copy-done.60, ...), custom_call_target="tpu_custom_call" | custom-call | flops 6039797 | bytes 2965 | tf_op jit(solution)/shard_map/pallas_call | solution.py:56
  165.3 2.7 add_convert_fusion.1
  178.4 4.7 %collective-permute-done.26.refs_5_ = bf16[256,384]{1,0:T(8,128)(2,1)S(1)} collective-permute-done((bf16[256,384]{1,0:T(8,128)(2,1)}, bf16[256,384]{1,0:T(8,128)(2,1)S(1)}, u32[]{:S(2)}, u32[]{:S(2)}) %collective-permute-start.26) | collective-permute-done | bytes 196640 | tf_op jit(solution)/shard_map/ppermute | solution.py:625
  183.2 13.9 %collective-permute-done.27.refs_6_ = bf16[256,384]{1,0:T(8,128)(2,1)} collective-permute-done((bf16[256,384]{1,0:T(8,128)(2,1)}, bf16[256,384]{1,0:T(8,128)(2,1)}, u32[]{:S(2)}, u32[]{:S(2)}) %collective-permute-start.27) | collective-permute-done | bytes 196640 | tf_op jit(solution)/shard_map/ppermute | solution.py:625
  197.1 6.8 %shard_map.212 = (bf16[256,576]{1,0:T(8,128)(2,1)}, bf16[4,576,128]{2,1,0:T(8,128)(2,1)}, bf16[4,576,128]{2,1,0:T(8,128)(2,1)}) custom-call(s32[2]{0:T(128)} %copy-done.56, bf16[256,576]{1,0:T(8,128)(2,1)} %copy-done.11, bf16[256,576]{1,0:T(8,128)(2,1)} %copy-done.52, f32[256,576]{1,0:T(8,128)} %get-tuple-element.154.refs_3_, ...), custom_call_target="tpu_custom_call" | custom-call | flops 905969 | bytes 8617 | tf_op jit(solution)/shard_map/pallas_call | solution.py:56
  208.6 8.1 %shard_map.213 = (bf16[256,1536]{1,0:T(8,128)(2,1)S(1)}, bf16[256,1536]{1,0:T(8,128)(2,1)S(1)}, f32[256,576]{1,0:T(8,128)S(1)}, bf16[256,576]{1,0:T(8,128)(2,1)S...) custom-call(s32[2]{0:T(128)S(1)} %copy-done.58, bf16[256,576]{1,0:T(8,128)(2,1)S(1)} %copy-done.14, ...), custom_call_target="tpu_custom_call" | custom-call | flops 1528823 | bytes 14499 | tf_op jit(solution)/shard_map/pallas_call | solution.py:56
  216.9 2.0 collective-permute-done.32
  220.4 4.3 %shard_map.214 = (bf16[4,3136,128]{2,1,0:T(8,128)(2,1)S(1)}, bf16[4,3136,128]{2,1,0:T(8,128)(2,1)}) custom-call(s32[2]{0:T(128)S(1)} %copy-done.58, bf16[256,1536]{1,0:T(8,128)(2,1)S(1)} %copy-done.41, bf16[256,576]{1,0:T(8,128)(2,1)S(1)} %copy-done.14, bf16[256,576]{1,0:T(8,128)(2,1)S(1)} %copy-done.51, bf16[256,1536]{1,0:T(8,128)(2,1)S(1)} %get-tuple-element.172.refs_4_, ...), custom_call_target="tpu_custom_call" | custom-call | flops 1528823 | bytes 10108 | tf_op jit(solution)/shard_map/pallas_call | solution.py:56
  226.8 6.4 %collective-permute-done.34 = bf16[4,3136,128]{2,1,0:T(8,128)(2,1)} collective-permute-done((bf16[4,3136,128]{2,1,0:T(8,128)(2,1)}, bf16[4,3136,128]{2,1,0:T(8,128)(2,1)}, u32[]{:S(2)}, u32[]{:S(2)}) %collective-permute-start.34) | collective-permute-done | bytes 3211296 | tf_op jit(solution)/shard_map/ppermute | solution.py:620
  233.3 3.7 %add_convert_fusion = bf16[4,3136,128]{2,1,0:T(8,128)(2,1)S(1)} fusion(bf16[4,3136,128]{2,1,0:T(8,128)(2,1)} %collective-permute-done.34, bf16[4,3136,128]{2,1,0:T(8,128)(2,1)} %copy-done.21), kind=kLoop, calls=%fused_computation | loop fusion | flops 6422528 | bytes 9633792 | tf_op jit(solution)/shard_map/convert_element_type | solution.py:834
  241.6 11.1 %shard_map.215 = (f32[256,576]{1,0:T(8,128)}, f32[256,384]{1,0:T(8,128)}, bf16[256,384]{1,0:T(8,128)(2,1)}, bf16[256,384]{1,0:T(8,128)(2,1)}, bf16[256,384]{1,0:T(8,128)(2,1)}) custom-call(s32[2]{0:T(128)} %copy-done.56, bf16[256,576]{1,0:T(8,128)(2,1)} %copy-done.35, bf16[256,576]{1,0:T(8,128)(2,1)} %copy-done.54, f32[16,256]{1,0:T(8,128)} %copy-done.59, ...), custom_call_target="tpu_custom_call" | custom-call | flops 6039797 | bytes 2965 | tf_op jit(solution)/shard_map/pallas_call | solution.py:56
  257.0 7.6 %collective-permute-done.38.refs_7_ = bf16[256,384]{1,0:T(8,128)(2,1)S(1)} collective-permute-done((bf16[256,384]{1,0:T(8,128)(2,1)}, bf16[256,384]{1,0:T(8,128)(2,1)S(1)}, u32[]{:S(2)}, u32[]{:S(2)}) %collective-permute-start.38) | collective-permute-done | bytes 196640 | tf_op jit(solution)/shard_map/ppermute | solution.py:625
  269.9 6.6 %collective-permute-done.37.refs_6_ = bf16[256,384]{1,0:T(8,128)(2,1)S(1)} collective-permute-done((bf16[256,384]{1,0:T(8,128)(2,1)S(1)}, bf16[256,384]{1,0:T(8,128)(2,1)S(1)}, u32[]{:S(2)}, u32[]{:S(2)}) %collective-permute-start.37) | collective-permute-done | bytes 196640 | tf_op jit(solution)/shard_map/ppermute | solution.py:625
  277.2 5.9 %shard_map.216 = (bf16[256,576]{1,0:T(8,128)(2,1)}, bf16[4,576,128]{2,1,0:T(8,128)(2,1)}, bf16[4,576,128]{2,1,0:T(8,128)(2,1)}) custom-call(s32[2]{0:T(128)} %copy-done.56, bf16[256,576]{1,0:T(8,128)(2,1)} %bitcast.228, bf16[256,576]{1,0:T(8,128)(2,1)} %copy-done.55, f32[256,576]{1,0:T(8,128)} %get-tuple-element.181.refs_3_, ...), custom_call_target="tpu_custom_call" | custom-call | flops 905969 | bytes 8617 | tf_op jit(solution)/shard_map/pallas_call | solution.py:56
  288.9 8.5 %collective-permute-done.48 = bf16[1,1408,128]{2,1,0:T(8,128)(2,1)S(1)} collective-permute-done((bf16[1,1408,128]{2,1,0:T(8,128)(2,1)S(1)}, bf16[1,1408,128]{2,1,0:T(8,128)(2,1)S(1)}, u32[]{:S(2)}, u32[]{:S(2)}) %collective-permute-start.48) | collective-permute-done | bytes 360480 | tf_op jit(solution)/shard_map/ppermute | solution.py:620
  304.4 2.1 collective-permute-done.51
  309.3 3.6 collective-permute-done.50
  314.9 2.4 collective-permute-done.52
  317.9 15.3 %collective-permute-done.60 = bf16[1568,128]{1,0:T(8,128)(2,1)S(1)} collective-permute-done((bf16[1568,128]{1,0:T(8,128)(2,1)S(1)}, bf16[1568,128]{1,0:T(8,128)(2,1)S(1)}, u32[]{:S(2)}, u32[]{:S(2)}) %collective-permute-start.60) | collective-permute-done | bytes 401440 | tf_op jit(solution)/shard_map/ppermute | solution.py:620
  334.3 16.5 %collective-permute-done.61 = bf16[1568,128]{1,0:T(8,128)(2,1)S(1)} collective-permute-done((bf16[1568,128]{1,0:T(8,128)(2,1)S(1)}, bf16[1568,128]{1,0:T(8,128)(2,1)S(1)}, u32[]{:S(2)}, u32[]{:S(2)}) %collective-permute-start.61) | collective-permute-done | bytes 401440 | tf_op jit(solution)/shard_map/ppermute | solution.py:620
  356.8 2.0 shard_map.217
  361.4 3.6 shard_map.218
  365.0 2.5 copy.57
  (412 shorter events, 106.9 us)
Async XLA Ops:
  2.6 10.0 %collective-permute-start.4 = (bf16[144,896]{1,0:T(8,128)(2,1)S(1)}, bf16[144,896]{1,0:T(8,128)(2,1)S(1)}, u32[]{:S(2)}, u32[]{:S(2)}) collective-permute-start(bf16[144,896]{1,0:T(8,128)(2,1)S(1)} %pad_maximum_fusion.16), channel_id=1, source_target_pairs={{0,2},{1,3},{2,0},{3,1},{4,6},{5,7},{6,4},{7,5},{8,10},{9,11},{10,... | collective-permute-start | bytes 774152 | tf_op jit(solution)/shard_map/ppermute | solution.py:620
  11.2 18.1 %collective-permute-start.1 = (bf16[192,640]{1,0:T(8,128)(2,1)}, bf16[192,640]{1,0:T(8,128)(2,1)}, u32[]{:S(2)}, u32[]{:S(2)}) collective-permute-start(bf16[192,640]{1,0:T(8,128)(2,1)} %broadcast_select_fusion.12), channel_id=1, source_target_pairs={{0,16},{16,0},{1,17},{17,1},{2,18},{18,2},{3,19},{19,3},{4,20},{20... | collective-permute-start | bytes 737288 | tf_op jit(solution)/shard_map/ppermute | solution.py:620
  12.1 19.6 %collective-permute-start = (bf16[144,1536]{1,0:T(8,128)(2,1)}, bf16[144,1536]{1,0:T(8,128)(2,1)}, u32[]{:S(2)}, u32[]{:S(2)}) collective-permute-start(bf16[144,1536]{1,0:T(8,128)(2,1)} %select_bitcast_fusion.16), channel_id=1, source_target_pairs={{0,16},{16,0},{1,17},{17,1},{2,18},{18,2},{3,19},{19,3},{4,20},{20... | collective-permute-start | bytes 1327112 | tf_op jit(solution)/shard_map/ppermute | solution.py:620
  12.9 13.7 %collective-permute-start.5 = (bf16[2,144,896]{2,1,0:T(8,128)(2,1)S(1)}, bf16[2,144,896]{2,1,0:T(8,128)(2,1)S(1)}, u32[]{:S(2)}, u32[]{:S(2)}) collective-permute-start(bf16[2,144,896]{2,1,0:T(8,128)(2,1)S(1)} %pad_maximum_fusion.11), channel_id=1, source_target_pairs={{0,1},{1,0},{2,3},{3,2},{4,5},{5,4},{6,7},{7,6},{8,9},{9,8},{10,11... | collective-permute-start | bytes 1548296 | tf_op jit(solution)/shard_map/ppermute | solution.py:620
  16.6 12.4 %collective-permute-start.3 = (bf16[2,144,896]{2,1,0:T(8,128)(2,1)S(1)}, bf16[2,144,896]{2,1,0:T(8,128)(2,1)S(1)}, u32[]{:S(2)}, u32[]{:S(2)}) collective-permute-start(bf16[2,144,896]{2,1,0:T(8,128)(2,1)S(1)} %pad_maximum_fusion.10), channel_id=1, source_target_pairs={{0,2},{1,3},{2,0},{3,1},{4,6},{5,7},{6,4},{7,5},{8,10},{9,11},{10,... | collective-permute-start | bytes 1548296 | tf_op jit(solution)/shard_map/ppermute | solution.py:620
  27.0 12.5 %collective-permute-start.8 = (bf16[576,896]{1,0:T(8,128)(2,1)S(1)}, bf16[576,896]{1,0:T(8,128)(2,1)S(1)}, u32[]{:S(2)}, u32[]{:S(2)}) collective-permute-start(bf16[576,896]{1,0:T(8,128)(2,1)S(1)} %bitcast.204), channel_id=1, source_target_pairs={{0,16},{16,0},{1,17},{17,1},{2,18},{18,2},{3,19},{19,3},{4,20},{20... | collective-permute-start | bytes 3096584 | tf_op jit(solution)/shard_map/ppermute | solution.py:620
  29.3 10.3 %collective-permute-start.7 = (bf16[576,896]{1,0:T(8,128)(2,1)S(1)}, bf16[576,896]{1,0:T(8,128)(2,1)}, u32[]{:S(2)}, u32[]{:S(2)}) collective-permute-start(bf16[576,896]{1,0:T(8,128)(2,1)S(1)} %bitcast.213), channel_id=1, source_target_pairs={{0,16},{16,0},{1,17},{17,1},{2,18},{18,2},{3,19},{19,3},{4,20},{20... | collective-permute-start | bytes 3096584 | tf_op jit(solution)/shard_map/ppermute | solution.py:620
  33.6 8.7 %collective-permute-start.10 = (bf16[192,640]{1,0:T(8,128)(2,1)}, bf16[192,640]{1,0:T(8,128)(2,1)}, u32[]{:S(2)}, u32[]{:S(2)}) collective-permute-start(bf16[192,640]{1,0:T(8,128)(2,1)} %get-tuple-element.119), channel_id=1, source_target_pairs={{0,2},{1,3},{2,0},{3,1},{4,6},{5,7},{6,4},{7,5},{8,10},{9,11},{10,... | collective-permute-start | bytes 737288 | tf_op jit(solution)/shard_map/ppermute | solution.py:620
  38.0 13.3 %collective-permute-start.6 = (bf16[144,1536]{1,0:T(8,128)(2,1)}, bf16[144,1536]{1,0:T(8,128)(2,1)S(1)}, u32[]{:S(2)}, u32[]{:S(2)}) collective-permute-start(bf16[144,1536]{1,0:T(8,128)(2,1)} %get-tuple-element.116), channel_id=1, source_target_pairs={{0,1},{1,0},{2,3},{3,2},{4,5},{5,4},{6,7},{7,6},{8,9},{9,8},{10,11... | collective-permute-start | bytes 1327112 | tf_op jit(solution)/shard_map/ppermute | solution.py:620
  43.8 31.2 %collective-permute-start.11 = (bf16[2,192,640]{2,1,0:T(8,128)(2,1)S(1)}, bf16[2,192,640]{2,1,0:T(8,128)(2,1)S(1)}, u32[]{:S(2)}, u32[]{:S(2)}) collective-permute-start(bf16[2,192,640]{2,1,0:T(8,128)(2,1)S(1)} %pad_maximum_fusion.12), channel_id=1, source_target_pairs={{0,1},{1,0},{2,3},{3,2},{4,5},{5,4},{6,7},{7,6},{8,9},{9,8},{10,11... | collective-permute-start | bytes 1474568 | tf_op jit(solution)/shard_map/ppermute | solution.py:620
  51.5 24.3 %collective-permute-start.9 = (bf16[2,144,1536]{2,1,0:T(8,128)(2,1)S(1)}, bf16[2,144,1536]{2,1,0:T(8,128)(2,1)S(1)}, u32[]{:S(2)}, u32[]{:S(2)}) collective-permute-start(bf16[2,144,1536]{2,1,0:T(8,128)(2,1)S(1)} %pad_maximum_fusion.6), channel_id=1, source_target_pairs={{0,2},{1,3},{2,0},{3,1},{4,6},{5,7},{6,4},{7,5},{8,10},{9,11},{10,... | collective-permute-start | bytes 2654216 | tf_op jit(solution)/shard_map/ppermute | solution.py:620
  53.0 9.5 %collective-permute-start.12 = (bf16[256,384]{1,0:T(8,128)(2,1)S(1)}, bf16[256,384]{1,0:T(8,128)(2,1)S(1)}, u32[]{:S(2)}, u32[]{:S(2)}) collective-permute-start(bf16[256,384]{1,0:T(8,128)(2,1)S(1)} %get-tuple-element.122.refs_2_.refs_4_), channel_id=1, source_target_pairs={{0,4},{4,8},{8,12},{1,5},{5,9},{9,13},{2,6},{6,10},{10,14},{3,7},{... | collective-permute-start | bytes 589832 | tf_op jit(solution)/shard_map/ppermute | solution.py:625
  56.5 9.5 %collective-permute-start.13 = (bf16[256,384]{1,0:T(8,128)(2,1)S(1)}, bf16[256,384]{1,0:T(8,128)(2,1)S(1)}, u32[]{:S(2)}, u32[]{:S(2)}) collective-permute-start(bf16[256,384]{1,0:T(8,128)(2,1)S(1)} %get-tuple-element.122.refs_2_.refs_4_), channel_id=1, source_target_pairs={{0,8},{4,12},{1,9},{5,13},{2,10},{6,14},{3,11},{7,15},{16,24},{20,... | collective-permute-start | bytes 589832 | tf_op jit(solution)/shard_map/ppermute | solution.py:625
  77.1 15.4 %collective-permute-start.18 = (bf16[192,640]{1,0:T(8,128)(2,1)S(1)}, bf16[192,640]{1,0:T(8,128)(2,1)S(1)}, u32[]{:S(2)}, u32[]{:S(2)}) collective-permute-start(bf16[192,640]{1,0:T(8,128)(2,1)S(1)} %copy-done.83), channel_id=1, source_target_pairs={{0,1},{1,0},{2,3},{3,2},{4,5},{5,4},{6,7},{7,6},{8,9},{9,8},{10,11... | collective-permute-start | bytes 737288 | tf_op jit(solution)/shard_map/ppermute | solution.py:620
  78.6 14.0 %collective-permute-start.17 = (bf16[144,1536]{1,0:T(8,128)(2,1)S(1)}, bf16[144,1536]{1,0:T(8,128)(2,1)S(1)}, u32[]{:S(2)}, u32[]{:S(2)}) collective-permute-start(bf16[144,1536]{1,0:T(8,128)(2,1)S(1)} %copy-done.76), channel_id=1, source_target_pairs={{0,2},{1,3},{2,0},{3,1},{4,6},{5,7},{6,4},{7,5},{8,10},{9,11},{10,... | collective-permute-start | bytes 1327112 | tf_op jit(solution)/shard_map/ppermute | solution.py:620
  93.4 27.6 %collective-permute-start.20 = (bf16[2,192,640]{2,1,0:T(8,128)(2,1)S(1)}, bf16[2,192,640]{2,1,0:T(8,128)(2,1)S(1)}, u32[]{:S(2)}, u32[]{:S(2)}) collective-permute-start(bf16[2,192,640]{2,1,0:T(8,128)(2,1)S(1)} %pad_maximum_fusion.13), channel_id=1, source_target_pairs={{0,2},{1,3},{2,0},{3,1},{4,6},{5,7},{6,4},{7,5},{8,10},{9,11},{10,... | collective-permute-start | bytes 1474568 | tf_op jit(solution)/shard_map/ppermute | solution.py:620
  93.9 27.7 %collective-permute-start.19 = (bf16[2,144,1536]{2,1,0:T(8,128)(2,1)S(1)}, bf16[2,144,1536]{2,1,0:T(8,128)(2,1)S(1)}, u32[]{:S(2)}, u32[]{:S(2)}) collective-permute-start(bf16[2,144,1536]{2,1,0:T(8,128)(2,1)S(1)} %pad_maximum_fusion.7), channel_id=1, source_target_pairs={{0,1},{1,0},{2,3},{3,2},{4,5},{5,4},{6,7},{7,6},{8,9},{9,8},{10,11... | collective-permute-start | bytes 2654216 | tf_op jit(solution)/shard_map/ppermute | solution.py:620
  95.4 13.4 %collective-permute-start.21 = (bf16[256,384]{1,0:T(8,128)(2,1)S(1)}, bf16[256,384]{1,0:T(8,128)(2,1)S(1)}, u32[]{:S(2)}, u32[]{:S(2)}) collective-permute-start(bf16[256,384]{1,0:T(8,128)(2,1)S(1)} %get-tuple-element.136.refs_2_.refs_4_), channel_id=1, source_target_pairs={{0,4},{4,8},{8,12},{1,5},{5,9},{9,13},{2,6},{6,10},{10,14},{3,7},{... | collective-permute-start | bytes 589832 | tf_op jit(solution)/shard_map/ppermute | solution.py:625
  101.8 10.0 %collective-permute-start.22 = (bf16[256,384]{1,0:T(8,128)(2,1)S(1)}, bf16[256,384]{1,0:T(8,128)(2,1)S(1)}, u32[]{:S(2)}, u32[]{:S(2)}) collective-permute-start(bf16[256,384]{1,0:T(8,128)(2,1)S(1)} %get-tuple-element.136.refs_2_.refs_4_), channel_id=1, source_target_pairs={{0,8},{4,12},{1,9},{5,13},{2,10},{6,14},{3,11},{7,15},{16,24},{20,... | collective-permute-start | bytes 589832 | tf_op jit(solution)/shard_map/ppermute | solution.py:625
  152.0 11.6 %collective-permute-start.29 = (bf16[4,3136,128]{2,1,0:T(8,128)(2,1)}, bf16[4,3136,128]{2,1,0:T(8,128)(2,1)S(1)}, u32[]{:S(2)}, u32[]{:S(2)}) collective-permute-start(bf16[4,3136,128]{2,1,0:T(8,128)(2,1)} %get-tuple-element.160), channel_id=1, source_target_pairs={{0,16},{16,0},{1,17},{17,1},{2,18},{18,2},{3,19},{19,3},{4,20},{20... | collective-permute-start | bytes 9633800 | tf_op jit(solution)/shard_map/ppermute | solution.py:620
  170.2 33.8 %collective-permute-start.31 = (bf16[2,1,1408,128]{3,2,1,0:T(8,128)(2,1)}, bf16[2,1,1408,128]{3,2,1,0:T(8,128)(2,1)}, u32[]{:S(2)}, u32[]{:S(2)}) collective-permute-start(bf16[2,1,1408,128]{3,2,1,0:T(8,128)(2,1)} %dynamic-slice_bitcast_fusion.3.refs_16_), channel_id=1, source_target_pairs={{0,2},{1,3},{2,0},{3,1},{4,6},{5,7},{6,4},{7,5},{8,10},{9,11},{10,... | collective-permute-start | bytes 2162696 | tf_op jit(solution)/shard_map/ppermute | solution.py:620
  171.7 11.4 %collective-permute-start.26 = (bf16[256,384]{1,0:T(8,128)(2,1)}, bf16[256,384]{1,0:T(8,128)(2,1)S(1)}, u32[]{:S(2)}, u32[]{:S(2)}) collective-permute-start(bf16[256,384]{1,0:T(8,128)(2,1)} %get-tuple-element.156), channel_id=1, source_target_pairs={{4,0},{8,4},{12,8},{5,1},{9,5},{13,9},{6,2},{10,6},{14,10},{7,3},{... | collective-permute-start | bytes 589832 | tf_op jit(solution)/shard_map/ppermute | solution.py:625
  173.0 24.1 %collective-permute-start.27 = (bf16[256,384]{1,0:T(8,128)(2,1)}, bf16[256,384]{1,0:T(8,128)(2,1)}, u32[]{:S(2)}, u32[]{:S(2)}) collective-permute-start(bf16[256,384]{1,0:T(8,128)(2,1)} %get-tuple-element.157), channel_id=1, source_target_pairs={{8,0},{12,4},{9,1},{13,5},{10,2},{14,6},{11,3},{15,7},{24,16},{28,... | collective-permute-start | bytes 589832 | tf_op jit(solution)/shard_map/ppermute | solution.py:625
  174.3 22.8 %collective-permute-start.28 = (bf16[256,384]{1,0:T(8,128)(2,1)}, bf16[256,384]{1,0:T(8,128)(2,1)}, u32[]{:S(2)}, u32[]{:S(2)}) collective-permute-start(bf16[256,384]{1,0:T(8,128)(2,1)} %get-tuple-element.158), channel_id=1, source_target_pairs={{12,0},{13,1},{14,2},{15,3},{28,16},{29,17},{30,18},{31,19}} | collective-permute-start | bytes 589832 | tf_op jit(solution)/shard_map/ppermute | solution.py:625
  177.9 28.2 %collective-permute-start.30 = (bf16[2,1,1728,128]{3,2,1,0:T(8,128)(2,1)}, bf16[2,1,1728,128]{3,2,1,0:T(8,128)(2,1)}, u32[]{:S(2)}, u32[]{:S(2)}) collective-permute-start(bf16[2,1,1728,128]{3,2,1,0:T(8,128)(2,1)} %dynamic-slice_bitcast_fusion.1.refs_15_), channel_id=1, source_target_pairs={{0,1},{1,0},{2,3},{3,2},{4,5},{5,4},{6,7},{7,6},{8,9},{9,8},{10,11... | collective-permute-start | bytes 2654216 | tf_op jit(solution)/shard_map/ppermute | solution.py:620
  205.6 11.2 %collective-permute-start.33 = (bf16[1,1408,128]{2,1,0:T(8,128)(2,1)S(1)}, bf16[1,1408,128]{2,1,0:T(8,128)(2,1)S(1)}, u32[]{:S(2)}, u32[]{:S(2)}) collective-permute-start(bf16[1,1408,128]{2,1,0:T(8,128)(2,1)S(1)} %dynamic-slice_bitcast_fusion.7), channel_id=1, source_target_pairs={{0,1},{1,0},{2,3},{3,2},{4,5},{5,4},{6,7},{7,6},{8,9},{9,8},{10,11... | collective-permute-start | bytes 1081352 | tf_op jit(solution)/shard_map/ppermute | solution.py:620
  207.9 11.0 %collective-permute-start.32 = (bf16[1,1728,128]{2,1,0:T(8,128)(2,1)S(1)}, bf16[1,1728,128]{2,1,0:T(8,128)(2,1)S(1)}, u32[]{:S(2)}, u32[]{:S(2)}) collective-permute-start(bf16[1,1728,128]{2,1,0:T(8,128)(2,1)S(1)} %dynamic-slice_bitcast_fusion.5), channel_id=1, source_target_pairs={{0,2},{1,3},{2,0},{3,1},{4,6},{5,7},{6,4},{7,5},{8,10},{9,11},{10,... | collective-permute-start | bytes 1327112 | tf_op jit(solution)/shard_map/ppermute | solution.py:620
  226.3 27.7 %collective-permute-start.41 = (bf16[4,576,128]{2,1,0:T(8,128)(2,1)}, bf16[4,576,128]{2,1,0:T(8,128)(2,1)S(1)}, u32[]{:S(2)}, u32[]{:S(2)}) collective-permute-start(bf16[4,576,128]{2,1,0:T(8,128)(2,1)} %get-tuple-element.190), channel_id=1, source_target_pairs={{0,16},{16,0},{1,17},{17,1},{2,18},{18,2},{3,19},{19,3},{4,20},{20... | collective-permute-start | bytes 1769480 | tf_op jit(solution)/shard_map/ppermute | solution.py:620
  226.8 11.8 %collective-permute-start.35 = (bf16[1568,128]{1,0:T(8,128)(2,1)S(1)}, bf16[1568,128]{1,0:T(8,128)(2,1)S(1)}, u32[]{:S(2)}, u32[]{:S(2)}) collective-permute-start(bf16[1568,128]{1,0:T(8,128)(2,1)S(1)} %fusion.17.refs_9_), channel_id=1, source_target_pairs={{0,4},{4,0},{8,12},{12,8},{1,5},{5,1},{9,13},{13,9},{2,6},{6,2},{1... | collective-permute-start | bytes 1204232 | tf_op jit(solution)/shard_map/ppermute | solution.py:620
  237.3 30.4 %collective-permute-start.39 = (bf16[2,1,1728,128]{3,2,1,0:T(8,128)(2,1)S(1)}, bf16[2,1,1728,128]{3,2,1,0:T(8,128)(2,1)}, u32[]{:S(2)}, u32[]{:S(2)}) collective-permute-start(bf16[2,1,1728,128]{3,2,1,0:T(8,128)(2,1)S(1)} %dynamic-slice_bitcast_fusion.refs_8_), channel_id=1, source_target_pairs={{0,1},{1,0},{2,3},{3,2},{4,5},{5,4},{6,7},{7,6},{8,9},{9,8},{10,11... | collective-permute-start | bytes 2654216 | tf_op jit(solution)/shard_map/ppermute | solution.py:620
  240.0 25.8 %collective-permute-start.42 = (bf16[1568,128]{1,0:T(8,128)(2,1)S(1)}, bf16[1568,128]{1,0:T(8,128)(2,1)S(1)}, u32[]{:S(2)}, u32[]{:S(2)}) collective-permute-start(bf16[1568,128]{1,0:T(8,128)(2,1)S(1)} %fusion.7.refs_10_), channel_id=1, source_target_pairs={{0,8},{4,12},{8,0},{12,4},{1,9},{5,13},{9,1},{13,5},{2,10},{6,14},... | collective-permute-start | bytes 1204232 | tf_op jit(solution)/shard_map/ppermute | solution.py:620
  240.7 26.0 %collective-permute-start.40 = (bf16[2,1,1408,128]{3,2,1,0:T(8,128)(2,1)S(1)}, bf16[2,1,1408,128]{3,2,1,0:T(8,128)(2,1)S(1)}, u32[]{:S(2)}, u32[]{:S(2)}) collective-permute-start(bf16[2,1,1408,128]{3,2,1,0:T(8,128)(2,1)S(1)} %dynamic-slice_bitcast_fusion.2.refs_9_), channel_id=1, source_target_pairs={{0,2},{1,3},{2,0},{3,1},{4,6},{5,7},{6,4},{7,5},{8,10},{9,11},{10,... | collective-permute-start | bytes 2162696 | tf_op jit(solution)/shard_map/ppermute | solution.py:620
  252.6 11.9 %collective-permute-start.38 = (bf16[256,384]{1,0:T(8,128)(2,1)}, bf16[256,384]{1,0:T(8,128)(2,1)S(1)}, u32[]{:S(2)}, u32[]{:S(2)}) collective-permute-start(bf16[256,384]{1,0:T(8,128)(2,1)} %get-tuple-element.185), channel_id=1, source_target_pairs={{12,0},{13,1},{14,2},{15,3},{28,16},{29,17},{30,18},{31,19}} | collective-permute-start | bytes 589832 | tf_op jit(solution)/shard_map/ppermute | solution.py:625
  254.3 15.6 %collective-permute-start.36 = (bf16[256,384]{1,0:T(8,128)(2,1)S(1)}, bf16[256,384]{1,0:T(8,128)(2,1)S(1)}, u32[]{:S(2)}, u32[]{:S(2)}) collective-permute-start(bf16[256,384]{1,0:T(8,128)(2,1)S(1)} %copy-done.100), channel_id=1, source_target_pairs={{4,0},{8,4},{12,8},{5,1},{9,5},{13,9},{6,2},{10,6},{14,10},{7,3},{... | collective-permute-start | bytes 589832 | tf_op jit(solution)/shard_map/ppermute | solution.py:625
  264.5 11.9 %collective-permute-start.37 = (bf16[256,384]{1,0:T(8,128)(2,1)S(1)}, bf16[256,384]{1,0:T(8,128)(2,1)S(1)}, u32[]{:S(2)}, u32[]{:S(2)}) collective-permute-start(bf16[256,384]{1,0:T(8,128)(2,1)S(1)} %copy-done.99), channel_id=1, source_target_pairs={{8,0},{12,4},{9,1},{13,5},{10,2},{14,6},{11,3},{15,7},{24,16},{28,... | collective-permute-start | bytes 589832 | tf_op jit(solution)/shard_map/ppermute | solution.py:625
  283.2 19.4 %collective-permute-start.53 = (bf16[2,1,288,128]{3,2,1,0:T(8,128)(2,1)}, bf16[2,1,288,128]{3,2,1,0:T(8,128)(2,1)S(1)}, u32[]{:S(2)}, u32[]{:S(2)}) collective-permute-start(bf16[2,1,288,128]{3,2,1,0:T(8,128)(2,1)} %dynamic-slice_bitcast_fusion.11.refs_17_), channel_id=1, source_target_pairs={{0,1},{1,0},{2,3},{3,2},{4,5},{5,4},{6,7},{7,6},{8,9},{9,8},{10,11... | collective-permute-start | bytes 442376 | tf_op jit(solution)/shard_map/ppermute | solution.py:620
  284.8 18.0 %collective-permute-start.55 = (bf16[2,1,288,128]{3,2,1,0:T(8,128)(2,1)}, bf16[2,1,288,128]{3,2,1,0:T(8,128)(2,1)S(1)}, u32[]{:S(2)}, u32[]{:S(2)}) collective-permute-start(bf16[2,1,288,128]{3,2,1,0:T(8,128)(2,1)} %dynamic-slice_bitcast_fusion.10.refs_18_), channel_id=1, source_target_pairs={{0,2},{1,3},{2,0},{3,1},{4,6},{5,7},{6,4},{7,5},{8,10},{9,11},{10,... | collective-permute-start | bytes 442376 | tf_op jit(solution)/shard_map/ppermute | solution.py:620
  285.4 31.9 %collective-permute-start.62 = (bf16[1568,128]{1,0:T(8,128)(2,1)S(1)}, bf16[1568,128]{1,0:T(8,128)(2,1)S(1)}, u32[]{:S(2)}, u32[]{:S(2)}) collective-permute-start(bf16[1568,128]{1,0:T(8,128)(2,1)S(1)} %copy-done.69), channel_id=1, source_target_pairs={{0,4},{4,0},{8,12},{12,8},{1,5},{5,1},{9,13},{13,9},{2,6},{6,2},{1... | collective-permute-start | bytes 1204232 | tf_op jit(solution)/shard_map/ppermute | solution.py:620
  285.4 12.0 %collective-permute-start.48 = (bf16[1,1408,128]{2,1,0:T(8,128)(2,1)S(1)}, bf16[1,1408,128]{2,1,0:T(8,128)(2,1)S(1)}, u32[]{:S(2)}, u32[]{:S(2)}) collective-permute-start(bf16[1,1408,128]{2,1,0:T(8,128)(2,1)S(1)} %copy-done.79), channel_id=1, source_target_pairs={{0,1},{1,0},{2,3},{3,2},{4,5},{5,4},{6,7},{7,6},{8,9},{9,8},{10,11... | collective-permute-start | bytes 1081352 | tf_op jit(solution)/shard_map/ppermute | solution.py:620
  286.0 14.4 %collective-permute-start.47 = (bf16[1,1728,128]{2,1,0:T(8,128)(2,1)S(1)}, bf16[1,1728,128]{2,1,0:T(8,128)(2,1)S(1)}, u32[]{:S(2)}, u32[]{:S(2)}) collective-permute-start(bf16[1,1728,128]{2,1,0:T(8,128)(2,1)S(1)} %copy-done.78), channel_id=1, source_target_pairs={{0,2},{1,3},{2,0},{3,1},{4,6},{5,7},{6,4},{7,5},{8,10},{9,11},{10,... | collective-permute-start | bytes 1327112 | tf_op jit(solution)/shard_map/ppermute | solution.py:620
  297.4 9.2 %collective-permute-start.46 = (bf16[2,1,288,128]{3,2,1,0:T(8,128)(2,1)S(1)}, bf16[2,1,288,128]{3,2,1,0:T(8,128)(2,1)S(1)}, u32[]{:S(2)}, u32[]{:S(2)}) collective-permute-start(bf16[2,1,288,128]{3,2,1,0:T(8,128)(2,1)S(1)} %dynamic-slice_bitcast_fusion.9), channel_id=1, source_target_pairs={{0,1},{1,0},{2,3},{3,2},{4,5},{5,4},{6,7},{7,6},{8,9},{9,8},{10,11... | collective-permute-start | bytes 442376 | tf_op jit(solution)/shard_map/ppermute | solution.py:620
  302.6 10.3 %collective-permute-start.50 = (bf16[1568,128]{1,0:T(8,128)(2,1)S(1)}, bf16[1568,128]{1,0:T(8,128)(2,1)S(1)}, u32[]{:S(2)}, u32[]{:S(2)}) collective-permute-start(bf16[1568,128]{1,0:T(8,128)(2,1)S(1)} %fusion.13), channel_id=1, source_target_pairs={{0,4},{4,0},{8,12},{12,8},{1,5},{5,1},{9,13},{13,9},{2,6},{6,2},{1... | collective-permute-start | bytes 1204232 | tf_op jit(solution)/shard_map/ppermute | solution.py:620
  302.8 14.5 %collective-permute-start.54 = (bf16[1,288,128]{2,1,0:T(8,128)(2,1)S(1)}, bf16[1,288,128]{2,1,0:T(8,128)(2,1)S(1)}, u32[]{:S(2)}, u32[]{:S(2)}) collective-permute-start(bf16[1,288,128]{2,1,0:T(8,128)(2,1)S(1)} %dynamic-slice_bitcast_fusion.13), channel_id=1, source_target_pairs={{0,2},{1,3},{2,0},{3,1},{4,6},{5,7},{6,4},{7,5},{8,10},{9,11},{10,... | collective-permute-start | bytes 221192 | tf_op jit(solution)/shard_map/ppermute | solution.py:620
  308.2 9.2 %collective-permute-start.56 = (bf16[1,288,128]{2,1,0:T(8,128)(2,1)S(1)}, bf16[1,288,128]{2,1,0:T(8,128)(2,1)S(1)}, u32[]{:S(2)}, u32[]{:S(2)}) collective-permute-start(bf16[1,288,128]{2,1,0:T(8,128)(2,1)S(1)} %dynamic-slice_bitcast_fusion.12), channel_id=1, source_target_pairs={{0,1},{1,0},{2,3},{3,2},{4,5},{5,4},{6,7},{7,6},{8,9},{9,8},{10,11... | collective-permute-start | bytes 221192 | tf_op jit(solution)/shard_map/ppermute | solution.py:620
  314.8 18.4 %collective-permute-start.60 = (bf16[1568,128]{1,0:T(8,128)(2,1)S(1)}, bf16[1568,128]{1,0:T(8,128)(2,1)S(1)}, u32[]{:S(2)}, u32[]{:S(2)}) collective-permute-start(bf16[1568,128]{1,0:T(8,128)(2,1)S(1)} %fusion.6), channel_id=1, source_target_pairs={{0,8},{4,12},{8,0},{12,4},{1,9},{5,13},{9,1},{13,5},{2,10},{6,14},... | collective-permute-start | bytes 1204232 | tf_op jit(solution)/shard_map/ppermute | solution.py:620
  317.5 15.9 %collective-permute-start.57 = (bf16[1152,128]{1,0:T(8,128)(2,1)S(1)}, bf16[1152,128]{1,0:T(8,128)(2,1)S(1)}, u32[]{:S(2)}, u32[]{:S(2)}) collective-permute-start(bf16[1152,128]{1,0:T(8,128)(2,1)S(1)} %pad_maximum_fusion.14), channel_id=1, source_target_pairs={{0,4},{4,0},{8,12},{12,8},{1,5},{5,1},{9,13},{13,9},{2,6},{6,2},{1... | collective-permute-start | bytes 884744 | tf_op jit(solution)/shard_map/ppermute | solution.py:620
  333.3 17.6 %collective-permute-start.61 = (bf16[1568,128]{1,0:T(8,128)(2,1)S(1)}, bf16[1568,128]{1,0:T(8,128)(2,1)S(1)}, u32[]{:S(2)}, u32[]{:S(2)}) collective-permute-start(bf16[1568,128]{1,0:T(8,128)(2,1)S(1)} %add_convert_fusion.4), channel_id=1, source_target_pairs={{0,4},{4,0},{8,12},{12,8},{1,5},{5,1},{9,13},{13,9},{2,6},{6,2},{1... | collective-permute-start | bytes 1204232 | tf_op jit(solution)/shard_map/ppermute | solution.py:620
  333.4 19.1 %collective-permute-start.58 = (bf16[1152,128]{1,0:T(8,128)(2,1)S(1)}, bf16[1152,128]{1,0:T(8,128)(2,1)S(1)}, u32[]{:S(2)}, u32[]{:S(2)}) collective-permute-start(bf16[1152,128]{1,0:T(8,128)(2,1)S(1)} %add_convert_fusion.7), channel_id=1, source_target_pairs={{0,8},{4,12},{8,0},{12,4},{1,9},{5,13},{9,1},{13,5},{2,10},{6,14},... | collective-permute-start | bytes 884744 | tf_op jit(solution)/shard_map/ppermute | solution.py:620
  (117 other events, 1148.5 us)

commit v4 on v3

--- a/solution.py
+++ b/solution.py
@@ -422,6 +422,10 @@
     return jnp.where(first, keep, other), jnp.where(first, other, keep)
 
 
+def gain_of(last_tile, shard):
+    return last_tile.astype(F32).T[LANES - HD : LANES - HD + 1, :shard]
+
+
 def unpack_mlp_kernel(pack, idx, zero, one, got, gate_out, up_out, down_out, o_out, gain_out):
     shard, half = pack.shard, pack.half
     both = halves(idx, zero, one, got)
@@ -429,20 +433,22 @@
         for k in range(pack.gate_tiles):
             at = k * pack.shard_step
             out[:, k * LANES : (k + 1) * LANES] = value[at : at + shard].astype(F32)
-    depth = down_out.shape[1]
+    depth = down_out.shape[0]
+    downs = []
     for side, value in enumerate(both):
         tiles = []
         for k in range(pack.down_tiles):
             at = pack.down_at + k * pack.half_step
             tiles.append(value[at : at + half])
-        wide_rows = jnp.concatenate(tiles, axis=1)[:, :depth]
-        down_out[side * half : (side + 1) * half, :] = wide_rows.astype(F32)
+        downs.append(jnp.concatenate(tiles, axis=1).astype(F32))
+    down_out[...] = jnp.concatenate(downs, axis=0).T[:depth]
     tiles = []
     for k in range(pack.down_tiles):
         at = pack.out_at + (k % pack.out_tiles) * pack.shard_step
         tiles.append(both[k // pack.out_tiles][at : at + shard])
     o_out[...] = jnp.concatenate(tiles, axis=1)[:, :depth].astype(F32)
-    gain_out[...] = tiles[-1].astype(F32)
+    at = pack.out_at + (pack.down_tiles - 1 - pack.out_tiles) * pack.shard_step
+    gain_out[...] = gain_of(both[1][at : at + pack.shard_step], shard)
 
 
 def unpack_mlp(pack, idx, zero, one, got, ff, depth):
@@ -451,9 +457,9 @@
         (
             shape((pack.shard, ff), F32),
             shape((pack.shard, ff), F32),
-            shape((2 * pack.half, depth), F32),
+            shape((depth, 2 * pack.half), F32),
             shape((pack.shard, depth), F32),
-            shape((pack.shard, LANES), F32),
+            shape((1, pack.shard), F32),
         ),
         [IN_SMEM] + [IN_VMEM] * 3,
         [],
@@ -465,7 +471,8 @@
 def unpack_entry_kernel(pack, idx, zero, one, got, q_out, k_out, v_out, gain_out):
     shard = pack.shard
     tiles = []
-    for value in halves(idx, zero, one, got):
+    both = halves(idx, zero, one, got)
+    for value in both:
         for k in range(pack.entry_tiles):
             at = k * pack.shard_step
             tiles.append(value[at : at + shard])
@@ -474,7 +481,8 @@
     q_out[...] = full[:, :qw]
     k_out[...] = full[:, qw : qw + kw]
     v_out[...] = full[:, qw + kw : qw + 2 * kw]
-    gain_out[...] = tiles[-1].astype(F32)
+    at = (pack.entry_tiles - 1) * pack.shard_step
+    gain_out[...] = gain_of(both[1][at : at + pack.shard_step], shard)
 
 
 def unpack_entry(pack, idx, zero, one, got):
@@ -485,7 +493,7 @@
             shape((pack.shard, qw), F32),
             shape((pack.shard, kw), F32),
             shape((pack.shard, kw), F32),
-            shape((pack.shard, LANES), F32),
+            shape((1, pack.shard), F32),
         ),
         [IN_SMEM] + [IN_VMEM] * 3,
         [],
@@ -901,6 +909,7 @@
     )
     a0 = start(joined(a_mine, a_theirs), entry_middle)
     late = sends(a0)[0]
+    m1 = held(m1, late)
     m0 = ctx_cut(last_sums(m0, (late,)))
     a1 = first_sums(a1, (m0[0],))
     a0 = first_sums(a0, (m0[0],))
@@ -908,8 +917,10 @@
     a1 = last_sums(a1, (m0,))
     a0 = last_sums(a0, (m0,))
     m1 = ctx_end(m1, (a0,))
-    a0 = sum_over_ctx(jnp.concatenate([a0, a1], axis=0))
-    m0 = ctx_end(ctx_middle(m0))
+    a0 = ctx_begin(ctx_cut(jnp.concatenate([a0, a1], axis=0)), ())
+    m0 = ctx_middle(m0, (a0,))
+    a0 = ctx_middle(a0, (m0,))
+    a0 = ctx_end(a0)
     a0, a1 = a0[: pack.entry_rows], a0[pack.entry_rows :]
 
     def own_layer(zero, one):
@@ -923,24 +934,24 @@
     section_out = jnp.stack(own_layer(outs[0], outs[1])).reshape(1, micro, seqs, block, depth)
     input_grad = jnp.stack(own_layer(entry[0], entry[1])).reshape(1, micro, seqs, block, depth)
     ff = gate_proj.shape[2]
+    a_got = other_core(pick(a1, a0))
+    query_g, key_g, value_g, attn_gain_g = unpack_entry(pack, idx, a0, a1, a_got)
+    m0 = ctx_end(m0, (query_g, section_out, input_grad))
     m_got = other_core(pick(m1, m0))
     gate_g, up_g, down_g, out_g, mlp_gain_g = unpack_mlp(pack, idx, m0, m1, m_got, ff, depth)
-    a_got = other_core(pick(a1, a0))
-    query_g, key_g, value_g, attn_gain_g = unpack_entry(pack, idx, a0, a1, a_got)
-    spare = LANES - HD
 
     return (
         section_out,
         input_grad,
-        attn_gain_g[:, spare][None],
+        attn_gain_g,
         query_g[None],
         key_g[None],
         value_g[None],
         out_g[None],
-        mlp_gain_g[:, spare][None],
+        mlp_gain_g,
         gate_g[None],
         up_g[None],
-        down_g[None],
+        down_g.T[None],
     )
 
 

time: 374 us -> 368 us (0.984)
  waiting for transfers between devices: 126 us -> 120 us
  local copies, waits for them, and re-layouts: 34.7 us -> 29.8 us
    ppermute x52 -> x53, waiting for transfers between devices: 83 us -> 77.7 us  [crossed(): return lax.ppermute(value, axis, [(i, i ^ mask) for i in range(count)])]
    ppermute x52 -> x53, starting transfers between devices: 34.6 us -> 37.4 us  [crossed(): return lax.ppermute(value, axis, [(i, i ^ mask) for i in range(count)])]
    unnamed x206 -> x203, local copies, waits for them, and re-layouts: 21.2 us -> 18.7 us
  transfers between devices with their start and end apart: 64 -> 65, of which waited for: 25 -> 30; matrix products, arithmetic and copies ran while one was open for 13% -> 13% of each run, Pallas kernels for 18% -> 18%
where the time goes in v4:
time: 368 us; the launch traced here: 362 us
  waiting for transfers between devices  120 us (33%)
  Pallas kernels  99.1 us (27%)
  starting transfers between devices  68.2 us (19%)
  other arithmetic  42.1 us (11%)
  local copies, waits for them, and re-layouts  29.8 us (8%)
    pallas_call x16, Pallas kernels, call(): pl.pallas_call(kernel, out_shape=tuple(outs), in_specs=in_specs, out_spec...  99.1 us
    ppermute x53, waiting for transfers between devices, crossed(): return lax.ppermute(value, axis, [(i, i ^ mask) for i in range(count)])  77.7 us
    ppermute x12, waiting for transfers between devices, shifted(): lax.ppermute(value, 'ctx', [(i, i + distance) for i in devices if i + dis...  42.4 us
    ppermute x53, starting transfers between devices, crossed(): return lax.ppermute(value, axis, [(i, i ^ mask) for i in range(count)])  37.4 us
    ppermute x12, starting transfers between devices, shifted(): lax.ppermute(value, 'ctx', [(i, i + distance) for i in devices if i + dis...  30.7 us
    unnamed x203, local copies, waits for them, and re-layouts  18.7 us
    select_n x8, other arithmetic, pick(): return jnp.where(first, a, b)  8.34 us
    convert_element_type x4, other arithmetic, joined(): return (mine.astype(F32) + got.astype(F32)).astype(BF)  8 us
  transfers between devices with their start and end apart: 65, of which 30 were waited for; matrix products, arithmetic and copies ran while one was open for 13% of the time, Pallas kernels for 18%

profile of v4, /device:TPU:0, one launch (start us, length us, event | category | flops | bytes accessed | tf_op | source)
XLA Modules:
  0.0 362.0 jit_solution(238724811936504921)
XLA Ops:
  2.6 3.0 collective-permute-start.4
  18.2 8.4 %collective-permute-done.5 = bf16[2,144,896]{2,1,0:T(8,128)(2,1)S(1)} collective-permute-done((bf16[2,144,896]{2,1,0:T(8,128)(2,1)S(1)}, bf16[2,144,896]{2,1,0:T(8,128)(2,1)S(1)}, u32[]{:S(2)}, u32[]{:S(2)}) %collective-permute-start.5) | collective-permute-done | bytes 516128 | tf_op jit(solution)/shard_map/ppermute | solution.py:628
  29.4 2.3 broadcast_select_fusion.10
  31.6 2.0 bitcast_select_fusion
  39.5 2.8 shard_map.203
  44.6 6.7 %collective-permute-done.6 = bf16[144,1536]{1,0:T(8,128)(2,1)S(1)} collective-permute-done((bf16[144,1536]{1,0:T(8,128)(2,1)}, bf16[144,1536]{1,0:T(8,128)(2,1)S(1)}, u32[]{:S(2)}, u32[]{:S(2)}) %collective-permute-start.6) | collective-permute-done | bytes 442400 | tf_op jit(solution)/shard_map/ppermute | solution.py:628
  53.0 3.5 collective-permute-start.12
  56.5 4.5 %collective-permute-start.13 = (bf16[256,384]{1,0:T(8,128)(2,1)S(1)}, bf16[256,384]{1,0:T(8,128)(2,1)S(1)}, u32[]{:S(2)}, u32[]{:S(2)}) collective-permute-start(bf16[256,384]{1,0:T(8,128)(2,1)S(1)} %get-tuple-element.126.refs_2_.refs_4_), channel_id=1, source_target_pairs={{0,8},{4,12},{1,9},{5,13},{2,10},{6,14},{3,11},{7,15},{16,24},{20,... | collective-permute-start | bytes 589832 | tf_op jit(solution)/shard_map/ppermute | solution.py:633
  62.5 3.4 collective-permute-done.13.refs_4_.refs_6_
  65.9 2.1 collective-permute-done.14.refs_5_.refs_7_
  68.0 7.0 %shard_map.204 = (bf16[256,576]{1,0:T(8,128)(2,1)S(1)}, f32[16,256]{1,0:T(8,128)S(1)}) custom-call(s32[2]{0:T(128)S(1)} %pad_add_fusion.refs_0_, bf16[256,576]{1,0:T(8,128)(2,1)S(1)} %get-tuple-element.125.refs_1_, bf16[256,384]{1,0:T(8,128)(2,1)S(1)} %get-tuple-element.126.refs_2_.refs_4_, bf16[256,384]{1,0:T(8,128)(2,1)S(1)} %collective-permute-done.12.refs_3_.refs_5_, ...), custom_call_target="tpu_custom_call" | custom-call | flops 2415919 | bytes 1392 | tf_op jit(solution)/shard_map/pallas_call | solution.py:56
  79.1 2.1 collective-permute-done.16.refs_8_
  81.3 6.4 %shard_map.205 = (bf16[256,576]{1,0:T(8,128)(2,1)S(1)}, f32[256,576]{1,0:T(8,128)S(1)}, bf16[256,576]{1,0:T(8,128)(2,1)S(1)}, f32[256,1536]{1,0:T(8,128)S(1)}, f...) custom-call(s32[2]{0:T(128)S(1)} %pad_add_fusion.refs_0_, bf16[256,576]{1,0:T(8,128)(2,1)S(1)} %bitcast.229, ...), custom_call_target="tpu_custom_call" | custom-call | flops 1528823 | bytes 13271 | tf_op jit(solution)/shard_map/pallas_call | solution.py:56
  88.6 3.9 %shard_map.206 = (bf16[256,576]{1,0:T(8,128)(2,1)S(1)}, bf16[256,576]{1,0:T(8,128)(2,1)S(1)}, bf16[256,384]{1,0:T(8,128)(2,1)S(1)}) custom-call(s32[2]{0:T(128)S(1)} %pad_add_fusion.refs_0_, bf16[256,576]{1,0:T(8,128)(2,1)S(1)} %get-tuple-element.200.refs_1_, bf16[576,896]{1,0:T(8,128)(2,1)S(1)} %bitcast.215, ...), custom_call_target="tpu_custom_call" | custom-call | flops 452984 | bytes 5472 | tf_op jit(solution)/shard_map/pallas_call | solution.py:56
  95.4 6.4 %collective-permute-start.21 = (bf16[256,384]{1,0:T(8,128)(2,1)S(1)}, bf16[256,384]{1,0:T(8,128)(2,1)S(1)}, u32[]{:S(2)}, u32[]{:S(2)}) collective-permute-start(bf16[256,384]{1,0:T(8,128)(2,1)S(1)} %get-tuple-element.140.refs_2_.refs_4_), channel_id=1, source_target_pairs={{0,4},{4,8},{8,12},{1,5},{5,9},{9,13},{2,6},{6,10},{10,14},{3,7},{... | collective-permute-start | bytes 589832 | tf_op jit(solution)/shard_map/ppermute | solution.py:633
  101.8 5.3 %collective-permute-start.22 = (bf16[256,384]{1,0:T(8,128)(2,1)S(1)}, bf16[256,384]{1,0:T(8,128)(2,1)S(1)}, u32[]{:S(2)}, u32[]{:S(2)}) collective-permute-start(bf16[256,384]{1,0:T(8,128)(2,1)S(1)} %get-tuple-element.140.refs_2_.refs_4_), channel_id=1, source_target_pairs={{0,8},{4,12},{1,9},{5,13},{2,10},{6,14},{3,11},{7,15},{16,24},{20,... | collective-permute-start | bytes 589832 | tf_op jit(solution)/shard_map/ppermute | solution.py:633
  108.9 2.9 collective-permute-done.22.refs_4_.refs_6_
  111.8 2.1 collective-permute-done.23.refs_5_.refs_7_
  113.9 7.0 %shard_map.207 = (bf16[256,576]{1,0:T(8,128)(2,1)S(1)}, f32[16,256]{1,0:T(8,128)S(1)}) custom-call(s32[2]{0:T(128)S(1)} %pad_add_fusion.refs_0_, bf16[256,576]{1,0:T(8,128)(2,1)S(1)} %get-tuple-element.139.refs_1_, bf16[256,384]{1,0:T(8,128)(2,1)S(1)} %get-tuple-element.140.refs_2_.refs_4_, bf16[256,384]{1,0:T(8,128)(2,1)S(1)} %collective-permute-done.21.refs_3_.refs_5_, ...), custom_call_target="tpu_custom_call" | custom-call | flops 2415919 | bytes 1392 | tf_op jit(solution)/shard_map/pallas_call | solution.py:56
  125.6 2.5 collective-permute-done.25.refs_8_
  129.7 6.6 %shard_map.208 = (bf16[256,576]{1,0:T(8,128)(2,1)S(1)}, f32[256,576]{1,0:T(8,128)S(1)}, bf16[256,576]{1,0:T(8,128)(2,1)S(1)}, f32[256,1536]{1,0:T(8,128)S(1)}, f...) custom-call(s32[2]{0:T(128)S(1)} %copy-done.57, bf16[256,576]{1,0:T(8,128)(2,1)S(1)} %get-tuple-element.200.refs_1_, ...), custom_call_target="tpu_custom_call" | custom-call | flops 1528823 | bytes 13271 | tf_op jit(solution)/shard_map/pallas_call | solution.py:56
  136.3 8.1 %shard_map.209 = (bf16[256,1536]{1,0:T(8,128)(2,1)S(1)}, bf16[256,1536]{1,0:T(8,128)(2,1)S(1)}, f32[256,576]{1,0:T(8,128)S(1)}, bf16[256,576]{1,0:T(8,128)(2,1)S...) custom-call(s32[2]{0:T(128)S(1)} %copy-done.57, bf16[256,576]{1,0:T(8,128)(2,1)S(1)} %bitcast.230, ...), custom_call_target="tpu_custom_call" | custom-call | flops 1528823 | bytes 14499 | tf_op jit(solution)/shard_map/pallas_call | solution.py:56
  146.0 4.3 %shard_map.210 = (bf16[4,3136,128]{2,1,0:T(8,128)(2,1)S(1)}, bf16[4,3136,128]{2,1,0:T(8,128)(2,1)}) custom-call(s32[2]{0:T(128)S(1)} %copy-done.57, bf16[256,1536]{1,0:T(8,128)(2,1)S(1)} %get-tuple-element.151.refs_1_, bf16[256,576]{1,0:T(8,128)(2,1)S(1)} %bitcast.231, bf16[256,576]{1,0:T(8,128)(2,1)S(1)} %get-tuple-element.152.refs_3_, ...), custom_call_target="tpu_custom_call" | custom-call | flops 1528823 | bytes 10108 | tf_op jit(solution)/shard_map/pallas_call | solution.py:56
  152.1 11.4 %shard_map.211 = (f32[256,576]{1,0:T(8,128)}, f32[256,384]{1,0:T(8,128)}, bf16[256,384]{1,0:T(8,128)(2,1)}, bf16[256,384]{1,0:T(8,128)(2,1)}, bf16[256,384]{1,0:T(8,128)(2,1)}) custom-call(s32[2]{0:T(128)} %copy-done.56, bf16[256,576]{1,0:T(8,128)(2,1)} %copy-done.29, bf16[256,576]{1,0:T(8,128)(2,1)} %copy-done.53, f32[16,256]{1,0:T(8,128)} %copy-done.60, ...), custom_call_target="tpu_custom_call" | custom-call | flops 6039797 | bytes 2965 | tf_op jit(solution)/shard_map/pallas_call | solution.py:56
  165.2 2.7 add_convert_fusion.1
  178.4 4.7 %collective-permute-done.26.refs_5_ = bf16[256,384]{1,0:T(8,128)(2,1)S(1)} collective-permute-done((bf16[256,384]{1,0:T(8,128)(2,1)}, bf16[256,384]{1,0:T(8,128)(2,1)S(1)}, u32[]{:S(2)}, u32[]{:S(2)}) %collective-permute-start.26) | collective-permute-done | bytes 196640 | tf_op jit(solution)/shard_map/ppermute | solution.py:633
  183.1 13.9 %collective-permute-done.27.refs_6_ = bf16[256,384]{1,0:T(8,128)(2,1)} collective-permute-done((bf16[256,384]{1,0:T(8,128)(2,1)}, bf16[256,384]{1,0:T(8,128)(2,1)}, u32[]{:S(2)}, u32[]{:S(2)}) %collective-permute-start.27) | collective-permute-done | bytes 196640 | tf_op jit(solution)/shard_map/ppermute | solution.py:633
  197.1 6.8 %shard_map.212 = (bf16[256,576]{1,0:T(8,128)(2,1)}, bf16[4,576,128]{2,1,0:T(8,128)(2,1)}, bf16[4,576,128]{2,1,0:T(8,128)(2,1)}) custom-call(s32[2]{0:T(128)} %copy-done.56, bf16[256,576]{1,0:T(8,128)(2,1)} %copy-done.11, bf16[256,576]{1,0:T(8,128)(2,1)} %copy-done.52, f32[256,576]{1,0:T(8,128)} %get-tuple-element.158.refs_3_, ...), custom_call_target="tpu_custom_call" | custom-call | flops 905969 | bytes 8617 | tf_op jit(solution)/shard_map/pallas_call | solution.py:56
  208.5 8.1 %shard_map.213 = (bf16[256,1536]{1,0:T(8,128)(2,1)S(1)}, bf16[256,1536]{1,0:T(8,128)(2,1)S(1)}, f32[256,576]{1,0:T(8,128)S(1)}, bf16[256,576]{1,0:T(8,128)(2,1)S...) custom-call(s32[2]{0:T(128)S(1)} %copy-done.58, bf16[256,576]{1,0:T(8,128)(2,1)S(1)} %copy-done.14, ...), custom_call_target="tpu_custom_call" | custom-call | flops 1528823 | bytes 14499 | tf_op jit(solution)/shard_map/pallas_call | solution.py:56
  216.8 2.0 collective-permute-done.32
  220.4 4.2 %shard_map.214 = (bf16[4,3136,128]{2,1,0:T(8,128)(2,1)S(1)}, bf16[4,3136,128]{2,1,0:T(8,128)(2,1)}) custom-call(s32[2]{0:T(128)S(1)} %copy-done.58, bf16[256,1536]{1,0:T(8,128)(2,1)S(1)} %copy-done.41, bf16[256,576]{1,0:T(8,128)(2,1)S(1)} %copy-done.14, bf16[256,576]{1,0:T(8,128)(2,1)S(1)} %copy-done.51, bf16[256,1536]{1,0:T(8,128)(2,1)S(1)} %get-tuple-element.176.refs_4_, ...), custom_call_target="tpu_custom_call" | custom-call | flops 1528823 | bytes 10108 | tf_op jit(solution)/shard_map/pallas_call | solution.py:56
  226.8 6.4 %collective-permute-done.34 = bf16[4,3136,128]{2,1,0:T(8,128)(2,1)} collective-permute-done((bf16[4,3136,128]{2,1,0:T(8,128)(2,1)}, bf16[4,3136,128]{2,1,0:T(8,128)(2,1)}, u32[]{:S(2)}, u32[]{:S(2)}) %collective-permute-start.34) | collective-permute-done | bytes 3211296 | tf_op jit(solution)/shard_map/ppermute | solution.py:628
  233.2 3.7 %add_convert_fusion = bf16[4,3136,128]{2,1,0:T(8,128)(2,1)S(1)} fusion(bf16[4,3136,128]{2,1,0:T(8,128)(2,1)} %collective-permute-done.34, bf16[4,3136,128]{2,1,0:T(8,128)(2,1)} %copy-done.21), kind=kLoop, calls=%fused_computation | loop fusion | flops 6422528 | bytes 9633792 | tf_op jit(solution)/shard_map/convert_element_type | solution.py:842
  241.5 11.0 %shard_map.215 = (f32[256,576]{1,0:T(8,128)}, f32[256,384]{1,0:T(8,128)}, bf16[256,384]{1,0:T(8,128)(2,1)}, bf16[256,384]{1,0:T(8,128)(2,1)}, bf16[256,384]{1,0:T(8,128)(2,1)}) custom-call(s32[2]{0:T(128)} %copy-done.56, bf16[256,576]{1,0:T(8,128)(2,1)} %copy-done.35, bf16[256,576]{1,0:T(8,128)(2,1)} %copy-done.54, f32[16,256]{1,0:T(8,128)} %copy-done.59, ...), custom_call_target="tpu_custom_call" | custom-call | flops 6039797 | bytes 2965 | tf_op jit(solution)/shard_map/pallas_call | solution.py:56
  256.9 7.6 %collective-permute-done.38.refs_7_ = bf16[256,384]{1,0:T(8,128)(2,1)S(1)} collective-permute-done((bf16[256,384]{1,0:T(8,128)(2,1)}, bf16[256,384]{1,0:T(8,128)(2,1)S(1)}, u32[]{:S(2)}, u32[]{:S(2)}) %collective-permute-start.38) | collective-permute-done | bytes 196640 | tf_op jit(solution)/shard_map/ppermute | solution.py:633
  270.9 5.6 %collective-permute-done.37.refs_6_ = bf16[256,384]{1,0:T(8,128)(2,1)S(1)} collective-permute-done((bf16[256,384]{1,0:T(8,128)(2,1)S(1)}, bf16[256,384]{1,0:T(8,128)(2,1)S(1)}, u32[]{:S(2)}, u32[]{:S(2)}) %collective-permute-start.37) | collective-permute-done | bytes 196640 | tf_op jit(solution)/shard_map/ppermute | solution.py:633
  277.1 5.9 %shard_map.216 = (bf16[256,576]{1,0:T(8,128)(2,1)}, bf16[4,576,128]{2,1,0:T(8,128)(2,1)}, bf16[4,576,128]{2,1,0:T(8,128)(2,1)}) custom-call(s32[2]{0:T(128)} %copy-done.56, bf16[256,576]{1,0:T(8,128)(2,1)} %bitcast.228, bf16[256,576]{1,0:T(8,128)(2,1)} %copy-done.55, f32[256,576]{1,0:T(8,128)} %get-tuple-element.185.refs_3_, ...), custom_call_target="tpu_custom_call" | custom-call | flops 905969 | bytes 8617 | tf_op jit(solution)/shard_map/pallas_call | solution.py:56
  290.3 7.5 %collective-permute-done.48 = bf16[1,1408,128]{2,1,0:T(8,128)(2,1)S(1)} collective-permute-done((bf16[1,1408,128]{2,1,0:T(8,128)(2,1)S(1)}, bf16[1,1408,128]{2,1,0:T(8,128)(2,1)S(1)}, u32[]{:S(2)}, u32[]{:S(2)}) %collective-permute-start.48) | collective-permute-done | bytes 360480 | tf_op jit(solution)/shard_map/ppermute | solution.py:628
  297.9 2.2 collective-permute-done.47
  304.9 3.6 %collective-permute-done.51 = bf16[2,1,288,128]{3,2,1,0:T(8,128)(2,1)S(1)} collective-permute-done((bf16[2,1,288,128]{3,2,1,0:T(8,128)(2,1)S(1)}, bf16[2,1,288,128]{3,2,1,0:T(8,128)(2,1)S(1)}, u32[]{:S(2)}, u32[]{:S(2)}) %collective-permute-start.51) | collective-permute-done | bytes 147488 | tf_op jit(solution)/shard_map/ppermute | solution.py:628
  310.5 2.1 collective-permute-done.50
  315.0 1.9 collective-permute-done.49
  319.6 11.8 %collective-permute-done.57 = bf16[576,128]{1,0:T(8,128)(2,1)S(1)} collective-permute-done((bf16[576,128]{1,0:T(8,128)(2,1)S(1)}, bf16[576,128]{1,0:T(8,128)(2,1)S(1)}, u32[]{:S(2)}, u32[]{:S(2)}) %collective-permute-start.57) | collective-permute-done | bytes 147488 | tf_op jit(solution)/shard_map/ppermute | solution.py:628
  334.2 7.4 %collective-permute-done.58 = bf16[576,128]{1,0:T(8,128)(2,1)S(1)} collective-permute-done((bf16[576,128]{1,0:T(8,128)(2,1)S(1)}, bf16[576,128]{1,0:T(8,128)(2,1)S(1)}, u32[]{:S(2)}, u32[]{:S(2)}) %collective-permute-start.58) | collective-permute-done | bytes 147488 | tf_op jit(solution)/shard_map/ppermute | solution.py:628
  341.9 2.1 collective-permute-start.62
  344.0 4.5 %collective-permute-done.60 = bf16[576,128]{1,0:T(8,128)(2,1)S(1)} collective-permute-done((bf16[576,128]{1,0:T(8,128)(2,1)S(1)}, bf16[576,128]{1,0:T(8,128)(2,1)S(1)}, u32[]{:S(2)}, u32[]{:S(2)}) %collective-permute-start.60) | collective-permute-done | bytes 147488 | tf_op jit(solution)/shard_map/ppermute | solution.py:628
  351.2 2.0 shard_map.217
  358.2 3.6 %shard_map.218 = (f32[144,1536]{1,0:T(8,128)}, f32[144,1536]{1,0:T(8,128)}, f32[576,384]{1,0:T(8,128)}, f32[144,576]{1,0:T(8,128)}, f32[1,144]{1,0:T(1,128)}) custom-call(s32[2]{0:T(128)} %copy-done.56, bf16[3136,128]{1,0:T(8,128)(2,1)} %get-tuple-element.288.refs_1_, bf16[3136,128]{1,0:T(8,128)(2,1)} %get-tuple-element.289.refs_2_, bf16[3136,128]{1,0:T(8,128)(2,1)} %copy-done.82), custom_call_target="tpu_custom_call" | custom-call | flops 1 | bytes 5395 | tf_op jit(solution)/shard_map/pallas_call | solution.py:56
  (409 shorter events, 113.1 us)
Async XLA Ops:
  2.6 10.0 %collective-permute-start.4 = (bf16[144,896]{1,0:T(8,128)(2,1)S(1)}, bf16[144,896]{1,0:T(8,128)(2,1)S(1)}, u32[]{:S(2)}, u32[]{:S(2)}) collective-permute-start(bf16[144,896]{1,0:T(8,128)(2,1)S(1)} %pad_maximum_fusion.15), channel_id=1, source_target_pairs={{0,2},{1,3},{2,0},{3,1},{4,6},{5,7},{6,4},{7,5},{8,10},{9,11},{10,... | collective-permute-start | bytes 774152 | tf_op jit(solution)/shard_map/ppermute | solution.py:628
  11.2 18.1 %collective-permute-start.1 = (bf16[192,640]{1,0:T(8,128)(2,1)}, bf16[192,640]{1,0:T(8,128)(2,1)}, u32[]{:S(2)}, u32[]{:S(2)}) collective-permute-start(bf16[192,640]{1,0:T(8,128)(2,1)} %broadcast_select_fusion.12), channel_id=1, source_target_pairs={{0,16},{16,0},{1,17},{17,1},{2,18},{18,2},{3,19},{19,3},{4,20},{20... | collective-permute-start | bytes 737288 | tf_op jit(solution)/shard_map/ppermute | solution.py:628
  12.1 19.6 %collective-permute-start = (bf16[144,1536]{1,0:T(8,128)(2,1)}, bf16[144,1536]{1,0:T(8,128)(2,1)}, u32[]{:S(2)}, u32[]{:S(2)}) collective-permute-start(bf16[144,1536]{1,0:T(8,128)(2,1)} %select_bitcast_fusion.16), channel_id=1, source_target_pairs={{0,16},{16,0},{1,17},{17,1},{2,18},{18,2},{3,19},{19,3},{4,20},{20... | collective-permute-start | bytes 1327112 | tf_op jit(solution)/shard_map/ppermute | solution.py:628
  12.9 13.7 %collective-permute-start.5 = (bf16[2,144,896]{2,1,0:T(8,128)(2,1)S(1)}, bf16[2,144,896]{2,1,0:T(8,128)(2,1)S(1)}, u32[]{:S(2)}, u32[]{:S(2)}) collective-permute-start(bf16[2,144,896]{2,1,0:T(8,128)(2,1)S(1)} %pad_maximum_fusion.11), channel_id=1, source_target_pairs={{0,1},{1,0},{2,3},{3,2},{4,5},{5,4},{6,7},{7,6},{8,9},{9,8},{10,11... | collective-permute-start | bytes 1548296 | tf_op jit(solution)/shard_map/ppermute | solution.py:628
  16.6 12.4 %collective-permute-start.3 = (bf16[2,144,896]{2,1,0:T(8,128)(2,1)S(1)}, bf16[2,144,896]{2,1,0:T(8,128)(2,1)S(1)}, u32[]{:S(2)}, u32[]{:S(2)}) collective-permute-start(bf16[2,144,896]{2,1,0:T(8,128)(2,1)S(1)} %pad_maximum_fusion.10), channel_id=1, source_target_pairs={{0,2},{1,3},{2,0},{3,1},{4,6},{5,7},{6,4},{7,5},{8,10},{9,11},{10,... | collective-permute-start | bytes 1548296 | tf_op jit(solution)/shard_map/ppermute | solution.py:628
  27.0 12.5 %collective-permute-start.8 = (bf16[576,896]{1,0:T(8,128)(2,1)S(1)}, bf16[576,896]{1,0:T(8,128)(2,1)S(1)}, u32[]{:S(2)}, u32[]{:S(2)}) collective-permute-start(bf16[576,896]{1,0:T(8,128)(2,1)S(1)} %bitcast.204), channel_id=1, source_target_pairs={{0,16},{16,0},{1,17},{17,1},{2,18},{18,2},{3,19},{19,3},{4,20},{20... | collective-permute-start | bytes 3096584 | tf_op jit(solution)/shard_map/ppermute | solution.py:628
  29.3 10.3 %collective-permute-start.7 = (bf16[576,896]{1,0:T(8,128)(2,1)S(1)}, bf16[576,896]{1,0:T(8,128)(2,1)}, u32[]{:S(2)}, u32[]{:S(2)}) collective-permute-start(bf16[576,896]{1,0:T(8,128)(2,1)S(1)} %bitcast.213), channel_id=1, source_target_pairs={{0,16},{16,0},{1,17},{17,1},{2,18},{18,2},{3,19},{19,3},{4,20},{20... | collective-permute-start | bytes 3096584 | tf_op jit(solution)/shard_map/ppermute | solution.py:628
  38.0 13.3 %collective-permute-start.6 = (bf16[144,1536]{1,0:T(8,128)(2,1)}, bf16[144,1536]{1,0:T(8,128)(2,1)S(1)}, u32[]{:S(2)}, u32[]{:S(2)}) collective-permute-start(bf16[144,1536]{1,0:T(8,128)(2,1)} %get-tuple-element.120), channel_id=1, source_target_pairs={{0,1},{1,0},{2,3},{3,2},{4,5},{5,4},{6,7},{7,6},{8,9},{9,8},{10,11... | collective-permute-start | bytes 1327112 | tf_op jit(solution)/shard_map/ppermute | solution.py:628
  43.8 31.2 %collective-permute-start.11 = (bf16[2,192,640]{2,1,0:T(8,128)(2,1)S(1)}, bf16[2,192,640]{2,1,0:T(8,128)(2,1)S(1)}, u32[]{:S(2)}, u32[]{:S(2)}) collective-permute-start(bf16[2,192,640]{2,1,0:T(8,128)(2,1)S(1)} %pad_maximum_fusion.12), channel_id=1, source_target_pairs={{0,1},{1,0},{2,3},{3,2},{4,5},{5,4},{6,7},{7,6},{8,9},{9,8},{10,11... | collective-permute-start | bytes 1474568 | tf_op jit(solution)/shard_map/ppermute | solution.py:628
  51.5 24.3 %collective-permute-start.9 = (bf16[2,144,1536]{2,1,0:T(8,128)(2,1)S(1)}, bf16[2,144,1536]{2,1,0:T(8,128)(2,1)S(1)}, u32[]{:S(2)}, u32[]{:S(2)}) collective-permute-start(bf16[2,144,1536]{2,1,0:T(8,128)(2,1)S(1)} %pad_maximum_fusion.6), channel_id=1, source_target_pairs={{0,2},{1,3},{2,0},{3,1},{4,6},{5,7},{6,4},{7,5},{8,10},{9,11},{10,... | collective-permute-start | bytes 2654216 | tf_op jit(solution)/shard_map/ppermute | solution.py:628
  53.0 9.5 %collective-permute-start.12 = (bf16[256,384]{1,0:T(8,128)(2,1)S(1)}, bf16[256,384]{1,0:T(8,128)(2,1)S(1)}, u32[]{:S(2)}, u32[]{:S(2)}) collective-permute-start(bf16[256,384]{1,0:T(8,128)(2,1)S(1)} %get-tuple-element.126.refs_2_.refs_4_), channel_id=1, source_target_pairs={{0,4},{4,8},{8,12},{1,5},{5,9},{9,13},{2,6},{6,10},{10,14},{3,7},{... | collective-permute-start | bytes 589832 | tf_op jit(solution)/shard_map/ppermute | solution.py:633
  56.5 9.5 %collective-permute-start.13 = (bf16[256,384]{1,0:T(8,128)(2,1)S(1)}, bf16[256,384]{1,0:T(8,128)(2,1)S(1)}, u32[]{:S(2)}, u32[]{:S(2)}) collective-permute-start(bf16[256,384]{1,0:T(8,128)(2,1)S(1)} %get-tuple-element.126.refs_2_.refs_4_), channel_id=1, source_target_pairs={{0,8},{4,12},{1,9},{5,13},{2,10},{6,14},{3,11},{7,15},{16,24},{20,... | collective-permute-start | bytes 589832 | tf_op jit(solution)/shard_map/ppermute | solution.py:633
  77.1 15.4 %collective-permute-start.18 = (bf16[192,640]{1,0:T(8,128)(2,1)S(1)}, bf16[192,640]{1,0:T(8,128)(2,1)S(1)}, u32[]{:S(2)}, u32[]{:S(2)}) collective-permute-start(bf16[192,640]{1,0:T(8,128)(2,1)S(1)} %copy-done.81), channel_id=1, source_target_pairs={{0,1},{1,0},{2,3},{3,2},{4,5},{5,4},{6,7},{7,6},{8,9},{9,8},{10,11... | collective-permute-start | bytes 737288 | tf_op jit(solution)/shard_map/ppermute | solution.py:628
  78.6 14.0 %collective-permute-start.17 = (bf16[144,1536]{1,0:T(8,128)(2,1)S(1)}, bf16[144,1536]{1,0:T(8,128)(2,1)S(1)}, u32[]{:S(2)}, u32[]{:S(2)}) collective-permute-start(bf16[144,1536]{1,0:T(8,128)(2,1)S(1)} %copy-done.76), channel_id=1, source_target_pairs={{0,2},{1,3},{2,0},{3,1},{4,6},{5,7},{6,4},{7,5},{8,10},{9,11},{10,... | collective-permute-start | bytes 1327112 | tf_op jit(solution)/shard_map/ppermute | solution.py:628
  93.3 27.6 %collective-permute-start.20 = (bf16[2,192,640]{2,1,0:T(8,128)(2,1)S(1)}, bf16[2,192,640]{2,1,0:T(8,128)(2,1)S(1)}, u32[]{:S(2)}, u32[]{:S(2)}) collective-permute-start(bf16[2,192,640]{2,1,0:T(8,128)(2,1)S(1)} %pad_maximum_fusion.13), channel_id=1, source_target_pairs={{0,2},{1,3},{2,0},{3,1},{4,6},{5,7},{6,4},{7,5},{8,10},{9,11},{10,... | collective-permute-start | bytes 1474568 | tf_op jit(solution)/shard_map/ppermute | solution.py:628
  93.9 27.7 %collective-permute-start.19 = (bf16[2,144,1536]{2,1,0:T(8,128)(2,1)S(1)}, bf16[2,144,1536]{2,1,0:T(8,128)(2,1)S(1)}, u32[]{:S(2)}, u32[]{:S(2)}) collective-permute-start(bf16[2,144,1536]{2,1,0:T(8,128)(2,1)S(1)} %pad_maximum_fusion.7), channel_id=1, source_target_pairs={{0,1},{1,0},{2,3},{3,2},{4,5},{5,4},{6,7},{7,6},{8,9},{9,8},{10,11... | collective-permute-start | bytes 2654216 | tf_op jit(solution)/shard_map/ppermute | solution.py:628
  95.4 13.4 %collective-permute-start.21 = (bf16[256,384]{1,0:T(8,128)(2,1)S(1)}, bf16[256,384]{1,0:T(8,128)(2,1)S(1)}, u32[]{:S(2)}, u32[]{:S(2)}) collective-permute-start(bf16[256,384]{1,0:T(8,128)(2,1)S(1)} %get-tuple-element.140.refs_2_.refs_4_), channel_id=1, source_target_pairs={{0,4},{4,8},{8,12},{1,5},{5,9},{9,13},{2,6},{6,10},{10,14},{3,7},{... | collective-permute-start | bytes 589832 | tf_op jit(solution)/shard_map/ppermute | solution.py:633
  101.8 10.0 %collective-permute-start.22 = (bf16[256,384]{1,0:T(8,128)(2,1)S(1)}, bf16[256,384]{1,0:T(8,128)(2,1)S(1)}, u32[]{:S(2)}, u32[]{:S(2)}) collective-permute-start(bf16[256,384]{1,0:T(8,128)(2,1)S(1)} %get-tuple-element.140.refs_2_.refs_4_), channel_id=1, source_target_pairs={{0,8},{4,12},{1,9},{5,13},{2,10},{6,14},{3,11},{7,15},{16,24},{20,... | collective-permute-start | bytes 589832 | tf_op jit(solution)/shard_map/ppermute | solution.py:633
  151.9 11.6 %collective-permute-start.29 = (bf16[4,3136,128]{2,1,0:T(8,128)(2,1)}, bf16[4,3136,128]{2,1,0:T(8,128)(2,1)S(1)}, u32[]{:S(2)}, u32[]{:S(2)}) collective-permute-start(bf16[4,3136,128]{2,1,0:T(8,128)(2,1)} %get-tuple-element.164), channel_id=1, source_target_pairs={{0,16},{16,0},{1,17},{17,1},{2,18},{18,2},{3,19},{19,3},{4,20},{20... | collective-permute-start | bytes 9633800 | tf_op jit(solution)/shard_map/ppermute | solution.py:628
  170.1 33.8 %collective-permute-start.31 = (bf16[2,1,1408,128]{3,2,1,0:T(8,128)(2,1)}, bf16[2,1,1408,128]{3,2,1,0:T(8,128)(2,1)}, u32[]{:S(2)}, u32[]{:S(2)}) collective-permute-start(bf16[2,1,1408,128]{3,2,1,0:T(8,128)(2,1)} %dynamic-slice_bitcast_fusion.3.refs_16_), channel_id=1, source_target_pairs={{0,2},{1,3},{2,0},{3,1},{4,6},{5,7},{6,4},{7,5},{8,10},{9,11},{10,... | collective-permute-start | bytes 2162696 | tf_op jit(solution)/shard_map/ppermute | solution.py:628
  171.6 11.5 %collective-permute-start.26 = (bf16[256,384]{1,0:T(8,128)(2,1)}, bf16[256,384]{1,0:T(8,128)(2,1)S(1)}, u32[]{:S(2)}, u32[]{:S(2)}) collective-permute-start(bf16[256,384]{1,0:T(8,128)(2,1)} %get-tuple-element.160), channel_id=1, source_target_pairs={{4,0},{8,4},{12,8},{5,1},{9,5},{13,9},{6,2},{10,6},{14,10},{7,3},{... | collective-permute-start | bytes 589832 | tf_op jit(solution)/shard_map/ppermute | solution.py:633
  172.9 24.1 %collective-permute-start.27 = (bf16[256,384]{1,0:T(8,128)(2,1)}, bf16[256,384]{1,0:T(8,128)(2,1)}, u32[]{:S(2)}, u32[]{:S(2)}) collective-permute-start(bf16[256,384]{1,0:T(8,128)(2,1)} %get-tuple-element.161), channel_id=1, source_target_pairs={{8,0},{12,4},{9,1},{13,5},{10,2},{14,6},{11,3},{15,7},{24,16},{28,... | collective-permute-start | bytes 589832 | tf_op jit(solution)/shard_map/ppermute | solution.py:633
  174.2 22.8 %collective-permute-start.28 = (bf16[256,384]{1,0:T(8,128)(2,1)}, bf16[256,384]{1,0:T(8,128)(2,1)}, u32[]{:S(2)}, u32[]{:S(2)}) collective-permute-start(bf16[256,384]{1,0:T(8,128)(2,1)} %get-tuple-element.162), channel_id=1, source_target_pairs={{12,0},{13,1},{14,2},{15,3},{28,16},{29,17},{30,18},{31,19}} | collective-permute-start | bytes 589832 | tf_op jit(solution)/shard_map/ppermute | solution.py:633
  177.8 28.2 %collective-permute-start.30 = (bf16[2,1,1728,128]{3,2,1,0:T(8,128)(2,1)}, bf16[2,1,1728,128]{3,2,1,0:T(8,128)(2,1)}, u32[]{:S(2)}, u32[]{:S(2)}) collective-permute-start(bf16[2,1,1728,128]{3,2,1,0:T(8,128)(2,1)} %dynamic-slice_bitcast_fusion.1.refs_15_), channel_id=1, source_target_pairs={{0,1},{1,0},{2,3},{3,2},{4,5},{5,4},{6,7},{7,6},{8,9},{9,8},{10,11... | collective-permute-start | bytes 2654216 | tf_op jit(solution)/shard_map/ppermute | solution.py:628
  205.5 11.2 %collective-permute-start.33 = (bf16[1,1408,128]{2,1,0:T(8,128)(2,1)S(1)}, bf16[1,1408,128]{2,1,0:T(8,128)(2,1)S(1)}, u32[]{:S(2)}, u32[]{:S(2)}) collective-permute-start(bf16[1,1408,128]{2,1,0:T(8,128)(2,1)S(1)} %dynamic-slice_bitcast_fusion.7), channel_id=1, source_target_pairs={{0,1},{1,0},{2,3},{3,2},{4,5},{5,4},{6,7},{7,6},{8,9},{9,8},{10,11... | collective-permute-start | bytes 1081352 | tf_op jit(solution)/shard_map/ppermute | solution.py:628
  207.9 11.0 %collective-permute-start.32 = (bf16[1,1728,128]{2,1,0:T(8,128)(2,1)S(1)}, bf16[1,1728,128]{2,1,0:T(8,128)(2,1)S(1)}, u32[]{:S(2)}, u32[]{:S(2)}) collective-permute-start(bf16[1,1728,128]{2,1,0:T(8,128)(2,1)S(1)} %dynamic-slice_bitcast_fusion.5), channel_id=1, source_target_pairs={{0,2},{1,3},{2,0},{3,1},{4,6},{5,7},{6,4},{7,5},{8,10},{9,11},{10,... | collective-permute-start | bytes 1327112 | tf_op jit(solution)/shard_map/ppermute | solution.py:628
  226.3 27.7 %collective-permute-start.41 = (bf16[4,576,128]{2,1,0:T(8,128)(2,1)S(1)}, bf16[4,576,128]{2,1,0:T(8,128)(2,1)S(1)}, u32[]{:S(2)}, u32[]{:S(2)}) collective-permute-start(bf16[4,576,128]{2,1,0:T(8,128)(2,1)S(1)} %copy-done.97), channel_id=1, source_target_pairs={{0,16},{16,0},{1,17},{17,1},{2,18},{18,2},{3,19},{19,3},{4,20},{20... | collective-permute-start | bytes 1769480 | tf_op jit(solution)/shard_map/ppermute | solution.py:628
  226.8 11.8 %collective-permute-start.35 = (bf16[1568,128]{1,0:T(8,128)(2,1)S(1)}, bf16[1568,128]{1,0:T(8,128)(2,1)S(1)}, u32[]{:S(2)}, u32[]{:S(2)}) collective-permute-start(bf16[1568,128]{1,0:T(8,128)(2,1)S(1)} %fusion.17.refs_9_), channel_id=1, source_target_pairs={{0,4},{4,0},{8,12},{12,8},{1,5},{5,1},{9,13},{13,9},{2,6},{6,2},{1... | collective-permute-start | bytes 1204232 | tf_op jit(solution)/shard_map/ppermute | solution.py:628
  237.2 31.4 %collective-permute-start.39 = (bf16[2,1,1728,128]{3,2,1,0:T(8,128)(2,1)S(1)}, bf16[2,1,1728,128]{3,2,1,0:T(8,128)(2,1)}, u32[]{:S(2)}, u32[]{:S(2)}) collective-permute-start(bf16[2,1,1728,128]{3,2,1,0:T(8,128)(2,1)S(1)} %dynamic-slice_bitcast_fusion.refs_8_), channel_id=1, source_target_pairs={{0,1},{1,0},{2,3},{3,2},{4,5},{5,4},{6,7},{7,6},{8,9},{9,8},{10,11... | collective-permute-start | bytes 2654216 | tf_op jit(solution)/shard_map/ppermute | solution.py:628
  240.0 25.8 %collective-permute-start.42 = (bf16[1568,128]{1,0:T(8,128)(2,1)S(1)}, bf16[1568,128]{1,0:T(8,128)(2,1)}, u32[]{:S(2)}, u32[]{:S(2)}) collective-permute-start(bf16[1568,128]{1,0:T(8,128)(2,1)S(1)} %fusion.7.refs_10_), channel_id=1, source_target_pairs={{0,8},{4,12},{8,0},{12,4},{1,9},{5,13},{9,1},{13,5},{2,10},{6,14},... | collective-permute-start | bytes 1204232 | tf_op jit(solution)/shard_map/ppermute | solution.py:628
  240.7 27.0 %collective-permute-start.40 = (bf16[2,1,1408,128]{3,2,1,0:T(8,128)(2,1)S(1)}, bf16[2,1,1408,128]{3,2,1,0:T(8,128)(2,1)S(1)}, u32[]{:S(2)}, u32[]{:S(2)}) collective-permute-start(bf16[2,1,1408,128]{3,2,1,0:T(8,128)(2,1)S(1)} %dynamic-slice_bitcast_fusion.2.refs_9_), channel_id=1, source_target_pairs={{0,2},{1,3},{2,0},{3,1},{4,6},{5,7},{6,4},{7,5},{8,10},{9,11},{10,... | collective-permute-start | bytes 2162696 | tf_op jit(solution)/shard_map/ppermute | solution.py:628
  252.6 11.9 %collective-permute-start.38 = (bf16[256,384]{1,0:T(8,128)(2,1)}, bf16[256,384]{1,0:T(8,128)(2,1)S(1)}, u32[]{:S(2)}, u32[]{:S(2)}) collective-permute-start(bf16[256,384]{1,0:T(8,128)(2,1)} %get-tuple-element.189), channel_id=1, source_target_pairs={{12,0},{13,1},{14,2},{15,3},{28,16},{29,17},{30,18},{31,19}} | collective-permute-start | bytes 589832 | tf_op jit(solution)/shard_map/ppermute | solution.py:633
  254.3 16.6 %collective-permute-start.36 = (bf16[256,384]{1,0:T(8,128)(2,1)S(1)}, bf16[256,384]{1,0:T(8,128)(2,1)S(1)}, u32[]{:S(2)}, u32[]{:S(2)}) collective-permute-start(bf16[256,384]{1,0:T(8,128)(2,1)S(1)} %copy-done.99), channel_id=1, source_target_pairs={{4,0},{8,4},{12,8},{5,1},{9,5},{13,9},{6,2},{10,6},{14,10},{7,3},{... | collective-permute-start | bytes 589832 | tf_op jit(solution)/shard_map/ppermute | solution.py:633
  264.5 12.0 %collective-permute-start.37 = (bf16[256,384]{1,0:T(8,128)(2,1)S(1)}, bf16[256,384]{1,0:T(8,128)(2,1)S(1)}, u32[]{:S(2)}, u32[]{:S(2)}) collective-permute-start(bf16[256,384]{1,0:T(8,128)(2,1)S(1)} %copy-done.98), channel_id=1, source_target_pairs={{8,0},{12,4},{9,1},{13,5},{10,2},{14,6},{11,3},{15,7},{24,16},{28,... | collective-permute-start | bytes 589832 | tf_op jit(solution)/shard_map/ppermute | solution.py:633
  283.2 18.5 %collective-permute-start.53 = (bf16[2,1,288,128]{3,2,1,0:T(8,128)(2,1)}, bf16[2,1,288,128]{3,2,1,0:T(8,128)(2,1)S(1)}, u32[]{:S(2)}, u32[]{:S(2)}) collective-permute-start(bf16[2,1,288,128]{3,2,1,0:T(8,128)(2,1)} %dynamic-slice_bitcast_fusion.11.refs_17_), channel_id=1, source_target_pairs={{0,1},{1,0},{2,3},{3,2},{4,5},{5,4},{6,7},{7,6},{8,9},{9,8},{10,11... | collective-permute-start | bytes 442376 | tf_op jit(solution)/shard_map/ppermute | solution.py:628
  284.7 19.2 %collective-permute-start.55 = (bf16[2,1,288,128]{3,2,1,0:T(8,128)(2,1)S(1)}, bf16[2,1,288,128]{3,2,1,0:T(8,128)(2,1)S(1)}, u32[]{:S(2)}, u32[]{:S(2)}) collective-permute-start(bf16[2,1,288,128]{3,2,1,0:T(8,128)(2,1)S(1)} %copy-done.86), channel_id=1, source_target_pairs={{0,2},{1,3},{2,0},{3,1},{4,6},{5,7},{6,4},{7,5},{8,10},{9,11},{10,... | collective-permute-start | bytes 442376 | tf_op jit(solution)/shard_map/ppermute | solution.py:628
  285.4 12.5 %collective-permute-start.48 = (bf16[1,1408,128]{2,1,0:T(8,128)(2,1)S(1)}, bf16[1,1408,128]{2,1,0:T(8,128)(2,1)S(1)}, u32[]{:S(2)}, u32[]{:S(2)}) collective-permute-start(bf16[1,1408,128]{2,1,0:T(8,128)(2,1)S(1)} %copy-done.79), channel_id=1, source_target_pairs={{0,1},{1,0},{2,3},{3,2},{4,5},{5,4},{6,7},{7,6},{8,9},{9,8},{10,11... | collective-permute-start | bytes 1081352 | tf_op jit(solution)/shard_map/ppermute | solution.py:628
  285.9 14.3 %collective-permute-start.47 = (bf16[1,1728,128]{2,1,0:T(8,128)(2,1)S(1)}, bf16[1,1728,128]{2,1,0:T(8,128)(2,1)S(1)}, u32[]{:S(2)}, u32[]{:S(2)}) collective-permute-start(bf16[1,1728,128]{2,1,0:T(8,128)(2,1)S(1)} %copy-done.78), channel_id=1, source_target_pairs={{0,2},{1,3},{2,0},{3,1},{4,6},{5,7},{6,4},{7,5},{8,10},{9,11},{10,... | collective-permute-start | bytes 1327112 | tf_op jit(solution)/shard_map/ppermute | solution.py:628
  288.8 16.0 %collective-permute-start.46 = (bf16[2,1,288,128]{3,2,1,0:T(8,128)(2,1)S(1)}, bf16[2,1,288,128]{3,2,1,0:T(8,128)(2,1)S(1)}, u32[]{:S(2)}, u32[]{:S(2)}) collective-permute-start(bf16[2,1,288,128]{3,2,1,0:T(8,128)(2,1)S(1)} %dynamic-slice_bitcast_fusion.9), channel_id=1, source_target_pairs={{0,1},{1,0},{2,3},{3,2},{4,5},{5,4},{6,7},{7,6},{8,9},{9,8},{10,11... | collective-permute-start | bytes 442376 | tf_op jit(solution)/shard_map/ppermute | solution.py:628
  301.6 10.9 %collective-permute-start.50 = (bf16[1568,128]{1,0:T(8,128)(2,1)S(1)}, bf16[1568,128]{1,0:T(8,128)(2,1)S(1)}, u32[]{:S(2)}, u32[]{:S(2)}) collective-permute-start(bf16[1568,128]{1,0:T(8,128)(2,1)S(1)} %fusion.13), channel_id=1, source_target_pairs={{0,4},{4,0},{8,12},{12,8},{1,5},{5,1},{9,13},{13,9},{2,6},{6,2},{1... | collective-permute-start | bytes 1204232 | tf_op jit(solution)/shard_map/ppermute | solution.py:628
  301.8 12.4 %collective-permute-start.54 = (bf16[1,288,128]{2,1,0:T(8,128)(2,1)S(1)}, bf16[1,288,128]{2,1,0:T(8,128)(2,1)S(1)}, u32[]{:S(2)}, u32[]{:S(2)}) collective-permute-start(bf16[1,288,128]{2,1,0:T(8,128)(2,1)S(1)} %dynamic-slice_bitcast_fusion.13), channel_id=1, source_target_pairs={{0,2},{1,3},{2,0},{3,1},{4,6},{5,7},{6,4},{7,5},{8,10},{9,11},{10,... | collective-permute-start | bytes 221192 | tf_op jit(solution)/shard_map/ppermute | solution.py:628
  304.0 10.8 %collective-permute-start.56 = (bf16[1,288,128]{2,1,0:T(8,128)(2,1)S(1)}, bf16[1,288,128]{2,1,0:T(8,128)(2,1)S(1)}, u32[]{:S(2)}, u32[]{:S(2)}) collective-permute-start(bf16[1,288,128]{2,1,0:T(8,128)(2,1)S(1)} %dynamic-slice_bitcast_fusion.12), channel_id=1, source_target_pairs={{0,1},{1,0},{2,3},{3,2},{4,5},{5,4},{6,7},{7,6},{8,9},{9,8},{10,11... | collective-permute-start | bytes 221192 | tf_op jit(solution)/shard_map/ppermute | solution.py:628
  308.5 11.0 %collective-permute-start.44 = (bf16[256,576]{1,0:T(8,128)(2,1)S(1)}, bf16[256,576]{1,0:T(8,128)(2,1)S(1)}, u32[]{:S(2)}, u32[]{:S(2)}) collective-permute-start(bf16[256,576]{1,0:T(8,128)(2,1)S(1)} %broadcast_select_fusion.8), channel_id=1, source_target_pairs={{0,16},{16,0},{1,17},{17,1},{2,18},{18,2},{3,19},{19,3},{4,20},{20... | collective-permute-start | bytes 884744 | tf_op jit(solution)/shard_map/ppermute | solution.py:628
  308.6 33.3 %collective-permute-start.63 = (bf16[1568,128]{1,0:T(8,128)(2,1)S(1)}, bf16[1568,128]{1,0:T(8,128)(2,1)S(1)}, u32[]{:S(2)}, u32[]{:S(2)}) collective-permute-start(bf16[1568,128]{1,0:T(8,128)(2,1)S(1)} %copy-done.69), channel_id=1, source_target_pairs={{0,4},{4,0},{8,12},{12,8},{1,5},{5,1},{9,13},{13,9},{2,6},{6,2},{1... | collective-permute-start | bytes 1204232 | tf_op jit(solution)/shard_map/ppermute | solution.py:628
  314.8 19.2 %collective-permute-start.59 = (bf16[1568,128]{1,0:T(8,128)(2,1)S(1)}, bf16[1568,128]{1,0:T(8,128)(2,1)S(1)}, u32[]{:S(2)}, u32[]{:S(2)}) collective-permute-start(bf16[1568,128]{1,0:T(8,128)(2,1)S(1)} %fusion.6), channel_id=1, source_target_pairs={{0,8},{4,12},{8,0},{12,4},{1,9},{5,13},{9,1},{13,5},{2,10},{6,14},... | collective-permute-start | bytes 1204232 | tf_op jit(solution)/shard_map/ppermute | solution.py:628
  319.2 12.3 %collective-permute-start.57 = (bf16[576,128]{1,0:T(8,128)(2,1)S(1)}, bf16[576,128]{1,0:T(8,128)(2,1)S(1)}, u32[]{:S(2)}, u32[]{:S(2)}) collective-permute-start(bf16[576,128]{1,0:T(8,128)(2,1)S(1)} %fusion.22), channel_id=1, source_target_pairs={{0,4},{4,0},{8,12},{12,8},{1,5},{5,1},{9,13},{13,9},{2,6},{6,2},{1... | collective-permute-start | bytes 442376 | tf_op jit(solution)/shard_map/ppermute | solution.py:628
  332.0 9.6 %collective-permute-start.58 = (bf16[576,128]{1,0:T(8,128)(2,1)S(1)}, bf16[576,128]{1,0:T(8,128)(2,1)S(1)}, u32[]{:S(2)}, u32[]{:S(2)}) collective-permute-start(bf16[576,128]{1,0:T(8,128)(2,1)S(1)} %add_convert_fusion.7), channel_id=1, source_target_pairs={{0,8},{4,12},{8,0},{12,4},{1,9},{5,13},{9,1},{13,5},{2,10},{6,14},... | collective-permute-start | bytes 442376 | tf_op jit(solution)/shard_map/ppermute | solution.py:628
  341.9 11.4 %collective-permute-start.62 = (bf16[1568,128]{1,0:T(8,128)(2,1)S(1)}, bf16[1568,128]{1,0:T(8,128)(2,1)S(1)}, u32[]{:S(2)}, u32[]{:S(2)}) collective-permute-start(bf16[1568,128]{1,0:T(8,128)(2,1)S(1)} %add_convert_fusion.4), channel_id=1, source_target_pairs={{0,4},{4,0},{8,12},{12,8},{1,5},{5,1},{9,13},{13,9},{2,6},{6,2},{1... | collective-permute-start | bytes 1204232 | tf_op jit(solution)/shard_map/ppermute | solution.py:628
  (117 other events, 1152.3 us)

commit v5 on v4

--- a/solution.py
+++ b/solution.py
@@ -465,6 +465,7 @@
         [],
         (idx, zero, one, got),
         1000,
+        limit=24,
     )
 
 
@@ -499,6 +500,7 @@
         [],
         (idx, zero, one, got),
         1000,
+        limit=24,
     )
 
 

time: 368 us -> 367 us (level)
    unnamed x203 -> x201, local copies, waits for them, and re-layouts: 18.7 us -> 18.2 us
  transfers between devices with their start and end apart: 65 -> 65, of which waited for: 30 -> 29; matrix products, arithmetic and copies ran while one was open for 13% -> 13% of each run, Pallas kernels for 18% -> 18%
where the time goes in v5:
time: 367 us; the launch traced here: 362 us
  waiting for transfers between devices  122 us (33%)
  Pallas kernels  97.5 us (27%)
  starting transfers between devices  68.1 us (19%)
  other arithmetic  42 us (11%)
  local copies, waits for them, and re-layouts  29.3 us (8%)
    pallas_call x16, Pallas kernels, call(): pl.pallas_call(kernel, out_shape=tuple(outs), in_specs=in_specs, out_spec...  97.5 us
    ppermute x53, waiting for transfers between devices, crossed(): return lax.ppermute(value, axis, [(i, i ^ mask) for i in range(count)])  79.4 us
    ppermute x12, waiting for transfers between devices, shifted(): lax.ppermute(value, 'ctx', [(i, i + distance) for i in devices if i + dis...  42.4 us
    ppermute x53, starting transfers between devices, crossed(): return lax.ppermute(value, axis, [(i, i ^ mask) for i in range(count)])  37.3 us
    ppermute x12, starting transfers between devices, shifted(): lax.ppermute(value, 'ctx', [(i, i + distance) for i in devices if i + dis...  30.7 us
    unnamed x201, local copies, waits for them, and re-layouts  18.2 us
    convert_element_type x4, other arithmetic, joined(): return (mine.astype(F32) + got.astype(F32)).astype(BF)  8 us
    select_n x8, other arithmetic, pick(): return jnp.where(first, a, b)  7.44 us
  transfers between devices with their start and end apart: 65, of which 29 were waited for; matrix products, arithmetic and copies ran while one was open for 13% of the time, Pallas kernels for 18%

profile of v5, /device:TPU:0, one launch (start us, length us, event | category | flops | bytes accessed | tf_op | source)
XLA Modules:
  0.0 361.5 jit_solution(18160565227940997896)
XLA Ops:
  2.6 3.0 collective-permute-start.4
  18.2 8.4 %collective-permute-done.5 = bf16[2,144,896]{2,1,0:T(8,128)(2,1)S(1)} collective-permute-done((bf16[2,144,896]{2,1,0:T(8,128)(2,1)S(1)}, bf16[2,144,896]{2,1,0:T(8,128)(2,1)S(1)}, u32[]{:S(2)}, u32[]{:S(2)}) %collective-permute-start.5) | collective-permute-done | bytes 516128 | tf_op jit(solution)/shard_map/ppermute | solution.py:630
  29.4 2.3 broadcast_select_fusion.10
  31.6 2.0 bitcast_select_fusion
  39.5 2.8 shard_map.203
  44.6 6.7 %collective-permute-done.6 = bf16[144,1536]{1,0:T(8,128)(2,1)S(1)} collective-permute-done((bf16[144,1536]{1,0:T(8,128)(2,1)}, bf16[144,1536]{1,0:T(8,128)(2,1)S(1)}, u32[]{:S(2)}, u32[]{:S(2)}) %collective-permute-start.6) | collective-permute-done | bytes 442400 | tf_op jit(solution)/shard_map/ppermute | solution.py:630
  53.0 3.5 collective-permute-start.12
  56.5 4.5 %collective-permute-start.13 = (bf16[256,384]{1,0:T(8,128)(2,1)S(1)}, bf16[256,384]{1,0:T(8,128)(2,1)S(1)}, u32[]{:S(2)}, u32[]{:S(2)}) collective-permute-start(bf16[256,384]{1,0:T(8,128)(2,1)S(1)} %get-tuple-element.126.refs_2_.refs_4_), channel_id=1, source_target_pairs={{0,8},{4,12},{1,9},{5,13},{2,10},{6,14},{3,11},{7,15},{16,24},{20,... | collective-permute-start | bytes 589832 | tf_op jit(solution)/shard_map/ppermute | solution.py:635
  62.5 3.4 collective-permute-done.13.refs_4_.refs_6_
  65.9 2.1 collective-permute-done.14.refs_5_.refs_7_
  68.0 7.0 %shard_map.204 = (bf16[256,576]{1,0:T(8,128)(2,1)S(1)}, f32[16,256]{1,0:T(8,128)S(1)}) custom-call(s32[2]{0:T(128)S(1)} %pad_add_fusion.refs_0_, bf16[256,576]{1,0:T(8,128)(2,1)S(1)} %get-tuple-element.125.refs_1_, bf16[256,384]{1,0:T(8,128)(2,1)S(1)} %get-tuple-element.126.refs_2_.refs_4_, bf16[256,384]{1,0:T(8,128)(2,1)S(1)} %collective-permute-done.12.refs_3_.refs_5_, ...), custom_call_target="tpu_custom_call" | custom-call | flops 2415919 | bytes 1392 | tf_op jit(solution)/shard_map/pallas_call | solution.py:56
  79.1 2.1 collective-permute-done.16.refs_8_
  81.3 6.4 %shard_map.205 = (bf16[256,576]{1,0:T(8,128)(2,1)S(1)}, f32[256,576]{1,0:T(8,128)S(1)}, bf16[256,576]{1,0:T(8,128)(2,1)S(1)}, f32[256,1536]{1,0:T(8,128)S(1)}, f...) custom-call(s32[2]{0:T(128)S(1)} %pad_add_fusion.refs_0_, bf16[256,576]{1,0:T(8,128)(2,1)S(1)} %bitcast.229, ...), custom_call_target="tpu_custom_call" | custom-call | flops 1528823 | bytes 13271 | tf_op jit(solution)/shard_map/pallas_call | solution.py:56
  88.6 3.9 %shard_map.206 = (bf16[256,576]{1,0:T(8,128)(2,1)S(1)}, bf16[256,576]{1,0:T(8,128)(2,1)S(1)}, bf16[256,384]{1,0:T(8,128)(2,1)S(1)}) custom-call(s32[2]{0:T(128)S(1)} %pad_add_fusion.refs_0_, bf16[256,576]{1,0:T(8,128)(2,1)S(1)} %get-tuple-element.200.refs_1_, bf16[576,896]{1,0:T(8,128)(2,1)S(1)} %bitcast.215, ...), custom_call_target="tpu_custom_call" | custom-call | flops 452984 | bytes 5472 | tf_op jit(solution)/shard_map/pallas_call | solution.py:56
  95.4 6.4 %collective-permute-start.21 = (bf16[256,384]{1,0:T(8,128)(2,1)S(1)}, bf16[256,384]{1,0:T(8,128)(2,1)S(1)}, u32[]{:S(2)}, u32[]{:S(2)}) collective-permute-start(bf16[256,384]{1,0:T(8,128)(2,1)S(1)} %get-tuple-element.140.refs_2_.refs_4_), channel_id=1, source_target_pairs={{0,4},{4,8},{8,12},{1,5},{5,9},{9,13},{2,6},{6,10},{10,14},{3,7},{... | collective-permute-start | bytes 589832 | tf_op jit(solution)/shard_map/ppermute | solution.py:635
  101.8 5.3 %collective-permute-start.22 = (bf16[256,384]{1,0:T(8,128)(2,1)S(1)}, bf16[256,384]{1,0:T(8,128)(2,1)S(1)}, u32[]{:S(2)}, u32[]{:S(2)}) collective-permute-start(bf16[256,384]{1,0:T(8,128)(2,1)S(1)} %get-tuple-element.140.refs_2_.refs_4_), channel_id=1, source_target_pairs={{0,8},{4,12},{1,9},{5,13},{2,10},{6,14},{3,11},{7,15},{16,24},{20,... | collective-permute-start | bytes 589832 | tf_op jit(solution)/shard_map/ppermute | solution.py:635
  108.8 2.9 collective-permute-done.22.refs_4_.refs_6_
  111.8 2.1 collective-permute-done.23.refs_5_.refs_7_
  113.9 7.0 %shard_map.207 = (bf16[256,576]{1,0:T(8,128)(2,1)S(1)}, f32[16,256]{1,0:T(8,128)S(1)}) custom-call(s32[2]{0:T(128)S(1)} %pad_add_fusion.refs_0_, bf16[256,576]{1,0:T(8,128)(2,1)S(1)} %get-tuple-element.139.refs_1_, bf16[256,384]{1,0:T(8,128)(2,1)S(1)} %get-tuple-element.140.refs_2_.refs_4_, bf16[256,384]{1,0:T(8,128)(2,1)S(1)} %collective-permute-done.21.refs_3_.refs_5_, ...), custom_call_target="tpu_custom_call" | custom-call | flops 2415919 | bytes 1392 | tf_op jit(solution)/shard_map/pallas_call | solution.py:56
  125.6 2.5 collective-permute-done.25.refs_8_
  129.7 6.6 %shard_map.208 = (bf16[256,576]{1,0:T(8,128)(2,1)S(1)}, f32[256,576]{1,0:T(8,128)S(1)}, bf16[256,576]{1,0:T(8,128)(2,1)S(1)}, f32[256,1536]{1,0:T(8,128)S(1)}, f...) custom-call(s32[2]{0:T(128)S(1)} %copy-done.57, bf16[256,576]{1,0:T(8,128)(2,1)S(1)} %get-tuple-element.200.refs_1_, ...), custom_call_target="tpu_custom_call" | custom-call | flops 1528823 | bytes 13271 | tf_op jit(solution)/shard_map/pallas_call | solution.py:56
  136.3 8.1 %shard_map.209 = (bf16[256,1536]{1,0:T(8,128)(2,1)S(1)}, bf16[256,1536]{1,0:T(8,128)(2,1)S(1)}, f32[256,576]{1,0:T(8,128)S(1)}, bf16[256,576]{1,0:T(8,128)(2,1)S...) custom-call(s32[2]{0:T(128)S(1)} %copy-done.57, bf16[256,576]{1,0:T(8,128)(2,1)S(1)} %bitcast.230, ...), custom_call_target="tpu_custom_call" | custom-call | flops 1528823 | bytes 14499 | tf_op jit(solution)/shard_map/pallas_call | solution.py:56
  146.0 4.3 %shard_map.210 = (bf16[4,3136,128]{2,1,0:T(8,128)(2,1)S(1)}, bf16[4,3136,128]{2,1,0:T(8,128)(2,1)}) custom-call(s32[2]{0:T(128)S(1)} %copy-done.57, bf16[256,1536]{1,0:T(8,128)(2,1)S(1)} %get-tuple-element.151.refs_1_, bf16[256,576]{1,0:T(8,128)(2,1)S(1)} %bitcast.231, bf16[256,576]{1,0:T(8,128)(2,1)S(1)} %get-tuple-element.152.refs_3_, ...), custom_call_target="tpu_custom_call" | custom-call | flops 1528823 | bytes 10108 | tf_op jit(solution)/shard_map/pallas_call | solution.py:56
  152.1 11.4 %shard_map.211 = (f32[256,576]{1,0:T(8,128)}, f32[256,384]{1,0:T(8,128)}, bf16[256,384]{1,0:T(8,128)(2,1)}, bf16[256,384]{1,0:T(8,128)(2,1)}, bf16[256,384]{1,0:T(8,128)(2,1)}) custom-call(s32[2]{0:T(128)} %copy-done.56, bf16[256,576]{1,0:T(8,128)(2,1)} %copy-done.29, bf16[256,576]{1,0:T(8,128)(2,1)} %copy-done.53, f32[16,256]{1,0:T(8,128)} %copy-done.61, ...), custom_call_target="tpu_custom_call" | custom-call | flops 6039797 | bytes 2965 | tf_op jit(solution)/shard_map/pallas_call | solution.py:56
  165.2 2.7 add_convert_fusion.1
  178.4 4.7 %collective-permute-done.26.refs_5_ = bf16[256,384]{1,0:T(8,128)(2,1)S(1)} collective-permute-done((bf16[256,384]{1,0:T(8,128)(2,1)}, bf16[256,384]{1,0:T(8,128)(2,1)S(1)}, u32[]{:S(2)}, u32[]{:S(2)}) %collective-permute-start.26) | collective-permute-done | bytes 196640 | tf_op jit(solution)/shard_map/ppermute | solution.py:635
  183.1 13.9 %collective-permute-done.27.refs_6_ = bf16[256,384]{1,0:T(8,128)(2,1)} collective-permute-done((bf16[256,384]{1,0:T(8,128)(2,1)}, bf16[256,384]{1,0:T(8,128)(2,1)}, u32[]{:S(2)}, u32[]{:S(2)}) %collective-permute-start.27) | collective-permute-done | bytes 196640 | tf_op jit(solution)/shard_map/ppermute | solution.py:635
  197.1 6.8 %shard_map.212 = (bf16[256,576]{1,0:T(8,128)(2,1)}, bf16[4,576,128]{2,1,0:T(8,128)(2,1)}, bf16[4,576,128]{2,1,0:T(8,128)(2,1)}) custom-call(s32[2]{0:T(128)} %copy-done.56, bf16[256,576]{1,0:T(8,128)(2,1)} %copy-done.11, bf16[256,576]{1,0:T(8,128)(2,1)} %copy-done.52, f32[256,576]{1,0:T(8,128)} %get-tuple-element.158.refs_3_, ...), custom_call_target="tpu_custom_call" | custom-call | flops 905969 | bytes 8617 | tf_op jit(solution)/shard_map/pallas_call | solution.py:56
  208.5 8.1 %shard_map.213 = (bf16[256,1536]{1,0:T(8,128)(2,1)S(1)}, bf16[256,1536]{1,0:T(8,128)(2,1)S(1)}, f32[256,576]{1,0:T(8,128)S(1)}, bf16[256,576]{1,0:T(8,128)(2,1)S...) custom-call(s32[2]{0:T(128)S(1)} %copy-done.58, bf16[256,576]{1,0:T(8,128)(2,1)S(1)} %copy-done.14, ...), custom_call_target="tpu_custom_call" | custom-call | flops 1528823 | bytes 14499 | tf_op jit(solution)/shard_map/pallas_call | solution.py:56
  220.4 4.2 %shard_map.214 = (bf16[4,3136,128]{2,1,0:T(8,128)(2,1)S(1)}, bf16[4,3136,128]{2,1,0:T(8,128)(2,1)}) custom-call(s32[2]{0:T(128)S(1)} %copy-done.58, bf16[256,1536]{1,0:T(8,128)(2,1)S(1)} %copy-done.41, bf16[256,576]{1,0:T(8,128)(2,1)S(1)} %copy-done.14, bf16[256,576]{1,0:T(8,128)(2,1)S(1)} %copy-done.51, bf16[256,1536]{1,0:T(8,128)(2,1)S(1)} %get-tuple-element.176.refs_4_, ...), custom_call_target="tpu_custom_call" | custom-call | flops 1528823 | bytes 10108 | tf_op jit(solution)/shard_map/pallas_call | solution.py:56
  226.8 6.4 %collective-permute-done.34 = bf16[4,3136,128]{2,1,0:T(8,128)(2,1)} collective-permute-done((bf16[4,3136,128]{2,1,0:T(8,128)(2,1)}, bf16[4,3136,128]{2,1,0:T(8,128)(2,1)}, u32[]{:S(2)}, u32[]{:S(2)}) %collective-permute-start.34) | collective-permute-done | bytes 3211296 | tf_op jit(solution)/shard_map/ppermute | solution.py:630
  233.2 3.7 %add_convert_fusion = bf16[4,3136,128]{2,1,0:T(8,128)(2,1)S(1)} fusion(bf16[4,3136,128]{2,1,0:T(8,128)(2,1)} %collective-permute-done.34, bf16[4,3136,128]{2,1,0:T(8,128)(2,1)} %copy-done.21), kind=kLoop, calls=%fused_computation | loop fusion | flops 6422528 | bytes 9633792 | tf_op jit(solution)/shard_map/convert_element_type | solution.py:844
  241.6 11.0 %shard_map.215 = (f32[256,576]{1,0:T(8,128)}, f32[256,384]{1,0:T(8,128)}, bf16[256,384]{1,0:T(8,128)(2,1)}, bf16[256,384]{1,0:T(8,128)(2,1)}, bf16[256,384]{1,0:T(8,128)(2,1)}) custom-call(s32[2]{0:T(128)} %copy-done.56, bf16[256,576]{1,0:T(8,128)(2,1)} %copy-done.35, bf16[256,576]{1,0:T(8,128)(2,1)} %copy-done.54, f32[16,256]{1,0:T(8,128)} %copy-done.60, ...), custom_call_target="tpu_custom_call" | custom-call | flops 6039797 | bytes 2965 | tf_op jit(solution)/shard_map/pallas_call | solution.py:56
  256.9 7.6 %collective-permute-done.38.refs_7_ = bf16[256,384]{1,0:T(8,128)(2,1)S(1)} collective-permute-done((bf16[256,384]{1,0:T(8,128)(2,1)}, bf16[256,384]{1,0:T(8,128)(2,1)S(1)}, u32[]{:S(2)}, u32[]{:S(2)}) %collective-permute-start.38) | collective-permute-done | bytes 196640 | tf_op jit(solution)/shard_map/ppermute | solution.py:635
  270.9 5.6 %collective-permute-done.37.refs_6_ = bf16[256,384]{1,0:T(8,128)(2,1)S(1)} collective-permute-done((bf16[256,384]{1,0:T(8,128)(2,1)S(1)}, bf16[256,384]{1,0:T(8,128)(2,1)S(1)}, u32[]{:S(2)}, u32[]{:S(2)}) %collective-permute-start.37) | collective-permute-done | bytes 196640 | tf_op jit(solution)/shard_map/ppermute | solution.py:635
  277.2 5.9 %shard_map.216 = (bf16[256,576]{1,0:T(8,128)(2,1)}, bf16[4,576,128]{2,1,0:T(8,128)(2,1)}, bf16[4,576,128]{2,1,0:T(8,128)(2,1)}) custom-call(s32[2]{0:T(128)} %copy-done.56, bf16[256,576]{1,0:T(8,128)(2,1)} %bitcast.228, bf16[256,576]{1,0:T(8,128)(2,1)} %copy-done.55, f32[256,576]{1,0:T(8,128)} %get-tuple-element.185.refs_3_, ...), custom_call_target="tpu_custom_call" | custom-call | flops 905969 | bytes 8617 | tf_op jit(solution)/shard_map/pallas_call | solution.py:56
  290.4 7.5 %collective-permute-done.48 = bf16[1,1408,128]{2,1,0:T(8,128)(2,1)S(1)} collective-permute-done((bf16[1,1408,128]{2,1,0:T(8,128)(2,1)S(1)}, bf16[1,1408,128]{2,1,0:T(8,128)(2,1)S(1)}, u32[]{:S(2)}, u32[]{:S(2)}) %collective-permute-start.48) | collective-permute-done | bytes 360480 | tf_op jit(solution)/shard_map/ppermute | solution.py:630
  298.0 2.2 collective-permute-done.47
  304.9 3.6 %collective-permute-done.51 = bf16[2,1,288,128]{3,2,1,0:T(8,128)(2,1)S(1)} collective-permute-done((bf16[2,1,288,128]{3,2,1,0:T(8,128)(2,1)S(1)}, bf16[2,1,288,128]{3,2,1,0:T(8,128)(2,1)S(1)}, u32[]{:S(2)}, u32[]{:S(2)}) %collective-permute-start.51) | collective-permute-done | bytes 147488 | tf_op jit(solution)/shard_map/ppermute | solution.py:630
  310.5 2.1 collective-permute-done.50
  314.9 2.0 collective-permute-done.49
  319.7 11.8 %collective-permute-done.57 = bf16[576,128]{1,0:T(8,128)(2,1)S(1)} collective-permute-done((bf16[576,128]{1,0:T(8,128)(2,1)S(1)}, bf16[576,128]{1,0:T(8,128)(2,1)S(1)}, u32[]{:S(2)}, u32[]{:S(2)}) %collective-permute-start.57) | collective-permute-done | bytes 147488 | tf_op jit(solution)/shard_map/ppermute | solution.py:630
  334.2 7.4 %collective-permute-done.58 = bf16[576,128]{1,0:T(8,128)(2,1)S(1)} collective-permute-done((bf16[576,128]{1,0:T(8,128)(2,1)S(1)}, bf16[576,128]{1,0:T(8,128)(2,1)S(1)}, u32[]{:S(2)}, u32[]{:S(2)}) %collective-permute-start.58) | collective-permute-done | bytes 147488 | tf_op jit(solution)/shard_map/ppermute | solution.py:630
  342.8 2.0 collective-permute-start.62
  344.8 3.7 %collective-permute-done.60 = bf16[576,128]{1,0:T(8,128)(2,1)S(1)} collective-permute-done((bf16[576,128]{1,0:T(8,128)(2,1)S(1)}, bf16[576,128]{1,0:T(8,128)(2,1)S(1)}, u32[]{:S(2)}, u32[]{:S(2)}) %collective-permute-start.60) | collective-permute-done | bytes 147488 | tf_op jit(solution)/shard_map/ppermute | solution.py:630
  351.4 2.7 collective-permute-done.62
  356.6 2.1 copy.53
  358.8 2.6 shard_map.218
  (407 shorter events, 113.6 us)
Async XLA Ops:
  2.6 10.0 %collective-permute-start.4 = (bf16[144,896]{1,0:T(8,128)(2,1)S(1)}, bf16[144,896]{1,0:T(8,128)(2,1)S(1)}, u32[]{:S(2)}, u32[]{:S(2)}) collective-permute-start(bf16[144,896]{1,0:T(8,128)(2,1)S(1)} %pad_maximum_fusion.15), channel_id=1, source_target_pairs={{0,2},{1,3},{2,0},{3,1},{4,6},{5,7},{6,4},{7,5},{8,10},{9,11},{10,... | collective-permute-start | bytes 774152 | tf_op jit(solution)/shard_map/ppermute | solution.py:630
  11.2 18.1 %collective-permute-start.1 = (bf16[192,640]{1,0:T(8,128)(2,1)}, bf16[192,640]{1,0:T(8,128)(2,1)}, u32[]{:S(2)}, u32[]{:S(2)}) collective-permute-start(bf16[192,640]{1,0:T(8,128)(2,1)} %broadcast_select_fusion.12), channel_id=1, source_target_pairs={{0,16},{16,0},{1,17},{17,1},{2,18},{18,2},{3,19},{19,3},{4,20},{20... | collective-permute-start | bytes 737288 | tf_op jit(solution)/shard_map/ppermute | solution.py:630
  12.1 19.6 %collective-permute-start = (bf16[144,1536]{1,0:T(8,128)(2,1)}, bf16[144,1536]{1,0:T(8,128)(2,1)}, u32[]{:S(2)}, u32[]{:S(2)}) collective-permute-start(bf16[144,1536]{1,0:T(8,128)(2,1)} %select_bitcast_fusion.16), channel_id=1, source_target_pairs={{0,16},{16,0},{1,17},{17,1},{2,18},{18,2},{3,19},{19,3},{4,20},{20... | collective-permute-start | bytes 1327112 | tf_op jit(solution)/shard_map/ppermute | solution.py:630
  12.9 13.7 %collective-permute-start.5 = (bf16[2,144,896]{2,1,0:T(8,128)(2,1)S(1)}, bf16[2,144,896]{2,1,0:T(8,128)(2,1)S(1)}, u32[]{:S(2)}, u32[]{:S(2)}) collective-permute-start(bf16[2,144,896]{2,1,0:T(8,128)(2,1)S(1)} %pad_maximum_fusion.11), channel_id=1, source_target_pairs={{0,1},{1,0},{2,3},{3,2},{4,5},{5,4},{6,7},{7,6},{8,9},{9,8},{10,11... | collective-permute-start | bytes 1548296 | tf_op jit(solution)/shard_map/ppermute | solution.py:630
  16.6 12.4 %collective-permute-start.3 = (bf16[2,144,896]{2,1,0:T(8,128)(2,1)S(1)}, bf16[2,144,896]{2,1,0:T(8,128)(2,1)S(1)}, u32[]{:S(2)}, u32[]{:S(2)}) collective-permute-start(bf16[2,144,896]{2,1,0:T(8,128)(2,1)S(1)} %pad_maximum_fusion.10), channel_id=1, source_target_pairs={{0,2},{1,3},{2,0},{3,1},{4,6},{5,7},{6,4},{7,5},{8,10},{9,11},{10,... | collective-permute-start | bytes 1548296 | tf_op jit(solution)/shard_map/ppermute | solution.py:630
  27.0 12.5 %collective-permute-start.8 = (bf16[576,896]{1,0:T(8,128)(2,1)S(1)}, bf16[576,896]{1,0:T(8,128)(2,1)S(1)}, u32[]{:S(2)}, u32[]{:S(2)}) collective-permute-start(bf16[576,896]{1,0:T(8,128)(2,1)S(1)} %bitcast.204), channel_id=1, source_target_pairs={{0,16},{16,0},{1,17},{17,1},{2,18},{18,2},{3,19},{19,3},{4,20},{20... | collective-permute-start | bytes 3096584 | tf_op jit(solution)/shard_map/ppermute | solution.py:630
  29.3 10.3 %collective-permute-start.7 = (bf16[576,896]{1,0:T(8,128)(2,1)S(1)}, bf16[576,896]{1,0:T(8,128)(2,1)}, u32[]{:S(2)}, u32[]{:S(2)}) collective-permute-start(bf16[576,896]{1,0:T(8,128)(2,1)S(1)} %bitcast.213), channel_id=1, source_target_pairs={{0,16},{16,0},{1,17},{17,1},{2,18},{18,2},{3,19},{19,3},{4,20},{20... | collective-permute-start | bytes 3096584 | tf_op jit(solution)/shard_map/ppermute | solution.py:630
  38.0 13.3 %collective-permute-start.6 = (bf16[144,1536]{1,0:T(8,128)(2,1)}, bf16[144,1536]{1,0:T(8,128)(2,1)S(1)}, u32[]{:S(2)}, u32[]{:S(2)}) collective-permute-start(bf16[144,1536]{1,0:T(8,128)(2,1)} %get-tuple-element.120), channel_id=1, source_target_pairs={{0,1},{1,0},{2,3},{3,2},{4,5},{5,4},{6,7},{7,6},{8,9},{9,8},{10,11... | collective-permute-start | bytes 1327112 | tf_op jit(solution)/shard_map/ppermute | solution.py:630
  43.8 31.2 %collective-permute-start.11 = (bf16[2,192,640]{2,1,0:T(8,128)(2,1)S(1)}, bf16[2,192,640]{2,1,0:T(8,128)(2,1)S(1)}, u32[]{:S(2)}, u32[]{:S(2)}) collective-permute-start(bf16[2,192,640]{2,1,0:T(8,128)(2,1)S(1)} %pad_maximum_fusion.12), channel_id=1, source_target_pairs={{0,1},{1,0},{2,3},{3,2},{4,5},{5,4},{6,7},{7,6},{8,9},{9,8},{10,11... | collective-permute-start | bytes 1474568 | tf_op jit(solution)/shard_map/ppermute | solution.py:630
  51.5 24.3 %collective-permute-start.9 = (bf16[2,144,1536]{2,1,0:T(8,128)(2,1)S(1)}, bf16[2,144,1536]{2,1,0:T(8,128)(2,1)S(1)}, u32[]{:S(2)}, u32[]{:S(2)}) collective-permute-start(bf16[2,144,1536]{2,1,0:T(8,128)(2,1)S(1)} %pad_maximum_fusion.6), channel_id=1, source_target_pairs={{0,2},{1,3},{2,0},{3,1},{4,6},{5,7},{6,4},{7,5},{8,10},{9,11},{10,... | collective-permute-start | bytes 2654216 | tf_op jit(solution)/shard_map/ppermute | solution.py:630
  53.0 9.5 %collective-permute-start.12 = (bf16[256,384]{1,0:T(8,128)(2,1)S(1)}, bf16[256,384]{1,0:T(8,128)(2,1)S(1)}, u32[]{:S(2)}, u32[]{:S(2)}) collective-permute-start(bf16[256,384]{1,0:T(8,128)(2,1)S(1)} %get-tuple-element.126.refs_2_.refs_4_), channel_id=1, source_target_pairs={{0,4},{4,8},{8,12},{1,5},{5,9},{9,13},{2,6},{6,10},{10,14},{3,7},{... | collective-permute-start | bytes 589832 | tf_op jit(solution)/shard_map/ppermute | solution.py:635
  56.5 9.5 %collective-permute-start.13 = (bf16[256,384]{1,0:T(8,128)(2,1)S(1)}, bf16[256,384]{1,0:T(8,128)(2,1)S(1)}, u32[]{:S(2)}, u32[]{:S(2)}) collective-permute-start(bf16[256,384]{1,0:T(8,128)(2,1)S(1)} %get-tuple-element.126.refs_2_.refs_4_), channel_id=1, source_target_pairs={{0,8},{4,12},{1,9},{5,13},{2,10},{6,14},{3,11},{7,15},{16,24},{20,... | collective-permute-start | bytes 589832 | tf_op jit(solution)/shard_map/ppermute | solution.py:635
  77.1 15.4 %collective-permute-start.18 = (bf16[192,640]{1,0:T(8,128)(2,1)S(1)}, bf16[192,640]{1,0:T(8,128)(2,1)S(1)}, u32[]{:S(2)}, u32[]{:S(2)}) collective-permute-start(bf16[192,640]{1,0:T(8,128)(2,1)S(1)} %copy-done.82), channel_id=1, source_target_pairs={{0,1},{1,0},{2,3},{3,2},{4,5},{5,4},{6,7},{7,6},{8,9},{9,8},{10,11... | collective-permute-start | bytes 737288 | tf_op jit(solution)/shard_map/ppermute | solution.py:630
  78.6 14.0 %collective-permute-start.17 = (bf16[144,1536]{1,0:T(8,128)(2,1)S(1)}, bf16[144,1536]{1,0:T(8,128)(2,1)S(1)}, u32[]{:S(2)}, u32[]{:S(2)}) collective-permute-start(bf16[144,1536]{1,0:T(8,128)(2,1)S(1)} %copy-done.77), channel_id=1, source_target_pairs={{0,2},{1,3},{2,0},{3,1},{4,6},{5,7},{6,4},{7,5},{8,10},{9,11},{10,... | collective-permute-start | bytes 1327112 | tf_op jit(solution)/shard_map/ppermute | solution.py:630
  93.3 27.6 %collective-permute-start.20 = (bf16[2,192,640]{2,1,0:T(8,128)(2,1)S(1)}, bf16[2,192,640]{2,1,0:T(8,128)(2,1)S(1)}, u32[]{:S(2)}, u32[]{:S(2)}) collective-permute-start(bf16[2,192,640]{2,1,0:T(8,128)(2,1)S(1)} %pad_maximum_fusion.13), channel_id=1, source_target_pairs={{0,2},{1,3},{2,0},{3,1},{4,6},{5,7},{6,4},{7,5},{8,10},{9,11},{10,... | collective-permute-start | bytes 1474568 | tf_op jit(solution)/shard_map/ppermute | solution.py:630
  93.9 27.7 %collective-permute-start.19 = (bf16[2,144,1536]{2,1,0:T(8,128)(2,1)S(1)}, bf16[2,144,1536]{2,1,0:T(8,128)(2,1)S(1)}, u32[]{:S(2)}, u32[]{:S(2)}) collective-permute-start(bf16[2,144,1536]{2,1,0:T(8,128)(2,1)S(1)} %pad_maximum_fusion.7), channel_id=1, source_target_pairs={{0,1},{1,0},{2,3},{3,2},{4,5},{5,4},{6,7},{7,6},{8,9},{9,8},{10,11... | collective-permute-start | bytes 2654216 | tf_op jit(solution)/shard_map/ppermute | solution.py:630
  95.4 13.4 %collective-permute-start.21 = (bf16[256,384]{1,0:T(8,128)(2,1)S(1)}, bf16[256,384]{1,0:T(8,128)(2,1)S(1)}, u32[]{:S(2)}, u32[]{:S(2)}) collective-permute-start(bf16[256,384]{1,0:T(8,128)(2,1)S(1)} %get-tuple-element.140.refs_2_.refs_4_), channel_id=1, source_target_pairs={{0,4},{4,8},{8,12},{1,5},{5,9},{9,13},{2,6},{6,10},{10,14},{3,7},{... | collective-permute-start | bytes 589832 | tf_op jit(solution)/shard_map/ppermute | solution.py:635
  101.8 10.0 %collective-permute-start.22 = (bf16[256,384]{1,0:T(8,128)(2,1)S(1)}, bf16[256,384]{1,0:T(8,128)(2,1)S(1)}, u32[]{:S(2)}, u32[]{:S(2)}) collective-permute-start(bf16[256,384]{1,0:T(8,128)(2,1)S(1)} %get-tuple-element.140.refs_2_.refs_4_), channel_id=1, source_target_pairs={{0,8},{4,12},{1,9},{5,13},{2,10},{6,14},{3,11},{7,15},{16,24},{20,... | collective-permute-start | bytes 589832 | tf_op jit(solution)/shard_map/ppermute | solution.py:635
  151.9 11.6 %collective-permute-start.29 = (bf16[4,3136,128]{2,1,0:T(8,128)(2,1)}, bf16[4,3136,128]{2,1,0:T(8,128)(2,1)S(1)}, u32[]{:S(2)}, u32[]{:S(2)}) collective-permute-start(bf16[4,3136,128]{2,1,0:T(8,128)(2,1)} %get-tuple-element.164), channel_id=1, source_target_pairs={{0,16},{16,0},{1,17},{17,1},{2,18},{18,2},{3,19},{19,3},{4,20},{20... | collective-permute-start | bytes 9633800 | tf_op jit(solution)/shard_map/ppermute | solution.py:630
  170.1 33.8 %collective-permute-start.31 = (bf16[2,1,1408,128]{3,2,1,0:T(8,128)(2,1)}, bf16[2,1,1408,128]{3,2,1,0:T(8,128)(2,1)}, u32[]{:S(2)}, u32[]{:S(2)}) collective-permute-start(bf16[2,1,1408,128]{3,2,1,0:T(8,128)(2,1)} %dynamic-slice_bitcast_fusion.3.refs_16_), channel_id=1, source_target_pairs={{0,2},{1,3},{2,0},{3,1},{4,6},{5,7},{6,4},{7,5},{8,10},{9,11},{10,... | collective-permute-start | bytes 2162696 | tf_op jit(solution)/shard_map/ppermute | solution.py:630
  171.7 11.5 %collective-permute-start.26 = (bf16[256,384]{1,0:T(8,128)(2,1)}, bf16[256,384]{1,0:T(8,128)(2,1)S(1)}, u32[]{:S(2)}, u32[]{:S(2)}) collective-permute-start(bf16[256,384]{1,0:T(8,128)(2,1)} %get-tuple-element.160), channel_id=1, source_target_pairs={{4,0},{8,4},{12,8},{5,1},{9,5},{13,9},{6,2},{10,6},{14,10},{7,3},{... | collective-permute-start | bytes 589832 | tf_op jit(solution)/shard_map/ppermute | solution.py:635
  173.0 24.1 %collective-permute-start.27 = (bf16[256,384]{1,0:T(8,128)(2,1)}, bf16[256,384]{1,0:T(8,128)(2,1)}, u32[]{:S(2)}, u32[]{:S(2)}) collective-permute-start(bf16[256,384]{1,0:T(8,128)(2,1)} %get-tuple-element.161), channel_id=1, source_target_pairs={{8,0},{12,4},{9,1},{13,5},{10,2},{14,6},{11,3},{15,7},{24,16},{28,... | collective-permute-start | bytes 589832 | tf_op jit(solution)/shard_map/ppermute | solution.py:635
  174.3 22.8 %collective-permute-start.28 = (bf16[256,384]{1,0:T(8,128)(2,1)}, bf16[256,384]{1,0:T(8,128)(2,1)}, u32[]{:S(2)}, u32[]{:S(2)}) collective-permute-start(bf16[256,384]{1,0:T(8,128)(2,1)} %get-tuple-element.162), channel_id=1, source_target_pairs={{12,0},{13,1},{14,2},{15,3},{28,16},{29,17},{30,18},{31,19}} | collective-permute-start | bytes 589832 | tf_op jit(solution)/shard_map/ppermute | solution.py:635
  177.9 28.2 %collective-permute-start.30 = (bf16[2,1,1728,128]{3,2,1,0:T(8,128)(2,1)}, bf16[2,1,1728,128]{3,2,1,0:T(8,128)(2,1)}, u32[]{:S(2)}, u32[]{:S(2)}) collective-permute-start(bf16[2,1,1728,128]{3,2,1,0:T(8,128)(2,1)} %dynamic-slice_bitcast_fusion.1.refs_15_), channel_id=1, source_target_pairs={{0,1},{1,0},{2,3},{3,2},{4,5},{5,4},{6,7},{7,6},{8,9},{9,8},{10,11... | collective-permute-start | bytes 2654216 | tf_op jit(solution)/shard_map/ppermute | solution.py:630
  205.5 11.2 %collective-permute-start.33 = (bf16[1,1408,128]{2,1,0:T(8,128)(2,1)S(1)}, bf16[1,1408,128]{2,1,0:T(8,128)(2,1)S(1)}, u32[]{:S(2)}, u32[]{:S(2)}) collective-permute-start(bf16[1,1408,128]{2,1,0:T(8,128)(2,1)S(1)} %dynamic-slice_bitcast_fusion.7), channel_id=1, source_target_pairs={{0,1},{1,0},{2,3},{3,2},{4,5},{5,4},{6,7},{7,6},{8,9},{9,8},{10,11... | collective-permute-start | bytes 1081352 | tf_op jit(solution)/shard_map/ppermute | solution.py:630
  207.9 11.0 %collective-permute-start.32 = (bf16[1,1728,128]{2,1,0:T(8,128)(2,1)S(1)}, bf16[1,1728,128]{2,1,0:T(8,128)(2,1)S(1)}, u32[]{:S(2)}, u32[]{:S(2)}) collective-permute-start(bf16[1,1728,128]{2,1,0:T(8,128)(2,1)S(1)} %dynamic-slice_bitcast_fusion.5), channel_id=1, source_target_pairs={{0,2},{1,3},{2,0},{3,1},{4,6},{5,7},{6,4},{7,5},{8,10},{9,11},{10,... | collective-permute-start | bytes 1327112 | tf_op jit(solution)/shard_map/ppermute | solution.py:630
  226.3 27.7 %collective-permute-start.41 = (bf16[4,576,128]{2,1,0:T(8,128)(2,1)S(1)}, bf16[4,576,128]{2,1,0:T(8,128)(2,1)S(1)}, u32[]{:S(2)}, u32[]{:S(2)}) collective-permute-start(bf16[4,576,128]{2,1,0:T(8,128)(2,1)S(1)} %copy-done.96), channel_id=1, source_target_pairs={{0,16},{16,0},{1,17},{17,1},{2,18},{18,2},{3,19},{19,3},{4,20},{20... | collective-permute-start | bytes 1769480 | tf_op jit(solution)/shard_map/ppermute | solution.py:630
  226.8 11.8 %collective-permute-start.35 = (bf16[1568,128]{1,0:T(8,128)(2,1)S(1)}, bf16[1568,128]{1,0:T(8,128)(2,1)S(1)}, u32[]{:S(2)}, u32[]{:S(2)}) collective-permute-start(bf16[1568,128]{1,0:T(8,128)(2,1)S(1)} %fusion.17.refs_9_), channel_id=1, source_target_pairs={{0,4},{4,0},{8,12},{12,8},{1,5},{5,1},{9,13},{13,9},{2,6},{6,2},{1... | collective-permute-start | bytes 1204232 | tf_op jit(solution)/shard_map/ppermute | solution.py:630
  237.3 31.4 %collective-permute-start.39 = (bf16[2,1,1728,128]{3,2,1,0:T(8,128)(2,1)S(1)}, bf16[2,1,1728,128]{3,2,1,0:T(8,128)(2,1)}, u32[]{:S(2)}, u32[]{:S(2)}) collective-permute-start(bf16[2,1,1728,128]{3,2,1,0:T(8,128)(2,1)S(1)} %dynamic-slice_bitcast_fusion.refs_8_), channel_id=1, source_target_pairs={{0,1},{1,0},{2,3},{3,2},{4,5},{5,4},{6,7},{7,6},{8,9},{9,8},{10,11... | collective-permute-start | bytes 2654216 | tf_op jit(solution)/shard_map/ppermute | solution.py:630
  240.0 25.8 %collective-permute-start.42 = (bf16[1568,128]{1,0:T(8,128)(2,1)S(1)}, bf16[1568,128]{1,0:T(8,128)(2,1)}, u32[]{:S(2)}, u32[]{:S(2)}) collective-permute-start(bf16[1568,128]{1,0:T(8,128)(2,1)S(1)} %fusion.7.refs_10_), channel_id=1, source_target_pairs={{0,8},{4,12},{8,0},{12,4},{1,9},{5,13},{9,1},{13,5},{2,10},{6,14},... | collective-permute-start | bytes 1204232 | tf_op jit(solution)/shard_map/ppermute | solution.py:630
  240.7 27.0 %collective-permute-start.40 = (bf16[2,1,1408,128]{3,2,1,0:T(8,128)(2,1)S(1)}, bf16[2,1,1408,128]{3,2,1,0:T(8,128)(2,1)S(1)}, u32[]{:S(2)}, u32[]{:S(2)}) collective-permute-start(bf16[2,1,1408,128]{3,2,1,0:T(8,128)(2,1)S(1)} %dynamic-slice_bitcast_fusion.2.refs_9_), channel_id=1, source_target_pairs={{0,2},{1,3},{2,0},{3,1},{4,6},{5,7},{6,4},{7,5},{8,10},{9,11},{10,... | collective-permute-start | bytes 2162696 | tf_op jit(solution)/shard_map/ppermute | solution.py:630
  252.6 11.9 %collective-permute-start.38 = (bf16[256,384]{1,0:T(8,128)(2,1)}, bf16[256,384]{1,0:T(8,128)(2,1)S(1)}, u32[]{:S(2)}, u32[]{:S(2)}) collective-permute-start(bf16[256,384]{1,0:T(8,128)(2,1)} %get-tuple-element.189), channel_id=1, source_target_pairs={{12,0},{13,1},{14,2},{15,3},{28,16},{29,17},{30,18},{31,19}} | collective-permute-start | bytes 589832 | tf_op jit(solution)/shard_map/ppermute | solution.py:635
  254.3 16.6 %collective-permute-start.36 = (bf16[256,384]{1,0:T(8,128)(2,1)S(1)}, bf16[256,384]{1,0:T(8,128)(2,1)S(1)}, u32[]{:S(2)}, u32[]{:S(2)}) collective-permute-start(bf16[256,384]{1,0:T(8,128)(2,1)S(1)} %copy-done.98), channel_id=1, source_target_pairs={{4,0},{8,4},{12,8},{5,1},{9,5},{13,9},{6,2},{10,6},{14,10},{7,3},{... | collective-permute-start | bytes 589832 | tf_op jit(solution)/shard_map/ppermute | solution.py:635
  264.5 12.0 %collective-permute-start.37 = (bf16[256,384]{1,0:T(8,128)(2,1)S(1)}, bf16[256,384]{1,0:T(8,128)(2,1)S(1)}, u32[]{:S(2)}, u32[]{:S(2)}) collective-permute-start(bf16[256,384]{1,0:T(8,128)(2,1)S(1)} %copy-done.97), channel_id=1, source_target_pairs={{8,0},{12,4},{9,1},{13,5},{10,2},{14,6},{11,3},{15,7},{24,16},{28,... | collective-permute-start | bytes 589832 | tf_op jit(solution)/shard_map/ppermute | solution.py:635
  283.2 18.5 %collective-permute-start.53 = (bf16[2,1,288,128]{3,2,1,0:T(8,128)(2,1)}, bf16[2,1,288,128]{3,2,1,0:T(8,128)(2,1)S(1)}, u32[]{:S(2)}, u32[]{:S(2)}) collective-permute-start(bf16[2,1,288,128]{3,2,1,0:T(8,128)(2,1)} %dynamic-slice_bitcast_fusion.11.refs_17_), channel_id=1, source_target_pairs={{0,1},{1,0},{2,3},{3,2},{4,5},{5,4},{6,7},{7,6},{8,9},{9,8},{10,11... | collective-permute-start | bytes 442376 | tf_op jit(solution)/shard_map/ppermute | solution.py:630
  284.8 19.2 %collective-permute-start.55 = (bf16[2,1,288,128]{3,2,1,0:T(8,128)(2,1)S(1)}, bf16[2,1,288,128]{3,2,1,0:T(8,128)(2,1)S(1)}, u32[]{:S(2)}, u32[]{:S(2)}) collective-permute-start(bf16[2,1,288,128]{3,2,1,0:T(8,128)(2,1)S(1)} %copy-done.86), channel_id=1, source_target_pairs={{0,2},{1,3},{2,0},{3,1},{4,6},{5,7},{6,4},{7,5},{8,10},{9,11},{10,... | collective-permute-start | bytes 442376 | tf_op jit(solution)/shard_map/ppermute | solution.py:630
  285.4 12.5 %collective-permute-start.48 = (bf16[1,1408,128]{2,1,0:T(8,128)(2,1)S(1)}, bf16[1,1408,128]{2,1,0:T(8,128)(2,1)S(1)}, u32[]{:S(2)}, u32[]{:S(2)}) collective-permute-start(bf16[1,1408,128]{2,1,0:T(8,128)(2,1)S(1)} %copy-done.80), channel_id=1, source_target_pairs={{0,1},{1,0},{2,3},{3,2},{4,5},{5,4},{6,7},{7,6},{8,9},{9,8},{10,11... | collective-permute-start | bytes 1081352 | tf_op jit(solution)/shard_map/ppermute | solution.py:630
  285.9 14.3 %collective-permute-start.47 = (bf16[1,1728,128]{2,1,0:T(8,128)(2,1)S(1)}, bf16[1,1728,128]{2,1,0:T(8,128)(2,1)S(1)}, u32[]{:S(2)}, u32[]{:S(2)}) collective-permute-start(bf16[1,1728,128]{2,1,0:T(8,128)(2,1)S(1)} %copy-done.79), channel_id=1, source_target_pairs={{0,2},{1,3},{2,0},{3,1},{4,6},{5,7},{6,4},{7,5},{8,10},{9,11},{10,... | collective-permute-start | bytes 1327112 | tf_op jit(solution)/shard_map/ppermute | solution.py:630
  288.8 16.0 %collective-permute-start.46 = (bf16[2,1,288,128]{3,2,1,0:T(8,128)(2,1)S(1)}, bf16[2,1,288,128]{3,2,1,0:T(8,128)(2,1)S(1)}, u32[]{:S(2)}, u32[]{:S(2)}) collective-permute-start(bf16[2,1,288,128]{3,2,1,0:T(8,128)(2,1)S(1)} %dynamic-slice_bitcast_fusion.9), channel_id=1, source_target_pairs={{0,1},{1,0},{2,3},{3,2},{4,5},{5,4},{6,7},{7,6},{8,9},{9,8},{10,11... | collective-permute-start | bytes 442376 | tf_op jit(solution)/shard_map/ppermute | solution.py:630
  301.6 10.9 %collective-permute-start.50 = (bf16[1568,128]{1,0:T(8,128)(2,1)S(1)}, bf16[1568,128]{1,0:T(8,128)(2,1)S(1)}, u32[]{:S(2)}, u32[]{:S(2)}) collective-permute-start(bf16[1568,128]{1,0:T(8,128)(2,1)S(1)} %fusion.13), channel_id=1, source_target_pairs={{0,4},{4,0},{8,12},{12,8},{1,5},{5,1},{9,13},{13,9},{2,6},{6,2},{1... | collective-permute-start | bytes 1204232 | tf_op jit(solution)/shard_map/ppermute | solution.py:630
  301.8 12.4 %collective-permute-start.54 = (bf16[1,288,128]{2,1,0:T(8,128)(2,1)S(1)}, bf16[1,288,128]{2,1,0:T(8,128)(2,1)S(1)}, u32[]{:S(2)}, u32[]{:S(2)}) collective-permute-start(bf16[1,288,128]{2,1,0:T(8,128)(2,1)S(1)} %dynamic-slice_bitcast_fusion.13), channel_id=1, source_target_pairs={{0,2},{1,3},{2,0},{3,1},{4,6},{5,7},{6,4},{7,5},{8,10},{9,11},{10,... | collective-permute-start | bytes 221192 | tf_op jit(solution)/shard_map/ppermute | solution.py:630
  304.1 10.7 %collective-permute-start.56 = (bf16[1,288,128]{2,1,0:T(8,128)(2,1)S(1)}, bf16[1,288,128]{2,1,0:T(8,128)(2,1)S(1)}, u32[]{:S(2)}, u32[]{:S(2)}) collective-permute-start(bf16[1,288,128]{2,1,0:T(8,128)(2,1)S(1)} %dynamic-slice_bitcast_fusion.12), channel_id=1, source_target_pairs={{0,1},{1,0},{2,3},{3,2},{4,5},{5,4},{6,7},{7,6},{8,9},{9,8},{10,11... | collective-permute-start | bytes 221192 | tf_op jit(solution)/shard_map/ppermute | solution.py:630
  308.5 11.0 %collective-permute-start.44 = (bf16[256,576]{1,0:T(8,128)(2,1)S(1)}, bf16[256,576]{1,0:T(8,128)(2,1)S(1)}, u32[]{:S(2)}, u32[]{:S(2)}) collective-permute-start(bf16[256,576]{1,0:T(8,128)(2,1)S(1)} %broadcast_select_fusion.8), channel_id=1, source_target_pairs={{0,16},{16,0},{1,17},{17,1},{2,18},{18,2},{3,19},{19,3},{4,20},{20... | collective-permute-start | bytes 884744 | tf_op jit(solution)/shard_map/ppermute | solution.py:630
  308.7 34.1 %collective-permute-start.63 = (bf16[1568,128]{1,0:T(8,128)(2,1)S(1)}, bf16[1568,128]{1,0:T(8,128)(2,1)S(1)}, u32[]{:S(2)}, u32[]{:S(2)}) collective-permute-start(bf16[1568,128]{1,0:T(8,128)(2,1)S(1)} %copy-done.70), channel_id=1, source_target_pairs={{0,4},{4,0},{8,12},{12,8},{1,5},{5,1},{9,13},{13,9},{2,6},{6,2},{1... | collective-permute-start | bytes 1204232 | tf_op jit(solution)/shard_map/ppermute | solution.py:630
  314.8 19.3 %collective-permute-start.59 = (bf16[1568,128]{1,0:T(8,128)(2,1)S(1)}, bf16[1568,128]{1,0:T(8,128)(2,1)S(1)}, u32[]{:S(2)}, u32[]{:S(2)}) collective-permute-start(bf16[1568,128]{1,0:T(8,128)(2,1)S(1)} %fusion.6), channel_id=1, source_target_pairs={{0,8},{4,12},{8,0},{12,4},{1,9},{5,13},{9,1},{13,5},{2,10},{6,14},... | collective-permute-start | bytes 1204232 | tf_op jit(solution)/shard_map/ppermute | solution.py:630
  319.2 12.2 %collective-permute-start.57 = (bf16[576,128]{1,0:T(8,128)(2,1)S(1)}, bf16[576,128]{1,0:T(8,128)(2,1)S(1)}, u32[]{:S(2)}, u32[]{:S(2)}) collective-permute-start(bf16[576,128]{1,0:T(8,128)(2,1)S(1)} %fusion.22), channel_id=1, source_target_pairs={{0,4},{4,0},{8,12},{12,8},{1,5},{5,1},{9,13},{13,9},{2,6},{6,2},{1... | collective-permute-start | bytes 442376 | tf_op jit(solution)/shard_map/ppermute | solution.py:630
  332.0 9.6 %collective-permute-start.58 = (bf16[576,128]{1,0:T(8,128)(2,1)S(1)}, bf16[576,128]{1,0:T(8,128)(2,1)S(1)}, u32[]{:S(2)}, u32[]{:S(2)}) collective-permute-start(bf16[576,128]{1,0:T(8,128)(2,1)S(1)} %add_convert_fusion.7), channel_id=1, source_target_pairs={{0,8},{4,12},{8,0},{12,4},{1,9},{5,13},{9,1},{13,5},{2,10},{6,14},... | collective-permute-start | bytes 442376 | tf_op jit(solution)/shard_map/ppermute | solution.py:630
  342.8 11.3 %collective-permute-start.62 = (bf16[1568,128]{1,0:T(8,128)(2,1)S(1)}, bf16[1568,128]{1,0:T(8,128)(2,1)S(1)}, u32[]{:S(2)}, u32[]{:S(2)}) collective-permute-start(bf16[1568,128]{1,0:T(8,128)(2,1)S(1)} %add_convert_fusion.4), channel_id=1, source_target_pairs={{0,4},{4,0},{8,12},{12,8},{1,5},{5,1},{9,13},{13,9},{2,6},{6,2},{1... | collective-permute-start | bytes 1204232 | tf_op jit(solution)/shard_map/ppermute | solution.py:630
  (116 other events, 1159.9 us)
